TPU v7x, 32 devices: a whole 2x2x4 slice. The times are simulated.
32 devices in a mesh: wide: 8 (over y, x, core), narrow: 4 (over z).
Axes of the slice: x: 2, y: 2, z: 4, core: 2. Of those that a mesh axis runs over, the one named last changes fastest.
Arguments:
- tokens: bfloat16 [8192, 1152], P(('wide', 'narrow')), may hold values from -6 to 6
- cotangent: bfloat16 [8192, 1152], P(('wide', 'narrow')), may hold values from -6 to 6
- segment_ids: int32 [8192], P('wide'), may hold values from 0 to 31, as said below
- patch_pos: int32 [8192], P('wide'), may hold values from 0 to 255, as said below
- time_index: int32 [32], P('wide'), may hold values from 0 to 999
- time_table: bfloat16 [1000, 1152], replicated, may hold values from -6 to 6
- norm_gain: float32 [2, 2, 1152], replicated, may hold values from 0.5 to 1.5
- norm_shift: float32 [2, 2, 1152], replicated, may hold values from -2 to 2
- attn_weight: bfloat16 [2, 6, 1152, 1152], P(None, None, 'wide', 'narrow'), may hold values from -0.1875 to 0.1875
- out_weight: bfloat16 [2, 1152, 1152], P(None, 'wide', 'narrow'), may hold values from -0.75 to 0.75
- qkv_bias: float32 [2, 2, 1152], P(None, None, 'narrow'), may hold values from -2 to 2
- out_bias: float32 [2, 2, 1152], replicated, may hold values from -2 to 2
- mlp_weight: bfloat16 [2, 2, 1152, 4608], P(None, None, 'wide', 'narrow'), may hold values from -0.1875 to 0.1875
- up_bias: float32 [2, 4608], P(None, 'narrow'), may hold values from -2 to 2
- rel_table: float32 [2, 16, 961], P(None, 'narrow'), may hold values from -5 to 5
Outputs:
- block_output: bfloat16 [8192, 1152], P(('wide', 'narrow'))
- input_grad: bfloat16 [8192, 1152], P(('wide', 'narrow'))
- time_grad: float32 [1000, 1152], replicated
- gain_grad: float32 [2, 2, 1152], replicated
- shift_grad: float32 [2, 2, 1152], replicated
- attn_weight_grad: float32 [2, 6, 1152, 1152], P(None, None, 'wide', 'narrow')
- out_weight_grad: float32 [2, 1152, 1152], P(None, 'wide', 'narrow')
- qkv_bias_grad: float32 [2, 2, 1152], P(None, None, 'narrow')
- out_bias_grad: float32 [2, 2, 1152], replicated
- mlp_weight_grad: float32 [2, 2, 1152, 4608], P(None, None, 'wide', 'narrow')
- up_bias_grad: float32 [2, 4608], P(None, 'narrow')
- rel_table_grad: float32 [2, 16, 961], P(None, 'narrow')
Inputs may be any that keep to these rules, and one draw needn't show every extreme that they name: `segment_ids`: image i has exactly 256 rows, all in the aligned block of 1024 rows numbered i // 4, in no particular order. `patch_pos`: within each image every position of the 16 x 16 patch grid occurs once; position p lies in grid row p // 16 and column p % 16.
All inputs are finite; a program needn't handle non-finite values.
Results may differ from a plain program's by a relative error of at most 0.024.
Values may be sent and summed in bfloat16 or wider, within the bound.
A program may use at most 320 MiB of HBM per device.

v0:
```python
import jax
import jax.numpy as jnp
from jax import lax
from jax.sharding import PartitionSpec as P

HEAD_DIM = 72
GRID = 16


eps_norm = 1e-06
masked_score = -1e30
query_rows = 512
highest = lax.Precision.HIGHEST


def layer_norm(values, norm_gain, norm_shift):
    average = jnp.mean(values, axis=-1, keepdims=True)
    centred = values - average
    variance = jnp.mean(centred * centred, axis=-1, keepdims=True)
    return centred * lax.rsqrt(variance + eps_norm) * norm_gain + norm_shift


def offset_onehot():
    near = jnp.arange(GRID, dtype=jnp.int32)
    span = jnp.arange(2 * GRID - 1, dtype=jnp.int32)
    return (span[None, None, :] == near[:, None, None] - near[None, :, None] + (GRID - 1)).astype(
        jnp.float32
    )


def pair_bias(bias_table):
    steps_hot = offset_onehot()
    head_count = bias_table.shape[0]
    table_grid = bias_table.reshape(head_count, 2 * GRID - 1, 2 * GRID - 1)
    row_part = jnp.einsum("ixa,hab->hixb", steps_hot, table_grid, precision=highest)
    pairs = jnp.einsum("jyb,hixb->hijxy", steps_hot, row_part, precision=highest)
    return pairs.reshape(head_count, GRID * GRID, GRID * GRID)


def fold_bias_grad(pair_grad):
    steps_hot = offset_onehot()
    head_count = pair_grad.shape[0]
    grid_grad = pair_grad.reshape(head_count, GRID, GRID, GRID, GRID)
    col_part = jnp.einsum("jyb,hijxy->hixb", steps_hot, grid_grad, precision=highest)
    table_grad = jnp.einsum("ixa,hixb->hab", steps_hot, col_part, precision=highest)
    return table_grad.reshape(head_count, (2 * GRID - 1) * (2 * GRID - 1))


def grid_order(image_local, positions):
    target = image_local * (GRID * GRID) + positions
    order = (
        jnp.zeros(target.shape, jnp.int32)
        .at[target]
        .set(jnp.arange(target.shape[0], dtype=jnp.int32))
    )
    return (target, order)


def rows_whole(piece):
    return lax.all_gather(piece, "narrow", axis=0, tiled=True)


def rows_share(term):
    return lax.psum_scatter(
        term.astype(jnp.bfloat16), "narrow", scatter_dimension=0, tiled=True
    ).astype(jnp.float32)


def split_blocks(array, block_rows):
    return array.reshape((array.shape[0] // block_rows, block_rows) + array.shape[1:])


def score_block(queries, key_rows, query_seg, key_seg, pairs):
    scores = jnp.einsum(
        "qhd,khd->hqk", queries, key_rows, preferred_element_type=jnp.float32
    ) * HEAD_DIM ** (-0.5)
    patches = GRID * GRID
    scores = scores + jnp.tile(
        pairs, (1, queries.shape[0] // patches, key_rows.shape[0] // patches)
    )
    same_image = (query_seg[:, None] == key_seg[None, :])[None]
    return jnp.where(same_image, scores, masked_score)


def attend(queries, key_rows, value_rows, segments, pairs):
    block_rows = min(query_rows, queries.shape[0])

    def one_block(block_items):
        block_queries, block_seg = block_items
        scores = score_block(block_queries, key_rows, block_seg, segments, pairs)
        row_top = jnp.max(scores, axis=-1, keepdims=True)
        exponent = jnp.exp(scores - row_top)
        row_total = jnp.sum(exponent, axis=-1, keepdims=True)
        weights_low = (exponent / row_total).astype(jnp.bfloat16)
        mixed_heads = jnp.einsum(
            "hqk,khd->qhd", weights_low, value_rows, preferred_element_type=jnp.float32
        )
        return (mixed_heads, (row_top + jnp.log(row_total))[..., 0])

    mixed_heads, log_totals = lax.map(
        one_block, (split_blocks(queries, block_rows), split_blocks(segments, block_rows))
    )
    return (mixed_heads.reshape(queries.shape), log_totals)


def attend_back(queries, key_rows, value_rows, mixed_grad, log_totals, segments, pairs):
    block_rows = min(query_rows, queries.shape[0])
    score_scale = HEAD_DIM ** (-0.5)
    patches = GRID * GRID
    head_count = pairs.shape[0]

    def one_block(carry, block_items):
        key_grad, value_grad, pos_grad = carry
        block_queries, block_grad, block_log, block_seg = block_items
        scores = score_block(block_queries, key_rows, block_seg, segments, pairs)
        attention = jnp.exp(scores - block_log[..., None])
        dot_back = jnp.einsum(
            "qhd,khd->hqk", block_grad, value_rows, preferred_element_type=jnp.float32
        )
        score_grad = attention * (dot_back - jnp.sum(attention * dot_back, axis=-1, keepdims=True))
        score_low = score_grad.astype(jnp.bfloat16)
        folded = score_low.astype(jnp.float32).reshape(
            head_count, block_rows // patches, patches, key_rows.shape[0] // patches, patches
        )
        pos_grad = pos_grad + jnp.sum(folded, axis=(1, 3))
        query_grad = (
            jnp.einsum("hqk,khd->qhd", score_low, key_rows, preferred_element_type=jnp.float32)
            * score_scale
        )
        key_grad = (
            key_grad
            + jnp.einsum(
                "hqk,qhd->khd", score_low, block_queries, preferred_element_type=jnp.float32
            )
            * score_scale
        )
        value_grad = value_grad + jnp.einsum(
            "hqk,qhd->khd",
            attention.astype(jnp.bfloat16),
            block_grad,
            preferred_element_type=jnp.float32,
        )
        return ((key_grad, value_grad, pos_grad), query_grad)

    start = (
        jnp.zeros(key_rows.shape, jnp.float32),
        jnp.zeros(value_rows.shape, jnp.float32),
        jnp.zeros(pairs.shape, jnp.float32),
    )
    items = (
        split_blocks(queries, block_rows),
        split_blocks(mixed_grad, block_rows),
        log_totals,
        split_blocks(segments, block_rows),
    )
    (key_grad, value_grad, pos_grad), query_grad = lax.scan(one_block, start, items)
    return (query_grad.reshape(queries.shape), key_grad, value_grad, fold_bias_grad(pos_grad))


def attention_part(residual, layer_params, weights, context):
    norm_gain, norm_shift, qkv_bias, out_bias, up_bias, bias_table = layer_params
    attn_full, out_full, mlp_full = weights
    segments, positions, image_local, onehot, time_rows = context
    normed, norm_back = jax.vjp(layer_norm, residual, norm_gain[0], norm_shift[0])
    normed_all = rows_whole(normed.astype(jnp.bfloat16))
    row_count = normed_all.shape[0]
    head_count = bias_table.shape[0]
    pairs = pair_bias(bias_table)
    target, order = grid_order(image_local, positions)
    spatial = jnp.einsum(
        "rd,jdc->jrc", normed_all, attn_full[0:3], preferred_element_type=jnp.float32
    )
    time_part = jnp.einsum(
        "id,jdc->jic", time_rows, attn_full[3:6], preferred_element_type=jnp.float32
    )
    time_spread = jnp.einsum(
        "ri,jic->jrc", onehot.astype(jnp.float32), time_part, precision=highest
    )
    queries = (
        (spatial[0] + time_spread[0] + qkv_bias[0])
        .astype(jnp.bfloat16)
        .reshape(row_count, head_count, -1)
    )
    key_rows = (spatial[1] + time_spread[1]).astype(jnp.bfloat16).reshape(row_count, head_count, -1)
    value_rows = (
        (spatial[2] + time_spread[2] + qkv_bias[1])
        .astype(jnp.bfloat16)
        .reshape(row_count, head_count, -1)
    )
    queries_s = jnp.take(queries, order, axis=0)
    keys_s = jnp.take(key_rows, order, axis=0)
    values_s = jnp.take(value_rows, order, axis=0)
    segments_s = jnp.take(segments, order, axis=0)
    mixed_s, log_totals = attend(queries_s, keys_s, values_s, segments_s, pairs)
    mixed_heads = jnp.take(mixed_s, target, axis=0)
    mixed_low = mixed_heads.reshape(row_count, -1).astype(jnp.bfloat16)
    branch = lax.dot_general(
        mixed_low, out_full, (((1,), (1,)), ((), ())), preferred_element_type=jnp.float32
    )
    middle = residual + (rows_share(branch) + out_bias[0])
    saved = (
        norm_back,
        normed_all,
        queries_s,
        keys_s,
        values_s,
        log_totals,
        mixed_low,
        pairs,
        segments_s,
        target,
        order,
    )
    return (middle, saved)


def mlp_front(middle, layer_params, weights):
    norm_gain, norm_shift, qkv_bias, out_bias, up_bias, bias_table = layer_params
    mlp_full = weights[2]
    normed_mid, norm_back_mid = jax.vjp(layer_norm, middle, norm_gain[1], norm_shift[1])
    normed_all = rows_whole(normed_mid.astype(jnp.bfloat16))
    hidden = jnp.dot(normed_all, mlp_full[0], preferred_element_type=jnp.float32) + up_bias
    activated, gelu_back = jax.vjp(lambda values: jax.nn.gelu(values, approximate=True), hidden)
    return (norm_back_mid, normed_all, gelu_back, activated.astype(jnp.bfloat16))


def layer_forward(residual, layer_params, weights, context):
    middle, unused_saved = attention_part(residual, layer_params, weights, context)
    unused_back, unused_rows, unused_gelu, activated = mlp_front(middle, layer_params, weights)
    branch = lax.dot_general(
        activated, weights[2][1], (((1,), (1,)), ((), ())), preferred_element_type=jnp.float32
    )
    return middle + (rows_share(branch) + layer_params[3][1])


def layer_backward(residual, gradient, layer_params, weights, context):
    attn_full, out_full, mlp_full = weights
    segments, positions, image_local, onehot, time_rows = context
    middle, saved = attention_part(residual, layer_params, weights, context)
    (
        norm_back,
        normed_all,
        queries_s,
        keys_s,
        values_s,
        log_totals,
        mixed_low,
        pairs,
        segments_s,
        target,
        order,
    ) = saved
    norm_back_mid, normed_mid_all, gelu_back, activated = mlp_front(middle, layer_params, weights)
    row_count = normed_all.shape[0]
    contract_rows = (((0,), (0,)), ((), ()))
    contract_cols = (((1,), (1,)), ((), ()))
    grad_low = gradient.astype(jnp.bfloat16)
    grad_all = rows_whole(grad_low)
    out_bias_mlp = jnp.sum(grad_low.astype(jnp.float32), axis=0)
    down_grad = lax.dot_general(
        grad_all, activated, contract_rows, preferred_element_type=jnp.float32
    )
    act_grad = jnp.dot(grad_all, mlp_full[1], preferred_element_type=jnp.float32)
    hidden_low = gelu_back(act_grad)[0].astype(jnp.bfloat16)
    up_bias_part = jnp.sum(hidden_low.astype(jnp.float32), axis=0)
    up_grad = lax.dot_general(
        normed_mid_all, hidden_low, contract_rows, preferred_element_type=jnp.float32
    )
    normed_mid_grad = lax.dot_general(
        hidden_low, mlp_full[0], contract_cols, preferred_element_type=jnp.float32
    )
    mid_from_norm, gain_mid, shift_mid = norm_back_mid(rows_share(normed_mid_grad))
    grad_mid = gradient + mid_from_norm
    mid_low = grad_mid.astype(jnp.bfloat16)
    mid_all = rows_whole(mid_low)
    out_bias_attn = jnp.sum(mid_low.astype(jnp.float32), axis=0)
    out_grad = lax.dot_general(
        mid_all, mixed_low, contract_rows, preferred_element_type=jnp.float32
    )
    mixed_grad = jnp.dot(mid_all, out_full, preferred_element_type=jnp.float32).astype(jnp.bfloat16)
    mixed_grad_s = jnp.take(mixed_grad.reshape(queries_s.shape), order, axis=0)
    query_grad_s, key_grad_s, value_grad_s, table_grad = attend_back(
        queries_s, keys_s, values_s, mixed_grad_s, log_totals, segments_s, pairs
    )
    query_grad = jnp.take(query_grad_s, target, axis=0)
    key_grad = jnp.take(key_grad_s, target, axis=0)
    value_grad = jnp.take(value_grad_s, target, axis=0)
    qkv_low = jnp.stack(
        [
            query_grad.reshape(row_count, -1),
            key_grad.reshape(row_count, -1),
            value_grad.reshape(row_count, -1),
        ]
    ).astype(jnp.bfloat16)
    spatial_grad = jnp.einsum(
        "rd,jrc->jdc", normed_all, qkv_low, preferred_element_type=jnp.float32
    )
    time_grad_rows = jnp.einsum(
        "ri,jrc->jic", onehot, qkv_low, preferred_element_type=jnp.float32
    ).astype(jnp.bfloat16)
    time_weight_grad = jnp.einsum(
        "id,jic->jdc", time_rows, time_grad_rows, preferred_element_type=jnp.float32
    )
    time_row_grad = jnp.einsum(
        "jic,jdc->id", time_grad_rows, attn_full[3:6], preferred_element_type=jnp.float32
    )
    bias_part = jnp.stack(
        [
            jnp.sum(qkv_low[0].astype(jnp.float32), axis=0),
            jnp.sum(qkv_low[2].astype(jnp.float32), axis=0),
        ]
    )
    normed_grad = jnp.einsum(
        "jrc,jdc->rd", qkv_low, attn_full[0:3], preferred_element_type=jnp.float32
    )
    input_from_norm, gain_in, shift_in = norm_back(rows_share(normed_grad))
    grad_in = grad_mid + input_from_norm
    attn_grad = jnp.concatenate([spatial_grad, time_weight_grad], axis=0)
    mlp_grad = jnp.stack([up_grad, down_grad])
    shard_grads = (
        lax.psum_scatter(
            attn_grad.astype(jnp.bfloat16), "wide", scatter_dimension=1, tiled=True
        ).astype(jnp.float32),
        lax.psum_scatter(
            out_grad.astype(jnp.bfloat16), "wide", scatter_dimension=0, tiled=True
        ).astype(jnp.float32),
        lax.psum_scatter(
            mlp_grad.astype(jnp.bfloat16), "wide", scatter_dimension=1, tiled=True
        ).astype(jnp.float32),
    )
    small_grads = (
        jnp.stack([gain_in, gain_mid]),
        jnp.stack([shift_in, shift_mid]),
        jnp.stack([out_bias_attn, out_bias_mlp]),
        bias_part,
        up_bias_part,
        table_grad,
    )
    return (grad_in, shard_grads, small_grads, time_row_grad)


def shards(
    tokens,
    cotangent,
    segment_ids,
    patch_pos,
    time_index,
    time_table,
    norm_gain,
    norm_shift,
    attn_weight,
    out_weight,
    qkv_bias,
    out_bias,
    mlp_weight,
    up_bias,
    rel_table,
):
    image_count = time_index.shape[0]
    image_local = segment_ids % image_count
    onehot = (image_local[:, None] == jnp.arange(image_count, dtype=jnp.int32)[None, :]).astype(
        jnp.bfloat16
    )
    step_hot = (
        time_index[:, None] == jnp.arange(time_table.shape[0], dtype=jnp.int32)[None, :]
    ).astype(jnp.bfloat16)
    time_rows = jnp.dot(step_hot, time_table, preferred_element_type=jnp.float32).astype(
        jnp.bfloat16
    )
    context = (segment_ids, patch_pos, image_local, onehot, time_rows)
    layer_count = attn_weight.shape[0]

    def layer_params(layer_at):
        return (
            norm_gain[layer_at],
            norm_shift[layer_at],
            qkv_bias[layer_at],
            out_bias[layer_at],
            up_bias[layer_at],
            rel_table[layer_at],
        )

    residual = tokens.astype(jnp.float32)
    layer_inputs = []
    kept_weights = []
    for layer_at in range(layer_count):
        weights = (
            lax.all_gather(attn_weight[layer_at], "wide", axis=1, tiled=True),
            lax.all_gather(out_weight[layer_at], "wide", axis=0, tiled=True),
            lax.all_gather(mlp_weight[layer_at], "wide", axis=1, tiled=True),
        )
        kept_weights.append(weights)
        layer_inputs.append(residual)
        residual = layer_forward(residual, layer_params(layer_at), weights, context)
    block_output = residual.astype(jnp.bfloat16)
    gradient = cotangent.astype(jnp.float32)
    shard_list = [None] * layer_count
    small_list = [None] * layer_count
    time_rows_grad = jnp.zeros(time_rows.shape, jnp.float32)
    for layer_at in reversed(range(layer_count)):
        weights = (
            lax.all_gather(attn_weight[layer_at], "wide", axis=1, tiled=True),
            lax.all_gather(out_weight[layer_at], "wide", axis=0, tiled=True),
            lax.all_gather(mlp_weight[layer_at], "wide", axis=1, tiled=True),
        )
        gradient, shard_grads, small_grads, time_row_grad = layer_backward(
            layer_inputs[layer_at], gradient, layer_params(layer_at), weights, context
        )
        shard_list[layer_at] = shard_grads
        small_list[layer_at] = small_grads
        time_rows_grad = time_rows_grad + time_row_grad
    input_grad = gradient.astype(jnp.bfloat16)

    def stacked(index_at, source):
        return jnp.stack([entry[index_at] for entry in source])

    wide_totals = (
        lax.psum(stacked(3, small_list).astype(jnp.bfloat16), "wide").astype(jnp.float32),
        lax.psum(stacked(4, small_list).astype(jnp.bfloat16), "wide").astype(jnp.float32),
        lax.psum(stacked(5, small_list).astype(jnp.bfloat16), "wide").astype(jnp.float32),
    )
    time_total = jnp.einsum(
        "is,id->sd", step_hot.astype(jnp.float32), time_rows_grad, precision=highest
    )
    global_totals = lax.psum(
        (stacked(0, small_list), stacked(1, small_list), stacked(2, small_list), time_total),
        ("wide", "narrow"),
    )
    return (
        block_output,
        input_grad,
        global_totals[3],
        global_totals[0],
        global_totals[1],
        stacked(0, shard_list),
        stacked(1, shard_list),
        wide_totals[0],
        global_totals[2],
        stacked(2, shard_list),
        wide_totals[1],
        wide_totals[2],
    )


def solution(mesh):
    return jax.shard_map(
        shards,
        mesh=mesh,
        in_specs=(
            P(("wide", "narrow"), None),
            P(("wide", "narrow"), None),
            P("wide"),
            P("wide"),
            P("wide"),
            P(),
            P(),
            P(),
            P(None, None, "wide", "narrow"),
            P(None, "wide", "narrow"),
            P(None, None, "narrow"),
            P(),
            P(None, None, "wide", "narrow"),
            P(None, "narrow"),
            P(None, "narrow", None),
        ),
        out_specs=(
            P(("wide", "narrow"), None),
            P(("wide", "narrow"), None),
            P(),
            P(),
            P(),
            P(None, None, "wide", "narrow"),
            P(None, "wide", "narrow"),
            P(None, None, "narrow"),
            P(),
            P(None, None, "wide", "narrow"),
            P(None, "narrow"),
            P(None, "narrow", None),
        ),
        check_vma=False,
    )
```

profile of v0, /device:TPU:0, one launch (start us, length us, event | category | flops | bytes accessed | tf_op | source)
XLA Modules:
  0.0 2248.3 jit_solution(8945055926354295744)
XLA Ops:
  46.4 13.9 all-gather.1
  66.5 41.1 %all-gather.21.cloned.1.call-done = bf16[1024,1152]{1,0:T(8,128)(2,1)} async-done(((bf16[256,1152]{1,0:T(8,128)(2,1)}), bf16[1024,1152]{1,0:T(8,128)(2,1)}) %all-gather.21.cloned.1.call-update) | async-done | bytes 2359312 | tf_op jit(solution)/shard_map/all_gather | solution.py:60
  157.0 54.6 %while.87 = (s32[]{:T(128)}, bf16[2,512,4,72]{1,3,2,0:T(8,128)(2,1)}, f32[2,4,512]{2,1,0:T(4,128)S(1)}, s32[2,512]{1,0:T(2,128)S(1)}, s32[1024]{0:T(1024)S(1)}, ...) while((s32[]{:T(128)}, ...), condition=%wide.wide.region_41.45_spmd, body=%wide.wide.region_38.44_spmd.sunk | while | flops 623376384 | bytes 67676352 | solution.py:100
  225.9 73.6 %while.84 = (s32[]{:T(128)}, bf16[2,512,4,72]{1,3,2,0:T(8,128)(2,1)}, s32[2,512]{1,0:T(2,128)S(1)}, s32[1024]{0:T(1024)S(1)}, bf16[2,512,4,72]{1,3,2,0:T(8,128)(...) while((s32[]{:T(128)}, ...), condition=%wide.wide.region_6.9_spmd, body=%wide.wide.region_3.8_spmd.sunk | while | flops 621285376 | bytes 104851608 | solution.py:100
  320.3 41.7 %reduce-scatter.21.cloned.1.call-done = bf16[256,1152]{1,0:T(8,128)(2,1)} async-done(((bf16[1024,1152]{1,0:T(8,128)(2,1)}), bf16[256,1152]{1,0:T(8,128)(2,1)}) %reduce-scatter.21.cloned.1.call-update) | async-done | bytes 589840 | tf_op jit(solution)/shard_map/reduce_scatter | solution.py:64
  362.0 50.3 %reduce-scatter.35.cloned.1.call-done = bf16[256,1152]{1,0:T(8,128)(2,1)} async-done(((bf16[1024,1152]{1,0:T(8,128)(2,1)}), bf16[256,1152]{1,0:T(8,128)(2,1)}) %reduce-scatter.35.cloned.1.call-update) | async-done | bytes 589840 | tf_op jit(solution)/shard_map/reduce_scatter | solution.py:64
  418.7 36.9 %all-gather.43.cloned.1.call-done = bf16[1,2,1152,1152]{3,2,1,0:T(8,128)(2,1)} async-done(((bf16[1,2,144,1152]{3,2,1,0:T(8,128)(2,1)}), bf16[1,2,1152,1152]{3,2,1,0:T(8,128)(2,1)}) %all-gather.43.cloned.1.call-update) | async-done | bytes 5308432 | tf_op jit(solution)/shard_map/all_gather | solution.py:390
  455.5 52.5 %all-gather.23.cloned.1.call-done = bf16[1024,1152]{1,0:T(8,128)(2,1)} async-done(((bf16[256,1152]{1,0:T(8,128)(2,1)}), bf16[1024,1152]{1,0:T(8,128)(2,1)}) %all-gather.23.cloned.1.call-update) | async-done | bytes 2359312 | tf_op jit(solution)/shard_map/all_gather | solution.py:60
  508.1 11.7 convolution_convert_fusion.11
  520.6 46.2 %reduce-scatter.23.cloned.1.call-done = bf16[256,1152]{1,0:T(8,128)(2,1)} async-done(((bf16[1024,1152]{1,0:T(8,128)(2,1)}), bf16[256,1152]{1,0:T(8,128)(2,1)}) %reduce-scatter.23.cloned.1.call-update) | async-done | bytes 589840 | tf_op jit(solution)/shard_map/reduce_scatter | solution.py:64
  589.8 16.1 all-gather.4
  618.8 46.7 %all-gather.25.cloned.1.call-done = bf16[1024,1152]{1,0:T(8,128)(2,1)} async-done(((bf16[256,1152]{1,0:T(8,128)(2,1)}), bf16[1024,1152]{1,0:T(8,128)(2,1)}) %all-gather.25.cloned.1.call-update) | async-done | bytes 2359312 | tf_op jit(solution)/shard_map/all_gather | solution.py:60
  715.1 54.5 %while.86 = (s32[]{:T(128)}, bf16[2,512,4,72]{1,3,2,0:T(8,128)(2,1)}, f32[2,4,512]{2,1,0:T(4,128)S(1)}, s32[2,512]{1,0:T(2,128)S(1)}, s32[1024]{0:T(1024)S(1)}, ...) while((s32[]{:T(128)}, ...), condition=%wide.wide.region_24.28_spmd, body=%wide.wide.region_21.27_spmd.sunk | while | flops 623376384 | bytes 67676352 | solution.py:100
  770.5 73.7 %while.85 = (s32[]{:T(128)}, bf16[2,512,4,72]{1,3,2,0:T(8,128)(2,1)}, s32[2,512]{1,0:T(2,128)S(1)}, s32[1024]{0:T(1024)S(1)}, bf16[2,512,4,72]{1,3,2,0:T(8,128)(...) while((s32[]{:T(128)}, ...), condition=%wide.wide.region_16.20_spmd, body=%wide.wide.region_13.19_spmd.sunk | while | flops 621285376 | bytes 104851608 | solution.py:100
  867.1 46.2 %reduce-scatter.29.cloned.1.call-done = bf16[256,1152]{1,0:T(8,128)(2,1)} async-done(((bf16[1024,1152]{1,0:T(8,128)(2,1)}), bf16[256,1152]{1,0:T(8,128)(2,1)}) %reduce-scatter.29.cloned.1.call-update) | async-done | bytes 589840 | tf_op jit(solution)/shard_map/reduce_scatter | solution.py:64
  916.8 39.3 %all-gather.47.cloned.1.call-done = bf16[1,2,1152,1152]{3,2,1,0:T(8,128)(2,1)} async-done(((bf16[1,2,144,1152]{3,2,1,0:T(8,128)(2,1)}), bf16[1,2,1152,1152]{3,2,1,0:T(8,128)(2,1)}) %all-gather.47.cloned.1.call-update) | async-done | bytes 5308432 | tf_op jit(solution)/shard_map/all_gather | solution.py:390
  956.1 52.5 %all-gather.31.cloned.1.call-done = bf16[1024,1152]{1,0:T(8,128)(2,1)} async-done(((bf16[256,1152]{1,0:T(8,128)(2,1)}), bf16[1024,1152]{1,0:T(8,128)(2,1)}) %all-gather.31.cloned.1.call-update) | async-done | bytes 2359312 | tf_op jit(solution)/shard_map/all_gather | solution.py:60
  1016.8 42.8 %all-gather.29.cloned.1.call-done = bf16[1024,1152]{1,0:T(8,128)(2,1)} async-done(((bf16[256,1152]{1,0:T(8,128)(2,1)}), bf16[1024,1152]{1,0:T(8,128)(2,1)}) %all-gather.29.cloned.1.call-update) | async-done | bytes 2359312 | tf_op jit(solution)/shard_map/all_gather | solution.py:60
  1074.6 47.0 %reduce-scatter.31.cloned.1.call-done = bf16[256,1152]{1,0:T(8,128)(2,1)} async-done(((bf16[1024,1152]{1,0:T(8,128)(2,1)}), bf16[256,1152]{1,0:T(8,128)(2,1)}) %reduce-scatter.31.cloned.1.call-update) | async-done | bytes 589840 | tf_op jit(solution)/shard_map/reduce_scatter | solution.py:64
  1139.9 38.6 %all-gather.33.cloned.1.call-done = bf16[1024,1152]{1,0:T(8,128)(2,1)} async-done(((bf16[256,1152]{1,0:T(8,128)(2,1)}), bf16[1024,1152]{1,0:T(8,128)(2,1)}) %all-gather.33.cloned.1.call-update) | async-done | bytes 2359312 | tf_op jit(solution)/shard_map/all_gather | solution.py:60
  1197.0 109.4 %while.88 = (s32[]{:T(128)}, f32[1024,4,72]{0,2,1:T(8,128)S(1)}, f32[1024,4,72]{0,2,1:T(8,128)}, f32[4,256,256]{2,1,0:T(8,128)}, bf16[2,512,4,72]{1,3,2,0:T(8,12...) while((s32[]{:T(128)}, f32[1024,4,72]{0,2,1:T(8,128)S(1)}, ...), condition=%wide.wide.region_34.38_spmd.clone, body=%wide.wide.region_31.37_spmd.clone.sunk | while | flops 1535424512 | bytes 169527696 | solution.py:156
  1345.1 47.0 %reduce-scatter.33.cloned.1.call-done = bf16[256,1152]{1,0:T(8,128)(2,1)} async-done(((bf16[1024,1152]{1,0:T(8,128)(2,1)}), bf16[256,1152]{1,0:T(8,128)(2,1)}) %reduce-scatter.33.cloned.1.call-update) | async-done | bytes 589840 | tf_op jit(solution)/shard_map/reduce_scatter | solution.py:64
  1397.2 50.1 %all-gather.27.cloned.1.call-done = bf16[1024,1152]{1,0:T(8,128)(2,1)} async-done(((bf16[256,1152]{1,0:T(8,128)(2,1)}), bf16[1024,1152]{1,0:T(8,128)(2,1)}) %all-gather.27.cloned.1.call-update) | async-done | bytes 2359312 | tf_op jit(solution)/shard_map/all_gather | solution.py:60
  1447.2 11.7 convolution_convert_fusion.10
  1459.6 46.4 %reduce-scatter.27.cloned.1.call-done = bf16[256,1152]{1,0:T(8,128)(2,1)} async-done(((bf16[1024,1152]{1,0:T(8,128)(2,1)}), bf16[256,1152]{1,0:T(8,128)(2,1)}) %reduce-scatter.27.cloned.1.call-update) | async-done | bytes 589840 | tf_op jit(solution)/shard_map/reduce_scatter | solution.py:64
  1510.4 47.0 %all-gather.37.cloned.1.call-done = bf16[1024,1152]{1,0:T(8,128)(2,1)} async-done(((bf16[256,1152]{1,0:T(8,128)(2,1)}), bf16[1024,1152]{1,0:T(8,128)(2,1)}) %all-gather.37.cloned.1.call-update) | async-done | bytes 2359312 | tf_op jit(solution)/shard_map/all_gather | solution.py:60
  1565.5 43.4 %all-gather.35.cloned.1.call-done = bf16[1024,1152]{1,0:T(8,128)(2,1)} async-done(((bf16[256,1152]{1,0:T(8,128)(2,1)}), bf16[1024,1152]{1,0:T(8,128)(2,1)}) %all-gather.35.cloned.1.call-update) | async-done | bytes 2359312 | tf_op jit(solution)/shard_map/all_gather | solution.py:60
  1625.6 47.0 %reduce-scatter.37.cloned.1.call-done = bf16[256,1152]{1,0:T(8,128)(2,1)} async-done(((bf16[1024,1152]{1,0:T(8,128)(2,1)}), bf16[256,1152]{1,0:T(8,128)(2,1)}) %reduce-scatter.37.cloned.1.call-update) | async-done | bytes 589840 | tf_op jit(solution)/shard_map/reduce_scatter | solution.py:64
  1767.0 112.8 %while.89 = (s32[]{:T(128)}, f32[1024,4,72]{0,2,1:T(8,128)S(1)}, f32[1024,4,72]{0,2,1:T(8,128)}, f32[4,256,256]{2,1,0:T(8,128)}, bf16[2,512,4,72]{1,3,2,0:T(8,12...) while((s32[]{:T(128)}, f32[1024,4,72]{0,2,1:T(8,128)S(1)}, ...), condition=%wide.wide.region_51.55_spmd.clone, body=%wide.wide.region_48.54_spmd.clone.sunk | while | flops 1535424512 | bytes 169527696 | solution.py:156
  1983.7 25.0 %all-reduce.1 = (bf16[2,2,288]{2,1,0:T(2,128)(2,1)S(1)}, bf16[2,1152]{1,0:T(2,128)(2,1)S(1)}, bf16[2,4,961]{2,1,0:T(4,128)(2,1)S(1)}) all-reduce(bf16[2,2,288]{2,1,0:T(2,128)(2,1)S(1)} %pad_maximum_fusion.11, bf16[2,1152]{1,0:T(2,128)(2,1)S(1)} %pad_maximum_fusion.10, ...), channel_id=1, replica_groups=mesh['wide'=8,'narrow'=4] {'wide'}, use_global_device_ids=true, to_apply=%region_74.78 | all-reduce | flops 11144 | bytes 44576 | tf_op jit(solution)/shard_map/psum | solution.py:418
  2035.2 41.3 %all-reduce = (f32[2,2,1152]{2,1,0:T(2,128)}, f32[2,2,1152]{2,1,0:T(2,128)}, f32[2,2,1152]{2,1,0:T(2,128)}) all-reduce(f32[2,2,1152]{2,1,0:T(2,128)S(1)} %pad_maximum_fusion.6, f32[2,2,1152]{2,1,0:T(2,128)S(1)} %pad_maximum_fusion.7, f32[2,2,1152]{2,1,0:T(2,128)S(1)} %pad_maximum_fusion.8), channel_id=1, replica_groups=mesh['wide'=8,'narrow'=4] {'wide','narrow'}, use_global_device_ids=true, to_apply=%region_60.64 | all-reduce | flops 13824 | bytes 110592 | tf_op jit(solution)/shard_map/psum | solution.py:425
  2095.1 141.0 %all-reduce.4.cloned.1.call-done = f32[1000,1152]{1,0:T(8,128)} async-done(((f32[1000,1152]{1,0:T(8,128)}), f32[1000,1152]{1,0:T(8,128)}) %all-reduce.4.cloned.1.call-update) | async-done | bytes 4608016 | tf_op jit(solution)/shard_map/psum | solution.py:425
  (890 shorter events, 1105.5 us)
Async XLA Ops:
  7.2 53.6 %all-gather.41.cloned.1.call-start = ((), (), s32[]{:S(2)}) async-start(), calls=%async_computation.41 | async-start | bytes 5971968 | tf_op jit(solution)/shard_map/all_gather | solution.py:388
  9.9 97.7 %all-gather.21.cloned.1.call-start = ((), (), s32[]{:S(2)}) async-start(), calls=%async_computation.16 | async-start | bytes 2949120 | tf_op jit(solution)/shard_map/all_gather | solution.py:60
  14.0 348.0 %reduce-scatter.21.cloned.1.call-start = ((), (), s32[]{:S(2)}) async-start(), calls=%async_computation.17 | async-start | bytes 2949120 | tf_op jit(solution)/shard_map/reduce_scatter | solution.py:64
  315.0 97.3 %reduce-scatter.35.cloned.1.call-start = ((), (), s32[]{:S(2)}) async-start(), calls=%async_computation.31 | async-start | bytes 2949120 | tf_op jit(solution)/shard_map/reduce_scatter | solution.py:64
  318.3 137.2 %all-gather.43.cloned.1.call-start = ((), (), s32[]{:S(2)}) async-start(), calls=%async_computation.42 | async-start | bytes 5971968 | tf_op jit(solution)/shard_map/all_gather | solution.py:390
  319.6 188.5 %all-gather.23.cloned.1.call-start = ((), (), s32[]{:S(2)}) async-start(), calls=%async_computation.18 | async-start | bytes 2949120 | tf_op jit(solution)/shard_map/all_gather | solution.py:60
  320.3 246.6 %copy-start.76 = (f32[1152]{0:T(1024)}, f32[1152]{0:T(1024)S(1)}, u32[]{:S(2)}) copy-start(f32[1152]{0:T(1024)S(1)} %get-tuple-element.756) | copy-start | bytes 13828
  418.0 148.9 %reduce-scatter.23.cloned.1.call-start = ((), (), s32[]{:S(2)}) async-start(), calls=%async_computation.19 | async-start | bytes 2949120 | tf_op jit(solution)/shard_map/reduce_scatter | solution.py:64
  519.8 93.3 %all-gather.45.cloned.1.call-start = ((), (), s32[]{:S(2)}) async-start(), calls=%async_computation.43 | async-start | bytes 5971968 | tf_op jit(solution)/shard_map/all_gather | solution.py:388
  520.6 144.9 %all-gather.25.cloned.1.call-start = ((), (), s32[]{:S(2)}) async-start(), calls=%async_computation.20 | async-start | bytes 2949120 | tf_op jit(solution)/shard_map/all_gather | solution.py:60
  569.8 343.5 %reduce-scatter.29.cloned.1.call-start = ((), (), s32[]{:S(2)}) async-start(), calls=%async_computation.25 | async-start | bytes 2949120 | tf_op jit(solution)/shard_map/reduce_scatter | solution.py:64
  866.3 89.8 %all-gather.47.cloned.1.call-start = ((), (), s32[]{:S(2)}) async-start(), calls=%async_computation.44 | async-start | bytes 5971968 | tf_op jit(solution)/shard_map/all_gather | solution.py:390
  867.1 141.5 %all-gather.31.cloned.1.call-start = ((), (), s32[]{:S(2)}) async-start(), calls=%async_computation.26 | async-start | bytes 2949120 | tf_op jit(solution)/shard_map/all_gather | solution.py:60
  916.0 143.5 %all-gather.29.cloned.1.call-start = ((), (), s32[]{:S(2)}) async-start(), calls=%async_computation.24 | async-start | bytes 2949120 | tf_op jit(solution)/shard_map/all_gather | solution.py:60
  916.8 204.7 %reduce-scatter.31.cloned.1.call-start = ((), (), s32[]{:S(2)}) async-start(), calls=%async_computation.27 | async-start | bytes 2949120 | tf_op jit(solution)/shard_map/reduce_scatter | solution.py:64
  1074.5 104.0 %all-gather.33.cloned.1.call-start = ((), (), s32[]{:S(2)}) async-start(), calls=%async_computation.28 | async-start | bytes 2949120 | tf_op jit(solution)/shard_map/all_gather | solution.py:60
  1128.4 216.7 %reduce-scatter.25.cloned.1.call-start = ((), (), s32[]{:S(2)}) async-start(), calls=%async_computation.21 | async-start | bytes 2949120 | tf_op jit(solution)/shard_map/reduce_scatter | solution.py:64
  1139.8 252.2 %reduce-scatter.33.cloned.1.call-start = ((), (), s32[]{:S(2)}) async-start(), calls=%async_computation.29 | async-start | bytes 2949120 | tf_op jit(solution)/shard_map/reduce_scatter | solution.py:64
  1345.0 102.2 %all-gather.27.cloned.1.call-start = ((), (), s32[]{:S(2)}) async-start(), calls=%async_computation.22 | async-start | bytes 2949120 | tf_op jit(solution)/shard_map/all_gather | solution.py:60
  1397.1 108.9 %reduce-scatter.27.cloned.1.call-start = ((), (), s32[]{:S(2)}) async-start(), calls=%async_computation.23 | async-start | bytes 2949120 | tf_op jit(solution)/shard_map/reduce_scatter | solution.py:64
  1459.0 98.4 %all-gather.37.cloned.1.call-start = ((), (), s32[]{:S(2)}) async-start(), calls=%async_computation.32 | async-start | bytes 2949120 | tf_op jit(solution)/shard_map/all_gather | solution.py:60
  1459.6 149.3 %all-gather.35.cloned.1.call-start = ((), (), s32[]{:S(2)}) async-start(), calls=%async_computation.30 | async-start | bytes 2949120 | tf_op jit(solution)/shard_map/all_gather | solution.py:60
  1510.4 162.2 %reduce-scatter.37.cloned.1.call-start = ((), (), s32[]{:S(2)}) async-start(), calls=%async_computation.33 | async-start | bytes 2949120 | tf_op jit(solution)/shard_map/reduce_scatter | solution.py:64
  1625.6 122.9 %all-gather.39.cloned.1.call-start = ((), (), s32[]{:S(2)}) async-start(), calls=%async_computation.34 | async-start | bytes 2949120 | tf_op jit(solution)/shard_map/all_gather | solution.py:60
  1679.3 284.7 %reduce-scatter.51.cloned.1.call-start = ((), (), s32[]{:S(2)}) async-start(), calls=%async_computation.46 | async-start | bytes 4644864
  1707.4 260.6 %reduce-scatter.47.cloned.1.call-start = ((), (), s32[]{:S(2)}) async-start(), calls=%async_computation.40 | async-start | bytes 5971968 | tf_op jit(solution)/shard_map/reduce_scatter | solution.py:327
  1722.0 246.0 %reduce-scatter.45.cloned.1.call-start = ((), (), s32[]{:S(2)}) async-start(), calls=%async_computation.39 | async-start | bytes 5971968 | tf_op jit(solution)/shard_map/reduce_scatter | solution.py:327
  1736.7 283.6 %reduce-scatter.43.cloned.1.call-start = ((), (), s32[]{:S(2)}) async-start(), calls=%async_computation.38 | async-start | bytes 995328 | tf_op jit(solution)/shard_map/reduce_scatter | solution.py:324
  1748.3 272.0 %reduce-scatter.41.cloned.1.call-start = ((), (), s32[]{:S(2)}) async-start(), calls=%async_computation.37 | async-start | bytes 995328 | tf_op jit(solution)/shard_map/reduce_scatter | solution.py:324
  1902.2 129.7 %reduce-scatter.39.cloned.1.call-start = ((), (), s32[]{:S(2)}) async-start(), calls=%async_computation.35 | async-start | bytes 2949120 | tf_op jit(solution)/shard_map/reduce_scatter | solution.py:64
  1921.5 164.4 %reduce-scatter.49.cloned.1.call-start = ((), (), s32[]{:S(2)}) async-start(), calls=%async_computation.45 | async-start | bytes 4644864
  1949.9 286.3 %all-reduce.4.cloned.1.call-start = ((), (), s32[]{:S(2)}) async-start(), calls=%async_computation.36 | async-start | bytes 9216000 | tf_op jit(solution)/shard_map/psum | solution.py:425
  (219 other events, 4346.9 us)
Sparse Core Ops, SparseCore 0:
  10.5 44.1 all-gather.40
  56.9 50.6 all-gather.20
  315.2 46.7 reduce-scatter.20
  364.7 47.5 reduce-scatter.34
  414.6 40.8 all-gather.42
  457.5 50.4 all-gather.22
  519.9 46.8 reduce-scatter.22
  568.7 44.3 all-gather.44
  615.3 50.1 all-gather.24
  866.5 46.7 reduce-scatter.28
  915.2 40.8 all-gather.46
  958.1 50.4 all-gather.30
  1010.2 49.2 all-gather.28
  1074.6 46.8 reduce-scatter.30
  1128.5 49.9 all-gather.32
  1181.2 46.8 reduce-scatter.24
  1345.1 46.9 reduce-scatter.32
  1397.2 49.9 all-gather.26
  1459.1 46.8 reduce-scatter.26
  1507.4 49.9 all-gather.36
  1559.6 49.2 all-gather.34
  1625.7 46.8 reduce-scatter.36
  1679.4 49.9 all-gather.38
  1732.7 49.8 reduce-scatter.50
  1786.1 57.2 reduce-scatter.46
  1846.7 57.2 reduce-scatter.44
  1907.1 35.0 reduce-scatter.42
  1945.8 35.1 reduce-scatter.40
  1983.8 47.9 reduce-scatter.38
  2035.2 50.7 reduce-scatter.48
  2092.2 143.8 all-reduce.3
where the time goes:
time: 2260 us; the launch traced here: 2250 us
  waiting for transfers between devices  1030 us (46%)
  local copies, waits for them, and re-layouts  554 us (25%)
  matrix products  366 us (16%)
  other arithmetic  181 us (8%)
  blocking collectives  96.4 us (4%)
    all_gather x10, waiting for transfers between devices, rows_whole(): return lax.all_gather(piece, 'narrow', axis=0, tiled=True)  415 us
    reduce_scatter x10, waiting for transfers between devices, rows_share(): lax.psum_scatter(term.astype(jnp.bfloat16), 'narrow', scatter_dimension=0...  381 us
    another operation x30, local copies, waits for them, and re-layouts, score_block(): jnp.tile(pairs, (1, queries.shape[0] // patches, key_rows.shape[0] // pat...  227 us
    psum x1, waiting for transfers between devices, shards(): lax.psum((stacked(0, small_list), stacked(1, small_list), stacked(2, smal...  141 us
    all_gather x2, waiting for transfers between devices, shards(): lax.all_gather(mlp_weight[layer_at], 'wide', axis=1, tiled=True)  76.1 us
    dot_general x12, matrix products, score_block(): jnp.einsum('qhd,khd->hqk', queries, key_rows, preferred_element_type=jnp....  75.8 us
    unnamed x372, local copies, waits for them, and re-layouts  65.4 us
    dot_general x8, matrix products, one_block(): jnp.einsum('hqk,khd->qhd', weights_low, value_rows, preferred_element_typ...  50.7 us
  transfers between devices with their start and end apart: 31, of which 23 were waited for; matrix products, arithmetic and copies ran while one was open for 27% of the time, Pallas kernels for 0%

commit v1 on v0

v1 whole, which is shorter than its diff:
```python
import functools

import jax
import jax.numpy as jnp
from jax import lax
from jax.experimental import pallas as pl
from jax.experimental.pallas import tpu as pltpu
from jax.sharding import PartitionSpec as P

HEAD_DIM = 72
GRID = 16
PATCHES = GRID * GRID
SPAN = 2 * GRID - 1


eps_norm = 1e-06
highest = lax.Precision.HIGHEST
f32 = jnp.float32
bf16 = jnp.bfloat16
ROWS_AXES = ("narrow", "wide")
MESH = pl.DeviceIdType.MESH


class Place:
    def __init__(self):
        wide = lax.axis_index("wide")
        self.z = lax.axis_index("narrow")
        self.y, self.x, self.c = wide // 4, (wide // 2) % 2, wide % 2

    def wide(self, flip_y=0, flip_x=0, flip_c=0):
        y = 1 - self.y if flip_y else self.y
        x = 1 - self.x if flip_x else self.x
        c = 1 - self.c if flip_c else self.c
        return y * 4 + x * 2 + c

    def along_z(self, steps):
        return lax.rem(self.z + steps, 4)

    def peers(self):
        across = [(self.wide(1, 0, 0), self.z), (self.wide(0, 1, 0), self.z), (self.wide(0, 0, 1), self.z)]
        return across + [(self.wide(), self.along_z(k)) for k in (1, 2, 3)]

    def greet(self):
        barrier = pltpu.get_barrier_semaphore()
        for peer in self.peers():
            pl.semaphore_signal(barrier, inc=1, device_id=peer, device_id_type=MESH)
        pl.semaphore_wait(barrier, 6)


def unit_cut(unit, rows):
    low = rows // 32 * 16
    return low if unit % 2 == 0 else rows - low


GATHER_SEMS = 3 + 24 + 28


class GatherUnit:
    def __init__(self, place, piece, whole, send, recv, cut):
        self.place, self.piece, self.whole = place, piece, whole
        self.send, self.recv = send, recv
        rows = piece.shape[0]
        self.halves = (pl.ds(0, cut), pl.ds(cut, rows - cut))
        self.whole_rows = pl.ds(0, rows)
        self.copies = {}

    def put(self, slot, peer, src, dst):
        copy = pltpu.make_async_remote_copy(
            src_ref=src, dst_ref=dst, send_sem=self.send.at[slot], recv_sem=self.recv.at[slot],
            device_id=peer, device_id_type=MESH,
        )
        copy.start()
        self.copies[slot] = copy

    def block(self, back, flip_y, flip_x, rows, flip_c=0):
        p = self.place
        return self.whole.at[p.along_z(4 - back), p.wide(flip_y, flip_x, flip_c), rows]

    def forward(self, slot, peer, back, flip_y, flip_x, rows):
        block = self.block(back, flip_y, flip_x, rows)
        self.put(slot, peer, block, block)

    def begin(self):
        p = self.place
        own = self.block(0, 0, 0, self.whole_rows)
        self.local = pltpu.make_async_copy(self.piece, own, self.send.at[GATHER_SEMS])
        self.local.start()
        for k in (1, 2, 3):
            self.put(k - 1, (p.wide(), p.along_z(k)), self.piece, own)
        for slot, peer, rows in ((3, (p.wide(1, 0), p.z), self.halves[0]), (15, (p.wide(0, 1), p.z), self.halves[1])):
            self.put(slot, peer, self.piece.at[rows], own.at[rows])
        self.put(27, (p.wide(0, 0, 1), p.z), self.piece, own)

    def second(self):
        p = self.place
        first, last = self.halves
        for k in (1, 2, 3):
            self.copies[k - 1].wait_recv()
            self.forward(3 + k, (p.wide(1, 0), p.z), k, 0, 0, first)
            self.forward(15 + k, (p.wide(0, 1), p.z), k, 0, 0, last)
            self.forward(27 + k, (p.wide(0, 0, 1), p.z), k, 0, 0, self.whole_rows)

    def third(self):
        p = self.place
        first, last = self.halves
        self.local.wait()
        for k in range(4):
            self.forward(7 + k, (p.wide(0, 1), p.z), k, 0, 0, first)
            self.forward(19 + k, (p.wide(1, 0), p.z), k, 0, 0, last)
        for k in range(4):
            self.copies[3 + k].wait_recv()
            self.forward(11 + k, (p.wide(0, 1), p.z), k, 1, 0, first)
            self.forward(31 + k, (p.wide(0, 0, 1), p.z), k, 1, 0, first)
            self.copies[15 + k].wait_recv()
            self.forward(23 + k, (p.wide(1, 0), p.z), k, 0, 1, last)
            self.forward(35 + k, (p.wide(0, 0, 1), p.z), k, 0, 1, last)

    def fourth(self):
        p = self.place
        first, last = self.halves
        core = (p.wide(0, 0, 1), p.z)
        for k in range(4):
            self.copies[7 + k].wait_recv()
            self.forward(39 + k, core, k, 0, 1, first)
            self.copies[19 + k].wait_recv()
            self.forward(43 + k, core, k, 1, 0, last)
        for k in range(4):
            self.copies[11 + k].wait_recv()
            self.forward(47 + k, core, k, 1, 1, first)
            self.copies[23 + k].wait_recv()
            self.forward(51 + k, core, k, 1, 1, last)

    def finish(self):
        for slot in range(27, 55):
            self.copies[slot].wait_recv()
        for slot in range(55):
            self.copies[slot].wait_send()


def gather_kernel(count, *refs):
    pieces, wholes = refs[:count], refs[count : 2 * count]
    send, recv = refs[2 * count :]
    place = Place()
    place.greet()
    units = [
        GatherUnit(place, pieces[u], wholes[u], send.at[u], recv.at[u], unit_cut(u, pieces[u].shape[0]))
        for u in range(count)
    ]
    for u in range(count + 3):
        if u < count:
            units[u].begin()
        if 0 <= u - 1 < count:
            units[u - 1].second()
            units[u - 1].third()
        if 0 <= u - 2 < count:
            units[u - 2].fourth()
        if 0 <= u - 3 < count:
            units[u - 3].finish()


def gather_units(pieces, collective_id):
    count = len(pieces)
    rows, cols = pieces[0].shape
    wholes = pl.pallas_call(
        functools.partial(gather_kernel, count),
        out_shape=[jax.ShapeDtypeStruct((4, 8, rows, cols), bf16)] * count,
        in_specs=[pl.BlockSpec(memory_space=pl.ANY)] * count,
        out_specs=[pl.BlockSpec(memory_space=pl.ANY)] * count,
        scratch_shapes=[pltpu.SemaphoreType.DMA((count, GATHER_SEMS + 1)), pltpu.SemaphoreType.DMA((count, GATHER_SEMS))],
        compiler_params=pltpu.CompilerParams(collective_id=collective_id, has_side_effects=True),
        name="gather_units",
    )(*pieces)
    return [w.reshape(4, 8 * rows, cols) for w in wholes]


SCATTER_SEMS = 4 * 5 + 3


def add_rows(total, part, rows):
    step = 16

    def one(at, carry):
        here = pl.ds(pl.multiple_of(at * step, step), step)
        both = total[here, :].astype(f32) + part[here, :].astype(f32)
        total[here, :] = both.astype(total.dtype)
        return carry

    lax.fori_loop(0, rows // step, one, 0)


class ScatterUnit:
    ORDER = (2, 1, 3, 0)

    def __init__(self, place, grads, out, total, from_core, far, near, from_z, send, recv, load, cut):
        self.place, self.grads, self.out = place, grads, out
        self.total, self.from_core, self.far, self.near, self.from_z = total, from_core, far, near, from_z
        self.send, self.recv, self.load = send, recv, load
        rows = grads.shape[4]
        self.rows, self.cut = rows, cut
        self.first, self.last = pl.ds(0, cut), pl.ds(cut, rows - cut)
        self.copies, self.loads = {}, {}

    def put(self, slot, peer, src, dst):
        copy = pltpu.make_async_remote_copy(
            src_ref=src, dst_ref=dst, send_sem=self.send.at[slot], recv_sem=self.recv.at[slot],
            device_id=peer, device_id_type=MESH,
        )
        copy.start()
        self.copies[slot] = copy

    def begin(self):
        p = self.place
        for k in self.ORDER:
            z = p.along_z(k)
            self.put(k, (p.wide(0, 0, 1), p.z), self.grads.at[z, :, :, 1 - p.c], self.from_core.at[k])
            self.loads[k] = pltpu.make_async_copy(self.grads.at[z, :, :, p.c], self.total.at[k], self.load.at[k])
            self.loads[k].start()

    def first_stage(self, k):
        p = self.place
        self.loads[k].wait()
        self.copies[k].wait_recv()
        for block in range(4):
            add_rows(self.total.at[k, block // 2, block % 2], self.from_core.at[k, block // 2, block % 2], self.rows)
        self.put(4 + k, (p.wide(0, 1), p.z), self.total.at[k, :, 1 - p.x, self.first], self.far.at[k, :, self.first])
        self.put(8 + k, (p.wide(1, 0), p.z), self.total.at[k, 1 - p.y, :, self.last], self.far.at[k, :, self.last])

    def second_stage(self, k):
        p = self.place
        self.copies[4 + k].wait_recv()
        for block in range(2):
            add_rows(self.total.at[k, block, p.x, self.first], self.far.at[k, block, self.first], self.cut)
        self.put(12 + k, (p.wide(1, 0), p.z), self.total.at[k, 1 - p.y, p.x, self.first], self.near.at[k, self.first])
        self.copies[8 + k].wait_recv()
        for block in range(2):
            add_rows(self.total.at[k, p.y, block, self.last], self.far.at[k, block, self.last], self.rows - self.cut)
        self.put(16 + k, (p.wide(0, 1), p.z), self.total.at[k, p.y, 1 - p.x, self.last], self.near.at[k, self.last])

    def third_stage(self, k):
        p = self.place
        self.copies[12 + k].wait_recv()
        self.copies[16 + k].wait_recv()
        add_rows(self.total.at[k, p.y, p.x], self.near.at[k], self.rows)
        if k:
            self.put(19 + k, (p.wide(), p.along_z(k)), self.total.at[k, p.y, p.x], self.from_z.at[k - 1])

    def finish(self):
        p = self.place
        for k in (1, 2, 3):
            self.copies[19 + k].wait_recv()
        own = self.total.at[0, p.y, p.x]
        step = 16

        def one(at, carry):
            here = pl.ds(pl.multiple_of(at * step, step), step)
            both = own[here, :].astype(f32)
            for k in range(3):
                both = both + self.from_z[k, here, :].astype(f32)
            self.out[here, :] = both
            return carry

        lax.fori_loop(0, self.rows // step, one, 0)
        for slot in self.copies:
            self.copies[slot].wait_send()


def scatter_scratch(count, rows, cols, cut):
    one = [
        pltpu.VMEM((4, 2, 2, rows, cols), bf16),
        pltpu.VMEM((4, 2, 2, rows, cols), bf16),
        pltpu.VMEM((4, 2, rows, cols), bf16),
        pltpu.VMEM((4, rows, cols), bf16),
        pltpu.VMEM((3, rows, cols), bf16),
    ]
    return one * count + [
        pltpu.SemaphoreType.DMA((count, SCATTER_SEMS)),
        pltpu.SemaphoreType.DMA((count, SCATTER_SEMS)),
        pltpu.SemaphoreType.DMA((count, 4)),
    ]


def scatter_kernel(count, *refs):
    grads, outs = refs[:count], refs[count : 2 * count]
    scratch = refs[2 * count : 7 * count]
    send, recv, load = refs[7 * count :]
    place = Place()
    place.greet()
    units = [
        ScatterUnit(place, grads[u], outs[u], *scratch[5 * u : 5 * u + 5], send.at[u], recv.at[u], load.at[u],
                    unit_cut(u, grads[u].shape[4]))
        for u in range(count)
    ]
    steps = [(u, k) for u in range(count) for k in ScatterUnit.ORDER]
    for u in range(count):
        units[u].begin()
    for at in range(len(steps) + 4):
        if at < len(steps):
            u, k = steps[at]
            units[u].first_stage(k)
        if 0 <= at - 1 < len(steps):
            u, k = steps[at - 1]
            units[u].second_stage(k)
        if 0 <= at - 2 < len(steps):
            u, k = steps[at - 2]
            units[u].third_stage(k)
        if 0 <= at - 4 < len(steps) and steps[at - 4][1] == 0:
            units[steps[at - 4][0]].finish()


def scatter_units(grads, collective_id):
    count = len(grads)
    cols = grads[0].shape[-1]
    rows = grads[0].shape[1] // 8
    return pl.pallas_call(
        functools.partial(scatter_kernel, count),
        out_shape=[jax.ShapeDtypeStruct((rows, cols), f32)] * count,
        in_specs=[pl.BlockSpec(memory_space=pl.ANY)] * count,
        out_specs=[pl.BlockSpec(memory_space=pltpu.VMEM)] * count,
        scratch_shapes=scatter_scratch(count, rows, cols, 0),
        compiler_params=pltpu.CompilerParams(
            collective_id=collective_id, has_side_effects=True, vmem_limit_bytes=62 * 2**20
        ),
        name="scatter_units",
    )(*[g.reshape(4, 2, 2, 2, rows, cols) for g in grads])


def by_links(rows):
    return lax.axis_size("wide") == 8 and lax.axis_size("narrow") == 4 and rows % 16 == 0


def gather_all(pieces):
    if by_links(pieces[0].shape[0]):
        return gather_units(pieces, 0)
    return [gather_unit(piece) for piece in pieces]


def scatter_all(grads):
    if by_links(grads[0].shape[1] // lax.axis_size("wide")):
        return scatter_units([item.astype(bf16) for item in grads], 1)
    return [scatter_unit(item).astype(f32) for item in grads]


def layer_norm(values, norm_gain, norm_shift):
    average = jnp.mean(values, axis=-1, keepdims=True)
    centred = values - average
    variance = jnp.mean(centred * centred, axis=-1, keepdims=True)
    scale = lax.rsqrt(variance + eps_norm)
    unit = centred * scale
    return unit * norm_gain + norm_shift, unit, scale


def layer_norm_back(grad, unit, scale, norm_gain):
    weighted = grad * norm_gain
    first = jnp.mean(weighted, axis=-1, keepdims=True)
    second = jnp.mean(weighted * unit, axis=-1, keepdims=True)
    from_norm = scale * (weighted - first - unit * second)
    return from_norm, jnp.sum(grad * unit, axis=0), jnp.sum(grad, axis=0)


def offset_onehot():
    near = jnp.arange(GRID, dtype=jnp.int32)
    span = jnp.arange(SPAN, dtype=jnp.int32)
    return (span[None, None, :] == near[:, None, None] - near[None, :, None] + (GRID - 1)).astype(f32)


def pair_bias(bias_table):
    steps_hot = offset_onehot()
    head_count = bias_table.shape[0]
    table_grid = bias_table.reshape(head_count, SPAN, SPAN)
    row_part = jnp.einsum("ixa,hab->hixb", steps_hot, table_grid, precision=highest)
    pairs = jnp.einsum("jyb,hixb->hijxy", steps_hot, row_part, precision=highest)
    return pairs.reshape(head_count, PATCHES, PATCHES)


def fold_bias_grad(pair_grad):
    steps_hot = offset_onehot()
    head_count = pair_grad.shape[0]
    grid_grad = pair_grad.reshape(head_count, GRID, GRID, GRID, GRID)
    col_part = jnp.einsum("jyb,hijxy->hixb", steps_hot, grid_grad, precision=highest)
    table_grad = jnp.einsum("ixa,hixb->hab", steps_hot, col_part, precision=highest)
    return table_grad.reshape(head_count, SPAN * SPAN)


def gather_unit(piece):
    parts = lax.axis_size("narrow")
    whole = lax.all_gather(piece, ROWS_AXES, axis=0, tiled=True)
    return whole.reshape(parts, whole.shape[0] // parts, whole.shape[1])


def scatter_unit(grads):
    flat = grads.astype(bf16).reshape(-1, grads.shape[-1])
    return lax.psum_scatter(flat, ROWS_AXES, scatter_dimension=0, tiled=True)


def to_heads(values):
    parts, rows, cols = values.shape
    split = values.reshape(parts, rows, cols // HEAD_DIM, HEAD_DIM)
    return split.transpose(0, 2, 1, 3).reshape(-1, rows, HEAD_DIM)


def from_heads(values, parts):
    heads, rows, _ = values.shape
    split = values.reshape(parts, heads // parts, rows, HEAD_DIM).transpose(0, 2, 1, 3)
    return split.reshape(parts, rows, -1)


def attention_forward(residual, proj, time_part, params, pairs):
    norm_gain, norm_shift, qkv_bias, out_bias = params
    parts = proj.shape[0]
    cols = proj.shape[2] // 4
    normed, unit, scale = layer_norm(residual, norm_gain[0], norm_shift[0])
    normed_low = normed.astype(bf16)
    spatial = jnp.einsum("rd,zdc->zrc", normed_low, proj[:, :, : 3 * cols], preferred_element_type=f32)
    offsets = time_part + jnp.stack([qkv_bias[0], jnp.zeros_like(qkv_bias[0]), qkv_bias[1]])
    offsets = offsets.reshape(3, parts, 1, cols)
    queries, key_rows, value_rows = (
        to_heads((spatial[:, :, j * cols : (j + 1) * cols] + offsets[j]).astype(bf16)) for j in range(3)
    )
    scores = jnp.einsum("hqd,hkd->hqk", queries, key_rows, preferred_element_type=f32)
    scores = scores * HEAD_DIM ** (-0.5) + pairs
    attention = jax.nn.softmax(scores, axis=-1)
    attention_low = attention.astype(bf16)
    mixed = jnp.einsum("hqk,hkd->hqd", attention_low, value_rows, preferred_element_type=f32)
    mixed_low = from_heads(mixed.astype(bf16), parts)
    branch = jnp.einsum("zrc,zdc->rd", mixed_low, proj[:, :, 3 * cols :], preferred_element_type=f32)
    middle = residual + (branch + out_bias[0])
    saved = (normed_low, unit, scale, queries, key_rows, value_rows, attention, mixed_low)
    return middle, saved


def mlp_forward(middle, up, down, params, up_bias):
    norm_gain, norm_shift, qkv_bias, out_bias = params
    parts = up.shape[0]
    normed, unit, scale = layer_norm(middle, norm_gain[1], norm_shift[1])
    normed_low = normed.astype(bf16)
    hidden = jnp.einsum("rd,zdc->zrc", normed_low, up, preferred_element_type=f32)
    hidden = hidden + up_bias.reshape(parts, 1, -1)
    activated = jax.nn.gelu(hidden, approximate=True).astype(bf16)
    branch = jnp.einsum("zrc,zdc->rd", activated, down, preferred_element_type=f32)
    return middle + (branch + out_bias[1]), (normed_low, unit, scale, hidden, activated)


def mlp_backward(gradient, up, down, params, saved):
    norm_gain = params[0]
    normed_low, unit, scale, hidden, activated = saved
    grad_low = gradient.astype(bf16)
    out_bias_grad = jnp.sum(grad_low.astype(f32), axis=0)
    down_grad = jnp.einsum("rd,zrc->zdc", grad_low, activated, preferred_element_type=f32)
    act_grad = jnp.einsum("rd,zdc->zrc", grad_low, down, preferred_element_type=f32)
    _, gelu_back = jax.vjp(lambda values: jax.nn.gelu(values, approximate=True), hidden)
    hidden_low = gelu_back(act_grad)[0].astype(bf16)
    up_bias_grad = jnp.sum(hidden_low.astype(f32), axis=1).reshape(-1)
    up_grad = jnp.einsum("rd,zrc->zdc", normed_low, hidden_low, preferred_element_type=f32)
    normed_grad = jnp.einsum("zrc,zdc->rd", hidden_low, up, preferred_element_type=f32)
    from_norm, gain_grad, shift_grad = layer_norm_back(normed_grad, unit, scale, norm_gain[1])
    return gradient + from_norm, up_grad, down_grad, (gain_grad, shift_grad, out_bias_grad, up_bias_grad)


def attention_backward(grad_mid, proj, params, saved):
    norm_gain = params[0]
    normed_low, unit, scale, queries, key_rows, value_rows, attention, mixed_low = saved
    parts = proj.shape[0]
    cols = proj.shape[2] // 4
    score_scale = HEAD_DIM ** (-0.5)
    mid_low = grad_mid.astype(bf16)
    out_bias_grad = jnp.sum(mid_low.astype(f32), axis=0)
    out_grad = jnp.einsum("rd,zrc->zdc", mid_low, mixed_low, preferred_element_type=f32)
    mixed_grad = jnp.einsum("rd,zdc->zrc", mid_low, proj[:, :, 3 * cols :], preferred_element_type=f32)
    mixed_grad = to_heads(mixed_grad.astype(bf16))
    dot_back = jnp.einsum("hqd,hkd->hqk", mixed_grad, value_rows, preferred_element_type=f32)
    score_grad = attention * (dot_back - jnp.sum(attention * dot_back, axis=-1, keepdims=True))
    score_low = score_grad.astype(bf16)
    table_grad = fold_bias_grad(score_low.astype(f32))
    query_grad = jnp.einsum("hqk,hkd->hqd", score_low, key_rows, preferred_element_type=f32) * score_scale
    key_grad = jnp.einsum("hqk,hqd->hkd", score_low, queries, preferred_element_type=f32) * score_scale
    value_grad = jnp.einsum("hqk,hqd->hkd", attention.astype(bf16), mixed_grad, preferred_element_type=f32)
    qkv_low = jnp.concatenate(
        [from_heads(item.astype(bf16), parts) for item in (query_grad, key_grad, value_grad)], axis=-1
    )
    spatial_grad = jnp.einsum("rd,zrc->zdc", normed_low, qkv_low, preferred_element_type=f32)
    proj_grad = jnp.concatenate([spatial_grad, out_grad], axis=-1)
    sums = jnp.sum(qkv_low.astype(f32), axis=1).reshape(parts, 3, cols).transpose(1, 0, 2).reshape(3, -1)
    normed_grad = jnp.einsum("zrc,zdc->rd", qkv_low, proj[:, :, : 3 * cols], preferred_element_type=f32)
    from_norm, gain_grad, shift_grad = layer_norm_back(normed_grad, unit, scale, norm_gain[0])
    return grad_mid + from_norm, proj_grad, sums, table_grad, (gain_grad, shift_grad, out_bias_grad)


def shards(
    tokens,
    cotangent,
    segment_ids,
    patch_pos,
    time_index,
    time_table,
    norm_gain,
    norm_shift,
    attn_weight,
    out_weight,
    qkv_bias,
    out_bias,
    mlp_weight,
    up_bias,
    rel_table,
):
    image_count = time_index.shape[0]
    layer_count = attn_weight.shape[0]
    narrow_at = lax.axis_index("narrow")
    wide_at = lax.axis_index("wide")
    wide_size = lax.axis_size("wide")
    own_rows = tokens.shape[0]
    in_rows, cols = attn_weight.shape[2:]
    image_local = segment_ids % image_count
    grid_slot = image_local * PATCHES + patch_pos
    own_slots = narrow_at * own_rows + jnp.arange(own_rows, dtype=jnp.int32)
    pick_in = (own_slots[:, None] == grid_slot[None, :]).astype(bf16)
    own_grid = lax.dynamic_slice_in_dim(grid_slot, narrow_at * own_rows, own_rows)
    pick_out = (own_grid[:, None] == jnp.arange(grid_slot.shape[0], dtype=jnp.int32)[None, :]).astype(bf16)

    def to_images(rows):
        every = lax.all_gather(rows, "narrow", axis=0, tiled=True)
        return jnp.dot(pick_in, every, preferred_element_type=f32)

    def to_rows(rows):
        every = lax.all_gather(rows, "narrow", axis=0, tiled=True)
        return jnp.dot(pick_out, every, preferred_element_type=f32).astype(bf16)

    steps_all = lax.all_gather(time_index, "wide", axis=0, tiled=True)
    step_hot = (steps_all[:, None] == jnp.arange(time_table.shape[0], dtype=jnp.int32)[None, :]).astype(bf16)
    time_rows = jnp.dot(step_hot, time_table, preferred_element_type=f32).astype(bf16)
    time_slice = lax.dynamic_slice_in_dim(time_rows, wide_at * in_rows, in_rows, axis=1)
    time_weight = attn_weight[:, 3:6]
    time_share = jnp.einsum("id,ljdc->ljic", time_slice, time_weight, preferred_element_type=f32)
    time_share = lax.psum_scatter(time_share, "wide", scatter_dimension=2, tiled=True)
    time_share = lax.all_gather(time_share, "narrow", axis=3, tiled=True)
    time_part = lax.dynamic_index_in_dim(time_share, narrow_at, axis=2, keepdims=False)

    tables = lax.all_gather(rel_table, "narrow", axis=1, tiled=True)
    qkv_bias_all = lax.all_gather(qkv_bias, "narrow", axis=2, tiled=True)
    up_bias_all = lax.all_gather(up_bias, "narrow", axis=1, tiled=True)

    def layer_params(at):
        return (norm_gain[at], norm_shift[at], qkv_bias_all[at], out_bias[at])

    weights = []
    for at in range(layer_count):
        packed = jnp.concatenate([attn_weight[at, 0], attn_weight[at, 1], attn_weight[at, 2], out_weight[at]], axis=1)
        weights += [packed, mlp_weight[at, 0], mlp_weight[at, 1]]
    weights = gather_all(weights)
    weights = [weights[3 * at : 3 * at + 3] for at in range(layer_count)]

    residual = to_images(tokens)
    kept = []
    for at in range(layer_count):
        pairs = pair_bias(tables[at])
        middle, attn_saved = attention_forward(residual, weights[at][0], time_part[at], layer_params(at), pairs)
        residual, mlp_saved = mlp_forward(middle, weights[at][1], weights[at][2], layer_params(at), up_bias_all[at])
        kept.append((attn_saved, mlp_saved))
    block_output = to_rows(residual.astype(bf16))
    gradient = to_images(cotangent)
    attn_grads, out_grads, mlp_grads = [], [], []
    time_sums, small = [], []
    for at in reversed(range(layer_count)):
        attn_saved, mlp_saved = kept[at]
        grad_mid, up_grad, down_grad, mlp_small = mlp_backward(
            gradient, weights[at][1], weights[at][2], layer_params(at), mlp_saved
        )
        gradient, proj_grad, sums, table_grad, attn_small = attention_backward(
            grad_mid, weights[at][0], layer_params(at), attn_saved
        )
        down_part, up_part, packed = scatter_all([down_grad, up_grad, proj_grad])
        mlp_grads.insert(0, jnp.stack([up_part, down_part]))
        attn_grads.insert(0, jnp.stack([packed[:, j * cols : (j + 1) * cols] for j in range(3)]))
        out_grads.insert(0, packed[:, 3 * cols :])
        time_sums.insert(0, sums)
        small.insert(
            0,
            (
                jnp.stack([attn_small[0], mlp_small[0]]),
                jnp.stack([attn_small[1], mlp_small[1]]),
                jnp.stack([attn_small[2], mlp_small[2]]),
                jnp.stack([sums[0], sums[2]]),
                mlp_small[3],
                table_grad,
            ),
        )
    input_grad = to_rows(gradient.astype(bf16))

    def stacked(index_at):
        return jnp.stack([entry[index_at] for entry in small])

    totals = lax.psum(tuple(stacked(index_at) for index_at in range(6)), ("wide", "narrow"))

    def own_part(array, axis):
        size = array.shape[axis] // lax.axis_size("narrow")
        return lax.dynamic_slice_in_dim(array, narrow_at * size, size, axis=axis)

    time_low = jnp.stack(time_sums).astype(bf16)
    time_all = lax.all_gather(time_low, ("wide", "narrow"), axis=0, tiled=False)
    time_own = own_part(time_all, 3)
    time_weight_grad = jnp.einsum("id,iljc->ljdc", time_slice, time_own, preferred_element_type=f32)
    trow_share = jnp.einsum("iljc,ljdc->id", time_own, time_weight, preferred_element_type=f32)
    trow_share = lax.psum(trow_share, "narrow")
    trow = lax.all_gather(trow_share, "wide", axis=1, tiled=True)
    time_grad = jnp.einsum("is,id->sd", step_hot.astype(f32), trow, precision=highest)
    attn_grad = jnp.concatenate([jnp.stack(attn_grads).astype(f32), time_weight_grad], axis=1)
    return (
        block_output,
        input_grad,
        time_grad,
        totals[0],
        totals[1],
        attn_grad,
        jnp.stack(out_grads).astype(f32),
        own_part(totals[3], 2),
        totals[2],
        jnp.stack(mlp_grads).astype(f32),
        own_part(totals[4], 1),
        own_part(totals[5], 1),
    )


def solution(mesh):
    return jax.shard_map(
        shards,
        mesh=mesh,
        in_specs=(
            P(("wide", "narrow"), None),
            P(("wide", "narrow"), None),
            P("wide"),
            P("wide"),
            P("wide"),
            P(),
            P(),
            P(),
            P(None, None, "wide", "narrow"),
            P(None, "wide", "narrow"),
            P(None, None, "narrow"),
            P(),
            P(None, None, "wide", "narrow"),
            P(None, "narrow"),
            P(None, "narrow", None),
        ),
        out_specs=(
            P(("wide", "narrow"), None),
            P(("wide", "narrow"), None),
            P(),
            P(),
            P(),
            P(None, None, "wide", "narrow"),
            P(None, "wide", "narrow"),
            P(None, None, "narrow"),
            P(),
            P(None, None, "wide", "narrow"),
            P(None, "narrow"),
            P(None, "narrow", None),
        ),
        check_vma=False,
    )
```

time: 2260 us -> 1390 us (0.62)
  waiting for transfers between devices: 1030 us -> 1.21 us
  Pallas kernels: 0 us -> 573 us
  local copies, waits for them, and re-layouts: 554 us -> 213 us
  blocking collectives: 96.4 us -> 260 us
  other arithmetic: 181 us -> 47.2 us
  matrix products: 366 us -> 273 us
    pallas_call x0 -> x3, Pallas kernels: none -> 573 us  [the longest x2 291 us: scatter_units(): pl.pallas_call(functools.partial(scatter_kernel, count), out_shape=[jax.S...]
    all_gather x14 -> x4, waiting for transfers between devices: 498 us -> 0.05 us  [the longest x2 0.03 us: to_images(): every = lax.all_gather(rows, 'narrow', axis=0, tiled=True)]
    reduce_scatter x14 -> x0, waiting for transfers between devices: 381 us -> none  [the longest x10 381 us: rows_share(): lax.psum_scatter(term.astype(jnp.bfloat16), 'narrow', scatter_dimension=0...]
    another operation x56 -> x37, local copies, waits for them, and re-layouts: 236 us -> 8.17 us  [the longest x30 227 us: score_block(): jnp.tile(pairs, (1, queries.shape[0] // patches, key_rows.shape[0] // pat...]
    all_gather x2 -> x6, blocking collectives: 30.1 us -> 234 us  [the longest x1 80.4 us: shards(): time_all = lax.all_gather(time_low, ('wide', 'narrow'), axis=0, tiled=False)]
    psum x1 -> x2, waiting for transfers between devices: 141 us -> 0.01 us  [shards(): lax.psum(tuple((stacked(index_at) for index_at in range(6))), ('wide', 'n...]
    gather x25 -> x0, local copies, waits for them, and re-layouts: 140 us -> none  [the longest x8 34.7 us: attention_part(): mixed_heads = jnp.take(mixed_s, target, axis=0)]
    dot_general x74 -> x45, matrix products: 338 us -> 214 us  [the longest x2 22.4 us: mlp_backward(): jnp.einsum('rd,zdc->zrc', grad_low, down, preferred_element_type=f32)]
  transfers between devices with their start and end apart: 31 -> 7, of which waited for: 23 -> 0; matrix products, arithmetic and copies ran while one was open for 27% -> 25% of each run, Pallas kernels for 0% -> 41%
where the time goes in v1:
time: 1390 us
  Pallas kernels  573 us (41%)
  matrix products  273 us (20%)
  blocking collectives  260 us (19%)
  local copies, waits for them, and re-layouts  213 us (15%)
  other arithmetic  47.2 us (3%)
  between operations  19.3 us (1%)
    pallas_call x2, Pallas kernels, scatter_units(): pl.pallas_call(functools.partial(scatter_kernel, count), out_shape=[jax.S...  291 us
    pallas_call x1, Pallas kernels, gather_units(): pl.pallas_call(functools.partial(gather_kernel, count), out_shape=[jax.Sh...  283 us
    all_gather x1, blocking collectives, shards(): time_all = lax.all_gather(time_low, ('wide', 'narrow'), axis=0, tiled=False)  80.4 us
    all_gather x1, blocking collectives, shards(): time_share = lax.all_gather(time_share, 'narrow', axis=3, tiled=True)  77.3 us
    reshape x4, local copies, waits for them, and re-layouts, pair_bias(): return pairs.reshape(head_count, PATCHES, PATCHES)  57.9 us
    all_gather x1, blocking collectives, shards(): qkv_bias_all = lax.all_gather(qkv_bias, 'narrow', axis=2, tiled=True)  39 us
    dot_general x2, matrix products, pair_bias(): jnp.einsum('jyb,hixb->hijxy', steps_hot, row_part, precision=highest)  34.8 us
    reshape x2, local copies, waits for them, and re-layouts, fold_bias_grad(): grid_grad = pair_grad.reshape(head_count, GRID, GRID, GRID, GRID)  31.8 us
  transfers between devices with their start and end apart: 7, of which 0 were waited for; matrix products, arithmetic and copies ran while one was open for 25% of the time, Pallas kernels for 41%

profile of v1, /device:TPU:0, one launch (start us, length us, event | category | flops | bytes accessed | tf_op | source)
XLA Modules:
  0.0 1387.4 jit_solution(7938510475731913866)
XLA Ops:
  11.0 9.5 all-reduce
  26.9 13.4 all_gather.39
  42.4 14.5 %all_gather.38 = f32[2,16,961]{2,0,1:T(2,128)S(1)} all-gather(f32[2,4,961]{2,0,1:T(2,128)S(1)} %copy.305), channel_id=1, replica_groups=mesh['wide'=8,'narrow'=4] {'narrow'}, dimensions={1}, use_global_device_ids=true | all-gather | bytes 153760 | tf_op jit(solution)/shard_map/all_gather | solution.py:537
  58.0 39.0 %all_gather.37 = f32[2,2,1152]{1,0,2:T(2,128)S(1)} all-gather(f32[2,2,288]{1,0,2:T(2,128)S(1)} %copy.300), channel_id=1, replica_groups=mesh['wide'=8,'narrow'=4] {'narrow'}, dimensions={2}, use_global_device_ids=true | all-gather | bytes 23040 | tf_op jit(solution)/shard_map/all_gather | solution.py:538
  97.0 29.2 %slice_reduce_fusion.1 = (f32[1152]{0:T(1024)S(1)}, f32[1152]{0:T(1024)S(1)}, f32[1152]{0:T(1024)S(1)}, f32[1152]{0:T(1024)S(1)}) fusion(f32[2,2,1152]{1,0,2:T(2,128)S(1)} %all_gather.37), kind=kLoop, calls=%fused_computation.197 | loop fusion | bytes 36864 | tf_op jit(solution)/shard_map/slice | solution.py:414
  131.7 17.7 %convolution_bitcast_fusion = f32[16,16,16,16,16]{4,3,2,1,0:T(8,128)} fusion(f32[16,16,16,31]{3,1,0,2:T(8,128)S(1)} %fusion.158, pred[16,16,31,1,1]{2,0,1,4,3:T(8,128)(4,1)S(1)} %get-tuple-element.158), kind=kOutput, calls=%fused_computation.6 | convolution fusion | flops 390070272 | bytes 4710144 | tf_op jit(solution)/shard_map/jyb,hixb->hijxy/dot_general | solution.py:371
  149.3 23.5 %reshape.451 = f32[16,256,256]{2,1,0:T(8,128)} reshape(f32[16,16,16,16,16]{4,3,2,1,0:T(8,128)} %convolution_bitcast_fusion) | data formatting | bytes 8388608 | tf_op jit(solution)/shard_map/reshape | solution.py:372
  178.2 17.1 %convolution_bitcast_fusion.1 = f32[16,16,16,16,16]{4,3,2,1,0:T(8,128)} fusion(f32[16,16,16,31]{3,1,0,2:T(8,128)S(1)} %fusion.160, pred[16,16,31,1,1]{2,0,1,4,3:T(8,128)(4,1)S(1)} %get-tuple-element.158), kind=kOutput, calls=%fused_computation.7 | convolution fusion | flops 390070272 | bytes 4710144 | tf_op jit(solution)/shard_map/jyb,hixb->hijxy/dot_general | solution.py:371
  195.3 23.5 %reshape.449 = f32[16,256,256]{2,1,0:T(8,128)} reshape(f32[16,16,16,16,16]{4,3,2,1,0:T(8,128)} %convolution_bitcast_fusion.1) | data formatting | bytes 8388608 | tf_op jit(solution)/shard_map/reshape | solution.py:372
  228.8 282.5 %gather_units.1 = (bf16[4,8,144,1152]{3,2,1,0:T(8,128)(2,1)}, bf16[4,8,144,1152]{3,2,1,0:T(8,128)(2,1)}, bf16[4,8,144,1152]{3,2,1,0:T(8,128)(2,1)}, bf16[4,8,144...) custom-call(bf16[144,1152]{1,0:T(8,128)(2,1)} %concatenate.65.refs_0_, ...), custom_call_target="tpu_custom_call" | custom-call | tf_op jit(solution)/shard_map/gather_units/pallas_call | solution.py:164
  513.2 77.3 %all_gather.36 = f32[2,3,4,1152]{2,0,1,3:T(2,128)S(1)} all-gather(f32[2,3,4,288]{2,0,1,3:T(2,128)S(1)} %copy.298), channel_id=1, replica_groups=mesh['wide'=8,'narrow'=4] {'narrow'}, dimensions={3}, use_global_device_ids=true | all-gather | bytes 138240 | tf_op jit(solution)/shard_map/all_gather | solution.py:534
  635.3 9.2 convolution_add_fusion.1
  644.5 9.3 fusion.228
  687.4 9.1 convolution_add_fusion
  699.2 11.4 convert_reduce_fusion
  741.9 11.0 convert_reduce_fusion.1
  796.6 17.4 %reshape.403 = bf16[16,16,16,16,16]{2,1,4,3,0:T(8,128)(2,1)} reshape(bf16[16,256,256]{1,2,0:T(8,128)(2,1)} %copy-done) | data formatting | bytes 4194304 | tf_op jit(solution)/shard_map/reshape | solution.py:378
  814.0 14.4 %reshape.404 = bf16[16,16,16,16,16]{2,1,4,3,0:T(8,128)(2,1)} reshape(bf16[16,256,256]{1,2,0:T(8,128)(2,1)S(1)} %multiply_convert_fusion.1) | data formatting | bytes 4194304 | tf_op jit(solution)/shard_map/reshape | solution.py:378
  828.4 9.8 fusion.72
  839.2 9.0 fusion.197
  850.4 9.0 fusion.195
  866.6 80.4 %all_gather.43 = bf16[32,2,3,1152]{3,1,2,0:T(2,128)(2,1)} all-gather(bf16[1,2,3,1152]{3,1,2,0:T(2,128)(2,1)S(1)} %copy.345), channel_id=1, replica_groups=mesh['wide'=8,'narrow'=4] {'wide','narrow'}, dimensions={0}, use_global_device_ids=true | all-gather | bytes 456192 | tf_op jit(solution)/shard_map/all_gather | solution.py:598
  955.1 11.4 copy.351
  966.5 11.4 copy.355
  978.6 9.5 convolution_convert_fusion.2
  995.8 9.8 convolution_convert_fusion.3
  1005.6 9.5 convolution_convert_fusion.1
  1016.4 13.1 pad_maximum_fusion.refs_2_
  1037.1 16.9 %psum.49 = f32[32,144]{1,0:T(8,128)S(1)} all-reduce(f32[32,144]{1,0:T(8,128)S(1)} %convolution_bitcast_fusion.8), channel_id=1, replica_groups=mesh['wide'=8,'narrow'=4] {'narrow'}, use_global_device_ids=true, to_apply=%region_25.26 | all-reduce | flops 4608 | bytes 36864 | tf_op jit(solution)/shard_map/psum | solution.py:602
  1054.0 9.2 all-gather
  1063.5 146.2 %scatter_units.2 = (f32[144,1152]{1,0:T(8,128)}, f32[144,1152]{1,0:T(8,128)}, f32[144,1152]{1,0:T(8,128)}) custom-call(bf16[4,2,2,2,144,1152]{5,4,3,2,1,0:T(8,128)(2,1)} %bitcast.454, bf16[4,2,2,2,144,1152]{5,4,3,2,1,0:T(8,128)(2,1)} %bitcast.445, bf16[4,2,2,2,144,1152]{5,4,3,2,1,0:T(8,128)(2,1)} %pad_maximum_fusion.refs_2_), custom_call_target="tpu_custom_call" | custom-call | tf_op jit(solution)/shard_map/scatter_units/pallas_call | solution.py:314
  1209.8 144.6 %scatter_units.3 = (f32[144,1152]{1,0:T(8,128)}, f32[144,1152]{1,0:T(8,128)}, f32[144,1152]{1,0:T(8,128)}) custom-call(bf16[4,2,2,2,144,1152]{5,4,3,2,1,0:T(8,128)(2,1)} %bitcast.453, bf16[4,2,2,2,144,1152]{5,4,3,2,1,0:T(8,128)(2,1)} %bitcast.446, bf16[4,2,2,2,144,1152]{5,4,3,2,1,0:T(8,128)(2,1)} %pad_maximum_fusion.1.refs_2_), custom_call_target="tpu_custom_call" | custom-call | tf_op jit(solution)/shard_map/scatter_units/pallas_call | solution.py:314
  (503 shorter events, 249.4 us)
Async XLA Ops:
  8.0 15.3 %copy-start.33 = (bf16[2,6,144,288]{3,2,1,0:T(8,128)(2,1)S(1)}, bf16[2,6,144,288]{3,2,1,0:T(8,128)(2,1)}, u32[]{:S(2)}) copy-start(bf16[2,6,144,288]{3,2,1,0:T(8,128)(2,1)} %param.23) | copy-start | bytes 2985988
  8.0 503.4 %all-reduce.9.cloned.1.call-start = ((), (), s32[]{:S(2)}) async-start(), calls=%async_computation.5 | async-start | bytes 589824
  24.3 33.2 %copy-start.59 = (bf16[2,144,288]{2,1,0:T(8,128)(2,1)S(1)}, bf16[2,144,288]{2,1,0:T(8,128)(2,1)}, u32[]{:S(2)}) copy-start(bf16[2,144,288]{2,1,0:T(8,128)(2,1)} %param.24) | copy-start | bytes 497668
  24.3 33.5 %copy-start.103 = (f32[2,2,288]{2,1,0:T(2,128)S(1)}, f32[2,2,288]{2,1,0:T(2,128)}, u32[]{:S(2)}) copy-start(f32[2,2,288]{2,1,0:T(2,128)} %param.25) | copy-start | bytes 13828
  24.3 581.7 %all-gather.6.cloned.1.call-start = ((), (), s32[]{:S(2)}) async-start(), calls=%async_computation | async-start | bytes 2949120 | tf_op jit(solution)/shard_map/all_gather | solution.py:520
  24.9 671.6 %all-gather.10.cloned.1.call-start = ((), (), s32[]{:S(2)}) async-start(), calls=%async_computation.2 | async-start | bytes 2949120 | tf_op jit(solution)/shard_map/all_gather | solution.py:520
  25.5 1341.6 %all-reduce.11.cloned.1.call-start = ((), (), s32[]{:S(2)}) async-start(), calls=%async_computation.6 | async-start | bytes 221184 | tf_op jit(solution)/shard_map/psum | solution.py:591
  26.1 31.4 %copy-start.61 = (s32[16,16]{0,1:T(8,128)}, s32[16,16]{0,1:T(8,128)S(1)}, u32[]{:S(2)}) copy-start(s32[16,16]{0,1:T(8,128)S(1)} %subtract_add_fusion) | copy-start | bytes 3076
  57.8 70.8 %copy-start.35 = (bf16[2,2,144,1152]{3,2,1,0:T(8,128)(2,1)S(1)}, bf16[2,2,144,1152]{3,2,1,0:T(8,128)(2,1)}, u32[]{:S(2)}) copy-start(bf16[2,2,144,1152]{3,2,1,0:T(8,128)(2,1)} %param.27) | copy-start | bytes 3981316
  97.0 32.7 %copy-start.58 = (pred[16,16,31]{2,0,1:T(8,128)(4,1)S(1)}, pred[16,16,31]{2,0,1:T(8,128)(4,1)}, u32[]{:S(2)}) copy-start(pred[16,16,31]{2,0,1:T(8,128)(4,1)} %get-tuple-element.159) | copy-start | bytes 23812
  225.6 285.8 %copy-start.101 = (s32[1024]{0:T(1024)}, s32[1024]{0:T(1024)S(1)}, u32[]{:S(2)}) copy-start(s32[1024]{0:T(1024)S(1)} %fusion.182) | copy-start | bytes 12292
  608.7 21.5 %copy-start.20 = (f32[256,1152]{1,0:T(8,128)}, f32[256,1152]{1,0:T(8,128)S(1)}, u32[]{:S(2)}) copy-start(f32[256,1152]{1,0:T(8,128)S(1)} %get-tuple-element.165) | copy-start | bytes 3538948
  630.2 14.3 %slice-start.8 = ((s8[10616832]{0:T(1024)(128)(4,1)}), s8[4194304]{0:T(1024)(128)(4,1)S(1)}, s32[]{:S(2)}) async-start(s8[10616832]{0:T(1024)(128)(4,1)} %bitcast.499), calls=%async_computation.15 | async-start | bytes 8388608
  635.0 121.5 %copy-start.5 = (f32[256,1152]{1,0:T(8,128)}, f32[256,1152]{1,0:T(8,128)S(1)}, u32[]{:S(2)}) copy-start(f32[256,1152]{1,0:T(8,128)S(1)} %get-tuple-element.169) | copy-start | bytes 3538948
  635.0 121.5 %copy-start.84 = (f32[256]{0:T(256)}, f32[256]{0:T(256)S(1)}, u32[]{:S(2)}) copy-start(f32[256]{0:T(256)S(1)} %broadcast_multiply_fusion.10) | copy-start | bytes 3076
  635.3 121.2 %copy-start.91 = (f32[256]{0:T(256)}, f32[256]{0:T(256)S(1)}, u32[]{:S(2)}) copy-start(f32[256]{0:T(256)S(1)} %add_rsqrt_fusion.2) | copy-start | bytes 3076
  687.0 27.1 %copy-start.6 = (f32[256,1152]{1,0:T(8,128)}, f32[256,1152]{1,0:T(8,128)S(1)}, u32[]{:S(2)}) copy-start(f32[256,1152]{1,0:T(8,128)S(1)} %get-tuple-element.175) | copy-start | bytes 3538948
  687.0 27.1 %copy-start.85 = (f32[256]{0:T(256)}, f32[256]{0:T(256)S(1)}, u32[]{:S(2)}) copy-start(f32[256]{0:T(256)S(1)} %broadcast_multiply_fusion.8) | copy-start | bytes 3076
  687.3 26.9 %copy-start.92 = (f32[256]{0:T(256)}, f32[256]{0:T(256)S(1)}, u32[]{:S(2)}) copy-start(f32[256]{0:T(256)S(1)} %add_rsqrt_fusion) | copy-start | bytes 3076
  696.5 14.2 %slice-start.14 = ((s8[10616832]{0:T(1024)(128)(4,1)}), s8[4194304]{0:T(1024)(128)(4,1)S(1)}, s32[]{:S(2)}) async-start(s8[10616832]{0:T(1024)(128)(4,1)} %bitcast.509), calls=%async_computation.21 | async-start | bytes 8388608
  699.2 15.0 %copy-start.39 = (f32[256,1152]{1,0:T(8,128)}, f32[256,1152]{1,0:T(8,128)S(1)}, u32[]{:S(2)}) copy-start(f32[256,1152]{1,0:T(8,128)S(1)} %fusion.95) | copy-start | bytes 3538948
  740.2 12.7 slice-start.5
  741.9 14.6 %copy-start.26 = (f32[256,1152]{1,0:T(8,128)}, f32[256,1152]{1,0:T(8,128)S(1)}, u32[]{:S(2)}) copy-start(f32[256,1152]{1,0:T(8,128)S(1)} %get-tuple-element.86) | copy-start | bytes 3538948
  814.0 14.5 %copy-start.7 = (f32[256,1152]{1,0:T(8,128)S(1)}, f32[256,1152]{1,0:T(8,128)}, u32[]{:S(2)}) copy-start(f32[256,1152]{1,0:T(8,128)} %copy-done.6) | copy-start | bytes 3538948
  814.0 14.5 %copy-start.94 = (f32[1152]{0:T(1024)S(1)}, f32[1152]{0:T(1024)}, u32[]{:S(2)}) copy-start(f32[1152]{0:T(1024)} %get-tuple-element.68) | copy-start | bytes 13828
  865.1 504.7 %all-reduce.7.cloned.1.call-start = ((), (), s32[]{:S(2)}) async-start(), calls=%async_computation.4 | async-start | bytes 262144 | tf_op jit(solution)/shard_map/psum | solution.py:591
  865.9 505.4 %all-gather.8.cloned.1.call-start = ((), (), s32[]{:S(2)}) async-start(), calls=%async_computation.1 | async-start | bytes 2949120 | tf_op jit(solution)/shard_map/all_gather | solution.py:524
  866.5 508.1 %all-gather.12.cloned.1.call-start = ((), (), s32[]{:S(2)}) async-start(), calls=%async_computation.3 | async-start | bytes 2949120 | tf_op jit(solution)/shard_map/all_gather | solution.py:524
  1016.3 20.5 %copy-start.51 = (bf16[32,2,3,288]{3,1,2,0:T(2,128)(2,1)}, bf16[32,2,3,288]{3,1,2,0:T(2,128)(2,1)S(1)}, u32[]{:S(2)}) copy-start(bf16[32,2,3,288]{3,1,2,0:T(2,128)(2,1)S(1)} %constant_dynamic-slice_fusion.4) | copy-start | bytes 331780
  1016.3 13.1 slice-start
  1016.4 13.1 slice-start.1
  1209.8 144.6 %copy-start.37 = (f32[144,1152]{1,0:T(8,128)S(1)}, f32[144,1152]{1,0:T(8,128)}, u32[]{:S(2)}) copy-start(f32[144,1152]{1,0:T(8,128)} %get-tuple-element.30) | copy-start | bytes 1990660
  (106 other events, 555.3 us)
Sparse Core Ops, SparseCore 0:
  24.4 52.7 all-reduce.8
  865.3 181.0 all-reduce.10
  1051.9 152.6 all-reduce.6
Sparse Core Ops, SparseCore 1:
  26.4 69.7 all-gather.5
  97.5 49.7 all-gather.9
  868.5 56.5 all-gather.7
  1015.2 48.4 all-gather.11

commit v2 on v1

v2 whole, which is shorter than its diff:
```python
import functools
import math

import jax
import jax.numpy as jnp
from jax import lax
from jax.experimental import pallas as pl
from jax.experimental.pallas import tpu as pltpu
from jax.sharding import PartitionSpec as P

HEAD_DIM = 72
GRID = 16
PATCHES = GRID * GRID
SPAN = 2 * GRID - 1


eps_norm = 1e-06
highest = lax.Precision.HIGHEST
f32 = jnp.float32
bf16 = jnp.bfloat16
ROWS_AXES = ("narrow", "wide")
MESH = pl.DeviceIdType.MESH


def layer_norm(values, norm_gain, norm_shift):
    average = jnp.mean(values, axis=-1, keepdims=True)
    centred = values - average
    variance = jnp.mean(centred * centred, axis=-1, keepdims=True)
    scale = lax.rsqrt(variance + eps_norm)
    unit = centred * scale
    return unit * norm_gain + norm_shift, unit, scale


def layer_norm_back(grad, unit, scale, norm_gain):
    weighted = grad * norm_gain
    first = jnp.mean(weighted, axis=-1, keepdims=True)
    second = jnp.mean(weighted * unit, axis=-1, keepdims=True)
    from_norm = scale * (weighted - first - unit * second)
    return from_norm, jnp.sum(grad * unit, axis=0), jnp.sum(grad, axis=0)


def offset_onehot():
    near = jnp.arange(GRID, dtype=jnp.int32)
    span = jnp.arange(SPAN, dtype=jnp.int32)
    return (span[None, None, :] == near[:, None, None] - near[None, :, None] + (GRID - 1)).astype(f32)


def pair_bias(bias_table):
    steps_hot = offset_onehot()
    head_count = bias_table.shape[0]
    table_grid = bias_table.reshape(head_count, SPAN, SPAN)
    row_part = jnp.einsum("ixa,hab->hixb", steps_hot, table_grid, precision=highest)
    pairs = jnp.einsum("jyb,hixb->hijxy", steps_hot, row_part, precision=highest)
    return pairs.reshape(head_count, PATCHES, PATCHES)


def fold_bias_grad(pair_grad):
    steps_hot = offset_onehot()
    head_count = pair_grad.shape[0]
    grid_grad = pair_grad.reshape(head_count, GRID, GRID, GRID, GRID)
    col_part = jnp.einsum("jyb,hijxy->hixb", steps_hot, grid_grad, precision=highest)
    table_grad = jnp.einsum("ixa,hixb->hab", steps_hot, col_part, precision=highest)
    return table_grad.reshape(head_count, SPAN * SPAN)


def gather_unit(piece):
    parts = lax.axis_size("narrow")
    whole = lax.all_gather(piece, ROWS_AXES, axis=0, tiled=True)
    return whole.reshape(parts, whole.shape[0] // parts, whole.shape[1])


def scatter_unit(grads):
    flat = grads.astype(bf16).reshape(-1, grads.shape[-1])
    return lax.psum_scatter(flat, ROWS_AXES, scatter_dimension=0, tiled=True)


def to_heads(values):
    parts, rows, cols = values.shape
    split = values.reshape(parts, rows, cols // HEAD_DIM, HEAD_DIM)
    return split.transpose(0, 2, 1, 3).reshape(-1, rows, HEAD_DIM)


def from_heads(values, parts):
    heads, rows, _ = values.shape
    split = values.reshape(parts, heads // parts, rows, HEAD_DIM).transpose(0, 2, 1, 3)
    return split.reshape(parts, rows, -1)


def attention_forward(residual, proj, time_part, params, pairs):
    norm_gain, norm_shift, qkv_bias, out_bias = params
    parts = proj.shape[0]
    cols = proj.shape[2] // 4
    normed, unit, scale = layer_norm(residual, norm_gain[0], norm_shift[0])
    normed_low = normed.astype(bf16)
    spatial = jnp.einsum("rd,zdc->zrc", normed_low, proj[:, :, : 3 * cols], preferred_element_type=f32)
    offsets = time_part + jnp.stack([qkv_bias[0], jnp.zeros_like(qkv_bias[0]), qkv_bias[1]])
    offsets = offsets.reshape(3, parts, 1, cols)
    queries, key_rows, value_rows = (
        to_heads((spatial[:, :, j * cols : (j + 1) * cols] + offsets[j]).astype(bf16)) for j in range(3)
    )
    scores = jnp.einsum("hqd,hkd->hqk", queries, key_rows, preferred_element_type=f32)
    scores = scores * HEAD_DIM ** (-0.5) + pairs
    attention = jax.nn.softmax(scores, axis=-1)
    attention_low = attention.astype(bf16)
    mixed = jnp.einsum("hqk,hkd->hqd", attention_low, value_rows, preferred_element_type=f32)
    mixed_low = from_heads(mixed.astype(bf16), parts)
    branch = jnp.einsum("zrc,zdc->rd", mixed_low, proj[:, :, 3 * cols :], preferred_element_type=f32)
    middle = residual + (branch + out_bias[0])
    saved = (normed_low, unit, scale, queries, key_rows, value_rows, attention, mixed_low)
    return middle, saved


def mlp_forward(middle, up, down, params, up_bias):
    norm_gain, norm_shift, qkv_bias, out_bias = params
    parts = up.shape[0]
    normed, unit, scale = layer_norm(middle, norm_gain[1], norm_shift[1])
    normed_low = normed.astype(bf16)
    hidden = jnp.einsum("rd,zdc->zrc", normed_low, up, preferred_element_type=f32)
    hidden = hidden + up_bias.reshape(parts, 1, -1)
    activated = jax.nn.gelu(hidden, approximate=True).astype(bf16)
    branch = jnp.einsum("zrc,zdc->rd", activated, down, preferred_element_type=f32)
    return middle + (branch + out_bias[1]), (normed_low, unit, scale, hidden, activated)


def mlp_backward(gradient, up, down, params, saved):
    norm_gain = params[0]
    normed_low, unit, scale, hidden, activated = saved
    grad_low = gradient.astype(bf16)
    out_bias_grad = jnp.sum(grad_low.astype(f32), axis=0)
    down_grad = jnp.einsum("rd,zrc->zdc", grad_low, activated, preferred_element_type=f32)
    act_grad = jnp.einsum("rd,zdc->zrc", grad_low, down, preferred_element_type=f32)
    _, gelu_back = jax.vjp(lambda values: jax.nn.gelu(values, approximate=True), hidden)
    hidden_low = gelu_back(act_grad)[0].astype(bf16)
    up_bias_grad = jnp.sum(hidden_low.astype(f32), axis=1).reshape(-1)
    up_grad = jnp.einsum("rd,zrc->zdc", normed_low, hidden_low, preferred_element_type=f32)
    normed_grad = jnp.einsum("zrc,zdc->rd", hidden_low, up, preferred_element_type=f32)
    from_norm, gain_grad, shift_grad = layer_norm_back(normed_grad, unit, scale, norm_gain[1])
    return gradient + from_norm, up_grad, down_grad, (gain_grad, shift_grad, out_bias_grad, up_bias_grad)


def attention_backward(grad_mid, proj, params, saved):
    norm_gain = params[0]
    normed_low, unit, scale, queries, key_rows, value_rows, attention, mixed_low = saved
    parts = proj.shape[0]
    cols = proj.shape[2] // 4
    score_scale = HEAD_DIM ** (-0.5)
    mid_low = grad_mid.astype(bf16)
    out_bias_grad = jnp.sum(mid_low.astype(f32), axis=0)
    out_grad = jnp.einsum("rd,zrc->zdc", mid_low, mixed_low, preferred_element_type=f32)
    mixed_grad = jnp.einsum("rd,zdc->zrc", mid_low, proj[:, :, 3 * cols :], preferred_element_type=f32)
    mixed_grad = to_heads(mixed_grad.astype(bf16))
    dot_back = jnp.einsum("hqd,hkd->hqk", mixed_grad, value_rows, preferred_element_type=f32)
    score_grad = attention * (dot_back - jnp.sum(attention * dot_back, axis=-1, keepdims=True))
    score_low = score_grad.astype(bf16)
    table_grad = fold_bias_grad(score_low.astype(f32))
    query_grad = jnp.einsum("hqk,hkd->hqd", score_low, key_rows, preferred_element_type=f32) * score_scale
    key_grad = jnp.einsum("hqk,hqd->hkd", score_low, queries, preferred_element_type=f32) * score_scale
    value_grad = jnp.einsum("hqk,hqd->hkd", attention.astype(bf16), mixed_grad, preferred_element_type=f32)
    qkv_low = jnp.concatenate(
        [from_heads(item.astype(bf16), parts) for item in (query_grad, key_grad, value_grad)], axis=-1
    )
    spatial_grad = jnp.einsum("rd,zrc->zdc", normed_low, qkv_low, preferred_element_type=f32)
    proj_grad = jnp.concatenate([spatial_grad, out_grad], axis=-1)
    sums = jnp.sum(qkv_low.astype(f32), axis=1).reshape(parts, 3, cols).transpose(1, 0, 2).reshape(3, -1)
    normed_grad = jnp.einsum("zrc,zdc->rd", qkv_low, proj[:, :, : 3 * cols], preferred_element_type=f32)
    from_norm, gain_grad, shift_grad = layer_norm_back(normed_grad, unit, scale, norm_gain[0])
    return grad_mid + from_norm, proj_grad, sums, table_grad, (gain_grad, shift_grad, out_bias_grad)


class Place:
    def __init__(self):
        wide = lax.axis_index("wide")
        self.z = lax.axis_index("narrow")
        self.y, self.x, self.c = wide // 4, (wide // 2) % 2, wide % 2

    def wide(self, flip_y=0, flip_x=0, flip_c=0):
        y = 1 - self.y if flip_y else self.y
        x = 1 - self.x if flip_x else self.x
        c = 1 - self.c if flip_c else self.c
        return y * 4 + x * 2 + c

    def along_z(self, steps):
        return lax.rem(self.z + steps, 4)

    def peers(self):
        across = [(self.wide(1, 0, 0), self.z), (self.wide(0, 1, 0), self.z), (self.wide(0, 0, 1), self.z)]
        return across + [(self.wide(), self.along_z(k)) for k in (1, 2, 3)]

    def greet(self):
        barrier = pltpu.get_barrier_semaphore()
        for peer in self.peers():
            pl.semaphore_signal(barrier, inc=1, device_id=peer, device_id_type=MESH)
        pl.semaphore_wait(barrier, 6)


def unit_cut(unit, rows):
    low = rows // 32 * 16
    return low if unit % 2 == 0 else rows - low


class Line:
    def __init__(self, place, block, send, recv):
        self.place, self.block, self.send, self.recv = place, block, send, recv

    def copy(self, src, origin, step, slot):
        place = self.place
        return pltpu.make_async_remote_copy(
            src_ref=src, dst_ref=self.block(origin), send_sem=self.send.at[slot], recv_sem=self.recv.at[origin],
            device_id=(place.wide(), place.z + step), device_id_type=MESH,
        )

    def begin(self, own):
        z = self.place.z

        @pl.when(z < 3)
        def _():
            self.copy(own, z, 1, z).start()

        @pl.when(z > 0)
        def _():
            self.copy(own, z, -1, 4).start()

    def arrive(self, far, then=lambda origin: None):
        z = self.place.z
        for side, valid, room in ((-1, z - far >= 0, z < 3), (1, z + far <= 3, z > 0)):

            @pl.when(valid)
            def _(side=side, room=room):
                origin = z + side * far
                here = self.block(origin)
                self.copy(here, origin, -side, origin).wait_recv()

                @pl.when(room)
                def _():
                    self.copy(here, origin, -side, origin).start()

                then(origin)

    def finish(self):
        z = self.place.z
        for origin in range(4):
            sent = jnp.where(origin <= z, z < 3, z > 0)

            @pl.when(sent)
            def _(origin=origin):
                self.copy(self.block(origin), origin, 0, origin).wait_send()

        @pl.when(z > 0)
        def _():
            self.copy(self.block(0), 0, 0, 4).wait_send()


LINE_SEMS = 5
GATHER_SEMS = 58
Y_FIRST, X_LAST, X_NEAR, X_FAR, Y_NEAR, Y_FAR = 5, 9, 13, 17, 21, 25
C_OWN, C_Y, C_X, C_X_NEAR, C_Y_NEAR, C_X_FAR, C_Y_FAR = 29, 33, 37, 41, 45, 49, 53


class GatherUnit:
    def __init__(self, place, piece, whole, send, recv, cut):
        self.place, self.piece, self.whole = place, piece, whole
        self.send, self.recv = send, recv
        self.rows = piece.shape[0]
        self.first, self.last, self.every = pl.ds(0, cut), pl.ds(cut, self.rows - cut), pl.ds(0, self.rows)
        self.line = Line(place, lambda origin: self.block(origin, 0, 0, self.every), send, recv)
        self.peer = {
            "y": (place.wide(1, 0, 0), place.z), "x": (place.wide(0, 1, 0), place.z), "c": (place.wide(0, 0, 1), place.z)
        }
        self.order = [place.along_z(k) for k in (0, 1, 3, 2)]
        self.sent = []

    def block(self, origin, flip_y, flip_x, rows):
        first = pl.multiple_of(self.place.wide(flip_y, flip_x) * self.rows + rows.start, 16)
        return self.whole.at[origin, pl.ds(first, rows.size)]

    def copy(self, base, axis, origin, flip_y, flip_x, rows, own=None):
        block = self.block(origin, flip_y, flip_x, rows)
        return pltpu.make_async_remote_copy(
            src_ref=block if own is None else own, dst_ref=block, send_sem=self.send.at[base + origin],
            recv_sem=self.recv.at[base + origin], device_id=self.peer[axis], device_id_type=MESH,
        )

    def put(self, *where):
        self.copy(*where).start()

    def wait(self, *where):
        self.copy(*where).wait_recv()

    def begin(self):
        z = self.place.z
        self.line.begin(self.piece)
        self.put(Y_FIRST, "y", z, 0, 0, self.first, self.piece.at[self.first])
        self.put(X_LAST, "x", z, 0, 0, self.last, self.piece.at[self.last])
        self.put(C_OWN, "c", z, 0, 0, self.every, self.piece)
        self.local = pltpu.make_async_copy(self.piece, self.block(z, 0, 0, self.every), self.send.at[GATHER_SEMS - 1])
        self.local.start()

    def second(self):
        def then(origin):
            self.put(Y_FIRST, "y", origin, 0, 0, self.first)
            self.put(X_LAST, "x", origin, 0, 0, self.last)
            self.put(C_OWN, "c", origin, 0, 0, self.every)

        for far in (1, 2, 3):
            self.line.arrive(far, then)
            yield

    def third(self):
        self.local.wait()
        for origin in self.order:
            self.put(X_NEAR, "x", origin, 0, 0, self.first)
            self.put(Y_NEAR, "y", origin, 0, 0, self.last)
        for at, origin in enumerate(self.order):
            self.wait(Y_FIRST, "y", origin, 1, 0, self.first)
            self.put(X_FAR, "x", origin, 1, 0, self.first)
            self.put(C_Y, "c", origin, 1, 0, self.first)
            self.wait(X_LAST, "x", origin, 0, 1, self.last)
            self.put(Y_FAR, "y", origin, 0, 1, self.last)
            self.put(C_X, "c", origin, 0, 1, self.last)
            if at % 2:
                yield

    def fourth(self):
        for at, origin in enumerate(self.order):
            self.wait(X_NEAR, "x", origin, 0, 1, self.first)
            self.put(C_X_NEAR, "c", origin, 0, 1, self.first)
            self.wait(Y_NEAR, "y", origin, 1, 0, self.last)
            self.put(C_Y_NEAR, "c", origin, 1, 0, self.last)
            if at % 2:
                yield
        for at, origin in enumerate(self.order):
            self.wait(X_FAR, "x", origin, 1, 1, self.first)
            self.put(C_X_FAR, "c", origin, 1, 1, self.first)
            self.wait(Y_FAR, "y", origin, 1, 1, self.last)
            self.put(C_Y_FAR, "c", origin, 1, 1, self.last)
            if at % 2:
                yield

    def finish(self):
        firsts = (Y_FIRST, X_NEAR, X_FAR, C_Y, C_X_NEAR, C_X_FAR)
        lasts = (X_LAST, Y_NEAR, Y_FAR, C_X, C_Y_NEAR, C_Y_FAR)
        for origin in range(4):
            for base in (C_Y, C_X_NEAR, C_X_FAR):
                self.wait(base, "c", origin, 0, 0, self.first)
            for base in (C_X, C_Y_NEAR, C_Y_FAR):
                self.wait(base, "c", origin, 0, 0, self.last)
            self.wait(C_OWN, "c", origin, 0, 0, self.every)
        for origin in range(4):
            for base in firsts:
                self.copy(base, "c", origin, 0, 0, self.first).wait_send()
            for base in lasts:
                self.copy(base, "c", origin, 0, 0, self.last).wait_send()
            self.copy(C_OWN, "c", origin, 0, 0, self.every).wait_send()
        self.line.finish()


def column_ids(width):
    return lax.broadcasted_iota(jnp.int32, (1, width), 1)


def unit_rows(values):
    average = jnp.mean(values, axis=-1, keepdims=True)
    centred = values - average
    variance = jnp.mean(centred * centred, axis=-1, keepdims=True)
    scale = lax.rsqrt(variance + eps_norm)
    return centred * scale, scale


def dot_plain(left, right):
    return lax.dot_general(left, right, (((1,), (0,)), ((), ())), preferred_element_type=f32)


def dot_turned(left, right):
    return lax.dot_general(left, right, (((1,), (1,)), ((), ())), preferred_element_type=f32)


def remote(src, dst, send, recv, peer):
    copy = pltpu.make_async_remote_copy(
        src_ref=src, dst_ref=dst, send_sem=send, recv_sem=recv, device_id=peer, device_id_type=MESH
    )
    copy.start()
    return copy


def z_line(place, every, send, recv):
    return Line(place, lambda origin: every.at[origin], send, recv)


class Stream:
    def __init__(self, slots, sems, sources):
        self.slots, self.sems, self.sources = slots, sems, sources
        self.started = 0

    def ensure(self, upto):
        while self.started <= upto and self.started < len(self.sources):
            at = self.started
            pltpu.make_async_copy(self.sources[at], self.slots.at[at % 2], self.sems.at[at % 2]).start()
            self.started += 1

    def take(self, at):
        self.ensure(at)
        pltpu.make_async_copy(self.sources[at], self.slots.at[at % 2], self.sems.at[at % 2]).wait()
        return self.slots.at[at % 2]


FORWARD_IN = 17
LAYER_SAVED = 6


def gelu(values):
    inner = math.sqrt(2.0 / math.pi) * (values + 0.044715 * values * values * values)
    return 0.5 * values * (1.0 + jnp.tanh(inner))


def window_bias(windows, put):
    for grid_row in range(GRID):
        shift = (GRID - 1 - grid_row) * GRID
        moved = windows if shift == 0 else pltpu.roll(windows, 512 - shift, 1)
        put(grid_row, moved[:, :PATCHES])


def forward_kernel(layers, *refs):
    units = 3 * layers
    refs = list(refs)

    def take(count):
        out = refs[:count]
        del refs[:count]
        return out

    (tokens, cot, pick, time_own, time_weight, windows_own, small_own, gains, shifts, out_bias) = take(10)
    pieces = take(units)
    wholes = take(units)
    saved = [take(LAYER_SAVED) for _ in range(layers)]
    block_out, grad_out, time_out, time_sel_out = take(4)
    (
        send, recv, z_send, z_recv, t_send, t_recv, save_sem, w_sem,
        w_slots, tok_all, cot_all, windows_all, small_all, time_all, share, share_y, share_x, share_c, share_z,
        x_buf, mid_buf, low_buf, acc_buf, s_buf, att_buf, act_buf, hid_buf, bias_buf,
    ) = refs
    place = Place()
    place.greet()
    gather = [
        GatherUnit(place, pieces[u], wholes[u], send.at[u], recv.at[u], unit_cut(u, pieces[u].shape[0]))
        for u in range(units)
    ]
    state = {"done": 0}
    tokens_n, d_model = tokens.shape
    head_cols = d_model // 4
    yp, xp, cp = ((place.wide(1, 0, 0), place.z), (place.wide(0, 1, 0), place.z), (place.wide(0, 0, 1), place.z))
    py, px, pc = place.y, place.x, place.c

    def comm_steps():
        gather[0].begin()
        time_all[py, px, pc] = time_own[...]
        first = remote(time_all.at[py, px, pc], time_all.at[py, px, pc], t_send.at[0], t_recv.at[0], cp)
        tok, win, small, cots, rz = (
            z_line(place, every, z_send.at[at], z_recv.at[at])
            for at, every in enumerate((tok_all, windows_all, small_all, cot_all, share_z))
        )
        small.begin(small_own)
        tok.begin(tokens)
        win.begin(windows_own)
        own = [
            pltpu.make_async_copy(tokens, tok_all.at[place.z], save_sem.at[0]),
            pltpu.make_async_copy(windows_own, windows_all.at[place.z], save_sem.at[1]),
            pltpu.make_async_copy(small_own, small_all.at[place.z], save_sem.at[2]),
            pltpu.make_async_copy(cot, cot_all.at[place.z], save_sem.at[3]),
        ]
        for copy in own:
            copy.start()
        gather[1].begin()
        first.wait_recv()
        second = remote(time_all.at[py, px], time_all.at[py, px], t_send.at[1], t_recv.at[1], xp)
        yield from gather[0].second()
        small.arrive(1)
        tok.arrive(1)
        win.arrive(1)
        second.wait_recv()
        third = remote(time_all.at[py], time_all.at[py], t_send.at[2], t_recv.at[2], yp)
        yield from gather[0].third()
        third.wait_recv()
        rows = time_all[...].reshape(128, d_model)
        cut = time_weight.shape[1]
        at_row = lax.broadcasted_iota(jnp.int32, (d_model, cut), 0)
        at_col = lax.broadcasted_iota(jnp.int32, (d_model, cut), 1)
        select = (at_row == at_col + place.wide() * cut).astype(bf16)
        picked = dot_plain(rows, select).astype(bf16)
        time_sel_out[...] = picked
        time_out[...] = rows
        for layer in range(layers):
            part = dot_plain(picked, time_weight[layer]).reshape(2, 2, 2, 16, d_model)
            share[:, :, :, layer] = part[:, :, :, :8]
        ry = remote(share.at[1 - py], share_y, t_send.at[3], t_recv.at[3], yp)
        gather[2].begin()
        small.arrive(2)
        tok.arrive(2)
        win.arrive(2)
        ry.wait_recv()
        share[py] = share[py] + share_y[...]
        rx = remote(share.at[py, 1 - px], share_x, t_send.at[4], t_recv.at[4], xp)
        yield from gather[1].second()
        rx.wait_recv()
        share[py, px] = share[py, px] + share_x[...]
        rc = remote(share.at[py, px, 1 - pc], share_c, t_send.at[5], t_recv.at[5], cp)
        rc.wait_recv()
        share[py, px, pc] = share[py, px, pc] + share_c[...]
        share_z[place.z] = share[py, px, pc]
        rz.begin(share_z.at[place.z])
        yield from gather[0].fourth()
        rz.arrive(1)
        yield from gather[1].third()
        rz.arrive(2)
        gather[0].finish()
        for line in (small, tok, win, rz):
            line.arrive(3)
            line.finish()
        for copy in own:
            copy.wait()
        state["done"] = 1
        for copy in (first, second, third, ry, rx, rc):
            copy.wait_send()
        yield
        for unit in range(3, units + 3):
            if unit < units:
                gather[unit].begin()
                yield
            if unit - 1 < units:
                yield from gather[unit - 1].second()
                yield from gather[unit - 1].third()
            if unit - 2 < units:
                yield from gather[unit - 2].fourth()
                gather[unit - 2].finish()
                state["done"] = unit - 1
                yield
            if unit == 3:
                cots.begin(cot)
            elif unit <= 6:
                cots.arrive(unit - 3)
            if unit == 6:
                cots.finish()

    stream = Stream(w_slots, w_sem, [wholes[u].at[z] for u in range(units) for z in range(4)])
    pending = {}

    def save(slot, src, dst):
        copy = pltpu.make_async_copy(src, dst, save_sem.at[slot])
        copy.start()
        pending[slot] = copy

    def settle(slot):
        if slot in pending:
            pending.pop(slot).wait()

    def weights(unit, z):
        at = unit * 4 + z
        stream.ensure(at)
        ready = state["done"] * 4
        stream.ensure(min(at + 1, ready - 1))
        return stream.take(at)

    def compute_steps():
        columns = column_ids(d_model)
        for layer in range(layers):
            x_save, mid_save, s_save, att_save, hid_save, act_save = saved[layer]
            row = 2 * layer
            yield 3 * layer + 1
            if layer == 0:
                total = dot_plain(pick[:, 0:tokens_n], tok_all[0])
                for z in range(1, 4):
                    total = total + dot_plain(pick[:, z * tokens_n : (z + 1) * tokens_n], tok_all[z])
                x_buf[...] = total
            settle(4)
            settle(5)
            save(4, x_buf, x_save)
            unit, _ = unit_rows(x_buf[...])
            low_buf[...] = (unit * gains[row : row + 1, :] + shifts[row : row + 1, :]).astype(bf16)
            settle(6)
            for z in range(4):
                yield 3 * layer + 1
                w = weights(3 * layer, z)
                share_rows = share_z[z, layer]
                at_image = lax.broadcasted_iota(jnp.int32, share_rows.shape, 0) == place.z
                offset = jnp.sum(jnp.where(at_image, share_rows, 0.0), axis=0, keepdims=True)
                offset = offset + small_all[z, 2 + layer : 3 + layer, :]
                s_buf[z] = (dot_plain(low_buf[...], w[...]) + offset).astype(bf16)
                q = s_buf[z, :, 0:head_cols]
                k = s_buf[z, :, head_cols : 2 * head_cols]
                v = s_buf[z, :, 2 * head_cols : 3 * head_cols]
                head_of = column_ids(head_cols) // HEAD_DIM
                slot = z % 2
                settle(8 + slot)

                def one_head(head, mixed):
                    here = head_of == head

                    def put(grid_row, block):
                        bias_buf[grid_row * GRID : (grid_row + 1) * GRID, :] = block

                    first_row = pl.multiple_of(head * GRID, GRID)
                    window_bias(windows_all[z, layer, pl.ds(first_row, GRID), :], put)
                    scores = dot_turned(jnp.where(here, q, 0), k)
                    scores = scores * HEAD_DIM ** (-0.5) + bias_buf[...]
                    top = jnp.max(scores, axis=-1, keepdims=True)
                    exponent = jnp.exp(scores - top)
                    attention = exponent / jnp.sum(exponent, axis=-1, keepdims=True)
                    att_buf[slot, head] = attention
                    return mixed + dot_plain(attention.astype(bf16), jnp.where(here, v, 0))

                mixed = lax.fori_loop(0, 4, one_head, jnp.zeros((tokens_n, head_cols), f32))
                save(8 + slot, att_buf.at[slot], att_save.at[z])
                s_buf[z, :, 3 * head_cols :] = mixed.astype(bf16)
                branch = dot_turned(jnp.where(columns >= 3 * head_cols, s_buf[z], 0), w[...])
                acc_buf[...] = branch if z == 0 else acc_buf[...] + branch
            save(6, s_buf, s_save)
            settle(4)
            mid_buf[...] = x_buf[...] + (acc_buf[...] + out_bias[row : row + 1, :])
            save(5, mid_buf, mid_save)
            unit, _ = unit_rows(mid_buf[...])
            low_buf[...] = (unit * gains[row + 1 : row + 2, :] + shifts[row + 1 : row + 2, :]).astype(bf16)
            settle(7)
            for z in range(4):
                yield 3 * layer + 2
                w = weights(3 * layer + 1, z)
                slot = z % 2
                settle(10 + slot)
                hid_buf[slot] = dot_plain(low_buf[...], w[...]) + small_all[z, layer : layer + 1, :]
                save(10 + slot, hid_buf.at[slot], hid_save.at[z])
                act_buf[z] = gelu(hid_buf[slot]).astype(bf16)
            save(7, act_buf, act_save)
            for z in range(4):
                yield 3 * layer + 3
                w = weights(3 * layer + 2, z)
                branch = dot_turned(act_buf[z], w[...])
                acc_buf[...] = branch if z == 0 else acc_buf[...] + branch
            x_buf[...] = mid_buf[...] + (acc_buf[...] + out_bias[row + 1 : row + 2, :])
        block_out[...] = x_buf[...].astype(bf16)
        total = dot_plain(pick[:, 0:tokens_n], cot_all[0])
        for z in range(1, 4):
            total = total + dot_plain(pick[:, z * tokens_n : (z + 1) * tokens_n], cot_all[z])
        grad_out[...] = total
        for slot in list(pending):
            settle(slot)

    interleave(comm_steps(), compute_steps(), state)


def interleave(comm, compute, state, pace=1):
    need = next(compute)
    count = 0
    for _ in comm:
        count += 1
        if count % pace == 0 and need is not None and state["done"] >= need:
            need = next(compute, None)
    while need is not None:
        need = next(compute, None)


def forward_all(tokens, cot, pick, time_own, time_weight, windows_own, small_own, gains, shifts, out_bias, pieces):
    layers = len(pieces) // 3
    units = len(pieces)
    rows, d_model = tokens.shape
    piece_rows = pieces[0].shape[0]
    any_space = pl.BlockSpec(memory_space=pl.ANY)
    vmem = pl.BlockSpec(memory_space=pltpu.VMEM)
    layer_shapes = [
        ((rows, d_model), f32),
        ((rows, d_model), f32),
        ((4, rows, d_model), bf16),
        ((4, 4, rows, rows), f32),
        ((4, rows, d_model), f32),
        ((4, rows, d_model), bf16),
    ]
    out_shape = (
        [jax.ShapeDtypeStruct((4, 8 * piece_rows, d_model), bf16)] * units
        + [jax.ShapeDtypeStruct(*item) for item in layer_shapes] * layers
        + [
            jax.ShapeDtypeStruct((rows, d_model), bf16),
            jax.ShapeDtypeStruct((rows, d_model), f32),
            jax.ShapeDtypeStruct((128, d_model), bf16),
            jax.ShapeDtypeStruct((128, piece_rows), bf16),
        ]
    )
    share_tail = (layers, 8, d_model)
    scratch = [
        pltpu.SemaphoreType.DMA((units, GATHER_SEMS)),
        pltpu.SemaphoreType.DMA((units, GATHER_SEMS)),
        pltpu.SemaphoreType.DMA((5, LINE_SEMS)),
        pltpu.SemaphoreType.DMA((5, LINE_SEMS)),
        pltpu.SemaphoreType.DMA((6,)),
        pltpu.SemaphoreType.DMA((6,)),
        pltpu.SemaphoreType.DMA((12,)),
        pltpu.SemaphoreType.DMA((2,)),
        pltpu.VMEM((2, d_model, d_model), bf16),
        pltpu.VMEM((4, rows, d_model), bf16),
        pltpu.VMEM((4, rows, d_model), bf16),
        pltpu.VMEM((4,) + windows_own.shape, f32),
        pltpu.VMEM((4,) + small_own.shape, f32),
        pltpu.VMEM((2, 2, 2, 16, d_model), bf16),
        pltpu.VMEM((2, 2, 2) + share_tail, f32),
        pltpu.VMEM((2, 2) + share_tail, f32),
        pltpu.VMEM((2,) + share_tail, f32),
        pltpu.VMEM(share_tail, f32),
        pltpu.VMEM((4,) + share_tail, f32),
        pltpu.VMEM((rows, d_model), f32),
        pltpu.VMEM((rows, d_model), f32),
        pltpu.VMEM((rows, d_model), bf16),
        pltpu.VMEM((rows, d_model), f32),
        pltpu.VMEM((4, rows, d_model), bf16),
        pltpu.VMEM((2, 4, rows, rows), f32),
        pltpu.VMEM((4, rows, d_model), bf16),
        pltpu.VMEM((2, rows, d_model), f32),
        pltpu.VMEM((rows, rows), f32),
    ]
    out = pl.pallas_call(
        functools.partial(forward_kernel, layers),
        out_shape=out_shape,
        in_specs=[any_space] * 2 + [vmem] * 8 + [any_space] * units,
        out_specs=[any_space] * (units + LAYER_SAVED * layers) + [vmem] * 4,
        scratch_shapes=scratch,
        compiler_params=pltpu.CompilerParams(
            collective_id=0, has_side_effects=True, vmem_limit_bytes=60 * 2**20
        ),
        name="forward_all",
    )(tokens, cot, pick, time_own, time_weight, windows_own, small_own, gains, shifts, out_bias, *pieces)
    wholes = out[:units]
    saved = [out[units + LAYER_SAVED * at : units + LAYER_SAVED * (at + 1)] for at in range(layers)]
    return wholes, saved, out[units + LAYER_SAVED * layers :]


def gelu_slope(values):
    factor = math.sqrt(2.0 / math.pi)
    square = values * values
    bend = jnp.tanh(factor * (values + 0.044715 * square * values))
    return 0.5 * (1.0 + bend) + 0.5 * values * (1.0 - bend * bend) * factor * (1.0 + 3 * 0.044715 * square)


def dot_rows(left, right):
    return lax.dot_general(left, right, (((0,), (0,)), ((), ())), preferred_element_type=f32)


def norm_back(grad, unit, scale, norm_gain):
    weighted = grad * norm_gain
    first = jnp.mean(weighted, axis=-1, keepdims=True)
    second = jnp.mean(weighted * unit, axis=-1, keepdims=True)
    return scale * (weighted - first - unit * second)


def column_sums(values):
    return jnp.sum(values, axis=0, keepdims=True)


def fold_window(grads):
    total = None
    empty = jnp.zeros((GRID, 512 - PATCHES), f32)
    for grid_row in range(GRID):
        wide = jnp.concatenate([grads[grid_row * GRID : (grid_row + 1) * GRID, :], empty], axis=1)
        shift = (GRID - 1 - grid_row) * GRID
        moved = wide if shift == 0 else pltpu.roll(wide, shift, 1)
        total = moved if total is None else total + moved
    return total


SCATTER_SEMS = 23


def add_rows(total, part, rows):
    step = 16

    def one(at, carry):
        here = pl.ds(pl.multiple_of(at * step, step), step)
        both = total[here, :].astype(f32) + part[here, :].astype(f32)
        total[here, :] = both.astype(total.dtype)
        return carry

    lax.fori_loop(0, rows // step, one, 0)


class ScatterUnit:
    def __init__(self, place, out, total, far, near, from_z, send, recv, cut):
        self.place, self.out = place, out
        self.total, self.far, self.near, self.from_z = total, far, near, from_z
        self.send, self.recv = send, recv
        self.rows, self.cut = total.shape[3], cut
        self.first, self.last = pl.ds(0, cut), pl.ds(cut, self.rows - cut)
        self.copies, self.unsent, self.closed = {}, set(), set()

    def put(self, slot, peer, src, dst):
        self.copies[slot] = remote(src, dst, self.send.at[slot], self.recv.at[slot], peer)
        self.unsent.add(slot)

    def settle(self, slots):
        for slot in sorted(self.unsent.intersection(slots)):
            self.copies[slot].wait_send()
            self.unsent.remove(slot)

    def first_stage(self, k):
        p = self.place
        self.put(4 + k, (p.wide(0, 1), p.z), self.total.at[k, :, 1 - p.x, self.first], self.far.at[k, :, self.first])
        self.put(8 + k, (p.wide(1, 0), p.z), self.total.at[k, 1 - p.y, :, self.last], self.far.at[k, :, self.last])

    def second_stage(self, k):
        p = self.place
        self.copies[4 + k].wait_recv()
        for block in range(2):
            add_rows(self.total.at[k, block, p.x, self.first], self.far.at[k, block, self.first], self.cut)
        self.put(12 + k, (p.wide(1, 0), p.z), self.total.at[k, 1 - p.y, p.x, self.first], self.near.at[k, self.first])
        self.copies[8 + k].wait_recv()
        for block in range(2):
            add_rows(self.total.at[k, p.y, block, self.last], self.far.at[k, block, self.last], self.rows - self.cut)
        self.put(16 + k, (p.wide(0, 1), p.z), self.total.at[k, p.y, 1 - p.x, self.last], self.near.at[k, self.last])

    def third_stage(self, k):
        p = self.place
        self.copies[12 + k].wait_recv()
        self.copies[16 + k].wait_recv()
        add_rows(self.total.at[k, p.y, p.x], self.near.at[k], self.rows)
        if k:
            self.put(19 + k, (p.wide(), p.along_z(k)), self.total.at[k, p.y, p.x], self.from_z.at[k - 1])
            self.closed.add(k)

    def finish(self):
        p = self.place
        for k in (1, 2, 3):
            self.copies[19 + k].wait_recv()
        own = self.total.at[0, p.y, p.x]
        step = 16

        def one(at, carry):
            here = pl.ds(pl.multiple_of(at * step, step), step)
            both = own[here, :].astype(f32)
            for k in range(3):
                both = both + self.from_z[k, here, :].astype(f32)
            self.out[here, :] = both
            return carry

        lax.fori_loop(0, self.rows // step, one, 0)
        self.settle(list(self.copies))
        self.closed.add(0)


FAR_FIRST = (2, 1, 3, 0)


def scatter_step(unit, k, late):
    unit.second_stage(k)

    def third():
        unit.third_stage(k)
        if k == 0:
            return ((late, unit.finish),)

    return ((late, third),)


def backward_kernel(last_layer, *refs):
    refs = list(refs)

    def take(count):
        out = refs[:count]
        del refs[:count]
        return out

    (
        grad, x_in, mid_in, gains, shifts, pick, rows_in, s_all, att_all, hid_all, act_all, proj, up, down,
    ) = take(14)
    proj_out, up_out, down_out, grad_out, rows_out, small_out, table_out, rows_all = take(8)
    (
        total_a, total_b, far, near, from_z, right_a, right_b, left, turned,
        w_slots, s_slots, att_slots, hid_slots, acc_buf, mid_grad, low_buf, head_grads,
        send, recv, left_send, left_recv, line_send, line_recv, w_sem, s_sem, att_sem, hid_sem, load_sem, credit,
    ) = refs
    place = Place()
    place.greet()
    rows, d_model = grad.shape
    cut = down_out.shape[0]
    head_cols = d_model // 4
    core = (place.wide(0, 0, 1), place.z)
    zs = {k: place.along_z(k) for k in range(4)}
    columns = column_ids(d_model)
    units = {
        name: ScatterUnit(
            place, out, total, far.at[at], near.at[at], from_z.at[at], send.at[at], recv.at[at], unit_cut(at, cut)
        )
        for at, (name, out, total) in enumerate(
            (("down", down_out, total_a), ("up", up_out, total_b), ("proj", proj_out, total_a))
        )
    }
    line = z_line(place, rows_all, line_send, line_recv)

    right_copies = {}

    def give_right(name, at, k, src, buffer):
        right_copies[name, k] = remote(
            src, buffer.at[zs[k], pl.ds(rows, rows)], send.at[at, k], recv.at[at, k], core
        )

    left_copies = {}

    def make_left(at, values):
        if at > 1:
            for copy in left_copies[at - 2]:
                copy.wait_send()
        flipped = turned.at[at % 2]
        flipped[...] = values.astype(f32).T.astype(bf16)
        copies = []
        for block in range(4):
            mine = pl.multiple_of((2 * block + place.c) * cut, 16)
            other = pl.multiple_of((2 * block + 1 - place.c) * cut, 16)
            here = pl.ds(block * cut, cut)
            copies.append(
                remote(
                    flipped.at[pl.ds(other, cut)], left.at[at, here, pl.ds(rows, rows)],
                    left_send.at[at, block], left_recv.at[at, block], core,
                )
            )
            left[at, here, 0:rows] = flipped[pl.ds(mine, cut), :]
        left_copies[at] = copies

    def left_ready(at):
        for copy in left_copies[at]:
            copy.wait_recv()

    loads, keep = [], []
    if last_layer:
        line.begin(rows_in)
        keep.append(pltpu.make_async_copy(rows_in, rows_all.at[place.z], load_sem.at[4]))
        keep[0].start()
    for k in FAR_FIRST:
        give_right("down", 0, k, act_all.at[zs[k]], right_a)
        load = pltpu.make_async_copy(act_all.at[zs[k]], right_a.at[zs[k], pl.ds(0, rows)], load_sem.at[k])
        load.start()
        loads.append((k, load))
    w_sources = []
    for k in FAR_FIRST:
        w_sources += [down.at[zs[k]], up.at[zs[k]]]
    w_sources += [proj.at[zs[k]] for k in FAR_FIRST]
    weights = Stream(w_slots, w_sem, w_sources)
    hidden = Stream(hid_slots, hid_sem, [hid_all.at[zs[k]] for k in FAR_FIRST])
    saved = Stream(s_slots, s_sem, [s_all.at[zs[k]] for k in FAR_FIRST])
    attentions = Stream(att_slots, att_sem, [att_all.at[zs[k]] for k in FAR_FIRST])
    for stream in (weights, hidden, saved, attentions):
        stream.ensure(1)

    def weight_grad(name, k, buffer, *lefts):
        unit = units[name]
        part = dot_plain(left[lefts[0]], buffer[zs[k]])
        if len(lefts) > 1:
            part = jnp.where(columns < 3 * head_cols, part, dot_plain(left[lefts[1]], buffer[zs[k]]))
        low = part.astype(bf16)
        for block in range(4):
            unit.total[k, block // 2, block % 2] = low[block * cut : (block + 1) * cut]

    def compute():
        low_buf[0] = grad[...].astype(bf16)
        small_out[...] = jnp.zeros_like(small_out)
        small_out[5:6, :] = column_sums(low_buf[0].astype(f32))
        make_left(0, low_buf[0])
        left_ready(0)
        for k, load in loads:
            load.wait()
            right_copies["down", k].wait_recv()
            weight_grad("down", k, right_a, 0)
            yield 2.0, [(units["down"], k)]
        for k, load in loads:
            right_copies["down", k].wait_send()
        pl.semaphore_signal(credit, inc=1, device_id=core, device_id_type=MESH)
        unit, scale = unit_rows(mid_in[...])
        make_left(1, (unit * gains[1:2, :] + shifts[1:2, :]).astype(bf16))
        left_ready(1)
        yield 3.0, []
        for at, k in enumerate(FAR_FIRST):
            w = weights.take(2 * at)
            hid = hidden.take(at)
            act_grad = dot_plain(low_buf[0], w[...])
            hid_grad = (act_grad * gelu_slope(hid[...])).astype(bf16)
            right_b[zs[k], 0:rows] = hid_grad
            weights.ensure(2 * at + 2)
            hidden.ensure(at + 2)
            give_right("up", 1, k, right_b.at[zs[k], pl.ds(0, rows)], right_b)
            small_out[pl.ds(6 + zs[k], 1), :] = column_sums(hid_grad.astype(f32))
            yield 2.5, []
            w = weights.take(2 * at + 1)
            part = dot_turned(right_b[zs[k], 0:rows], w[...])
            acc_buf[...] = part if at == 0 else acc_buf[...] + part
            weights.ensure(2 * at + 3)
            yield 1.5, []
            right_copies["up", k].wait_recv()
            weight_grad("up", k, right_b, 1)
            yield 1.5, [(units["up"], k)]
        unit, scale = unit_rows(mid_in[...])
        from_norm = norm_back(acc_buf[...], unit, scale, gains[1:2, :])
        small_out[1:2, :] = column_sums(acc_buf[...] * unit)
        small_out[3:4, :] = column_sums(acc_buf[...])
        mid_grad[...] = grad[...] + from_norm
        low_buf[0] = mid_grad[...].astype(bf16)
        small_out[4:5, :] = column_sums(low_buf[0].astype(f32))
        yield 3.0, []
        make_left(2, low_buf[0])
        unit, scale = unit_rows(x_in[...])
        make_left(3, (unit * gains[0:1, :] + shifts[0:1, :]).astype(bf16))
        left_ready(2)
        left_ready(3)
        pl.semaphore_wait(credit, 1)
        yield 4.0, []
        head_of = column_ids(head_cols) // HEAD_DIM
        score_scale = HEAD_DIM ** (-0.5)
        for at, k in enumerate(FAR_FIRST):
            w = weights.take(8 + at)
            s = saved.take(at)
            attention_slot = attentions.take(at)
            low_buf[1] = dot_plain(low_buf[0], w[...]).astype(bf16)
            mixed_grad = low_buf[1, :, 3 * head_cols :]
            q = s[:, 0:head_cols]
            key = s[:, head_cols : 2 * head_cols]
            v = s[:, 2 * head_cols : 3 * head_cols]
            head_grads[...] = jnp.zeros_like(head_grads)

            def one_head(head, carry):
                here = head_of == head
                attention = attention_slot[head]
                own_grad = jnp.where(here, mixed_grad, 0)
                dot_back = dot_turned(own_grad, v)
                both = attention * dot_back
                score_low = (both - attention * jnp.sum(both, axis=-1, keepdims=True)).astype(bf16)
                first_row = pl.multiple_of(head * GRID, GRID)
                table_out[zs[k], pl.ds(first_row, GRID), :] = fold_window(score_low.astype(f32))
                head_grads[0] += dot_plain(score_low, jnp.where(here, key, 0))
                head_grads[1] += dot_rows(score_low, jnp.where(here, q, 0))
                head_grads[2] += dot_rows(attention.astype(bf16), own_grad)
                return carry

            lax.fori_loop(0, 4, one_head, 0)
            here = right_a.at[zs[k]]
            here[0:rows, 0:head_cols] = (head_grads[0] * score_scale).astype(bf16)
            here[0:rows, head_cols : 2 * head_cols] = (head_grads[1] * score_scale).astype(bf16)
            here[0:rows, 2 * head_cols : 3 * head_cols] = head_grads[2].astype(bf16)
            here[0:rows, 3 * head_cols :] = s[:, 3 * head_cols :]
            give_right("proj", 2, k, right_a.at[zs[k], pl.ds(0, rows)], right_a)
            saved.ensure(at + 2)
            attentions.ensure(at + 2)
            yield 6.0, []
            own = right_a[zs[k], 0:rows]
            small_out[pl.ds(10 + zs[k], 1), :] = column_sums(own.astype(f32))
            part = dot_turned(jnp.where(columns < 3 * head_cols, own, 0), w[...])
            acc_buf[...] = part if at == 0 else acc_buf[...] + part
            weights.ensure(8 + at + 2)
            right_copies["proj", k].wait_recv()
            yield 2.0, [], (units["down"], k)
            units["down"].settle((4 + k, 8 + k, 12 + k, 16 + k, 19 + k))
            weight_grad("proj", k, right_a, 3, 2)
            yield 2.0, [(units["proj"], k)]
        unit, scale = unit_rows(x_in[...])
        from_norm = norm_back(acc_buf[...], unit, scale, gains[0:1, :])
        small_out[0:1, :] = column_sums(acc_buf[...] * unit)
        small_out[2:3, :] = column_sums(acc_buf[...])
        grad_out[...] = mid_grad[...] + from_norm
        if not last_layer:
            low_buf[0] = grad_out[...].astype(bf16)
            line.begin(low_buf.at[0])
            keep.append(pltpu.make_async_copy(low_buf.at[0], rows_all.at[place.z], load_sem.at[4]))
            keep[0].start()
        yield 2.0, []

    def more_events():
        if last_layer:
            return [(20.0 * far_off, functools.partial(line.arrive, far_off)) for far_off in (1, 2, 3)]
        return []

    merge_steps(compute(), more_events(), 10.7, 9.0)
    for (name, k), copy in right_copies.items():
        if name != "down":
            copy.wait_send()
    for at in (2, 3):
        for copy in left_copies[at]:
            copy.wait_send()
    if not last_layer:
        for far_off in (1, 2, 3):
            line.arrive(far_off)
    line.finish()
    keep[0].wait()
    gathered = pltpu.make_async_copy(rows_all, right_b.at[:, pl.ds(0, rows)], load_sem.at[4])
    gathered.start()
    gathered.wait()
    total = dot_plain(pick[:, 0:rows], right_b[0, 0:rows])
    for z in range(1, 4):
        total = total + dot_plain(pick[:, z * rows : (z + 1) * rows], right_b[z, 0:rows])
    rows_out[...] = total.astype(bf16)


def merge_steps(compute, events, links, late):
    clock, link_free = 0.0, 0.0
    events = list(events)

    def run_first():
        events.sort(key=lambda item: item[0])
        at, step = events.pop(0)
        for delay, following in step() or ():
            events.append((max(clock, at) + delay, following))
        return max(clock, at)

    while True:
        while events and min(item[0] for item in events) <= clock:
            clock = run_first()
        made = next(compute, None)
        if made is None:
            break
        clock += made[0]
        for unit, k in made[1]:
            unit.first_stage(k)
            start = max(clock, link_free)
            link_free = start + links
            events.append((start + late, functools.partial(scatter_step, unit, k, late)))
        if len(made) > 2:
            unit, k = made[2]
            while k not in unit.closed:
                clock = run_first()
    while events:
        clock = run_first()


def backward_layer(last_layer, grad, saved, gains, shifts, pick, rows_in, weights):
    x_in, mid_in, s_all, att_all, hid_all, act_all = saved
    proj, up, down = weights
    rows, d_model = grad.shape
    cut = d_model // 8
    any_space = pl.BlockSpec(memory_space=pl.ANY)
    vmem = pl.BlockSpec(memory_space=pltpu.VMEM)
    block = jax.ShapeDtypeStruct((cut, d_model), f32)
    out_shape = [
        block,
        block,
        block,
        jax.ShapeDtypeStruct((rows, d_model), f32),
        jax.ShapeDtypeStruct((rows, d_model), bf16),
        jax.ShapeDtypeStruct((16, d_model), f32),
        jax.ShapeDtypeStruct((4, 4 * GRID, 512), f32),
        jax.ShapeDtypeStruct((4, rows, d_model), bf16),
    ]
    dma = pltpu.SemaphoreType.DMA
    scratch = [
        pltpu.VMEM((4, 2, 2, cut, d_model), bf16),
        pltpu.VMEM((4, 2, 2, cut, d_model), bf16),
        pltpu.VMEM((3, 4, 2, cut, d_model), bf16),
        pltpu.VMEM((3, 4, cut, d_model), bf16),
        pltpu.VMEM((3, 3, cut, d_model), bf16),
        pltpu.VMEM((4, 2 * rows, d_model), bf16),
        pltpu.VMEM((4, 2 * rows, d_model), bf16),
        pltpu.VMEM((4, 4 * cut, 2 * rows), bf16),
        pltpu.VMEM((2, d_model, rows), bf16),
        pltpu.VMEM((2, d_model, d_model), bf16),
        pltpu.VMEM((2, rows, d_model), bf16),
        pltpu.VMEM((2, 4, rows, rows), f32),
        pltpu.VMEM((2, rows, d_model), f32),
        pltpu.VMEM((rows, d_model), f32),
        pltpu.VMEM((rows, d_model), f32),
        pltpu.VMEM((2, rows, d_model), bf16),
        pltpu.VMEM((3, rows, d_model // 4), f32),
        dma((3, SCATTER_SEMS)),
        dma((3, SCATTER_SEMS)),
        dma((4, 4)),
        dma((4, 4)),
        dma((LINE_SEMS,)),
        dma((LINE_SEMS,)),
        dma((2,)),
        dma((2,)),
        dma((2,)),
        dma((2,)),
        dma((5,)),
        pltpu.SemaphoreType.REGULAR,
    ]
    return pl.pallas_call(
        functools.partial(backward_kernel, last_layer),
        out_shape=out_shape,
        in_specs=[vmem] * 6 + [any_space] * 8,
        out_specs=[vmem] * 7 + [any_space],
        scratch_shapes=scratch,
        compiler_params=pltpu.CompilerParams(
            collective_id=1 if last_layer else 2, has_side_effects=True, vmem_limit_bytes=63 * 2**20
        ),
        name="backward_last" if last_layer else "backward_first",
    )(grad, x_in, mid_in, gains, shifts, pick, rows_in, s_all, att_all, hid_all, act_all, proj, up, down)


def shards_plain(
    tokens,
    cotangent,
    segment_ids,
    patch_pos,
    time_index,
    time_table,
    norm_gain,
    norm_shift,
    attn_weight,
    out_weight,
    qkv_bias,
    out_bias,
    mlp_weight,
    up_bias,
    rel_table,
):
    image_count = time_index.shape[0]
    layer_count = attn_weight.shape[0]
    narrow_at = lax.axis_index("narrow")
    wide_at = lax.axis_index("wide")
    wide_size = lax.axis_size("wide")
    own_rows = tokens.shape[0]
    in_rows, cols = attn_weight.shape[2:]
    image_local = segment_ids % image_count
    grid_slot = image_local * PATCHES + patch_pos
    own_slots = narrow_at * own_rows + jnp.arange(own_rows, dtype=jnp.int32)
    pick_in = (own_slots[:, None] == grid_slot[None, :]).astype(bf16)
    own_grid = lax.dynamic_slice_in_dim(grid_slot, narrow_at * own_rows, own_rows)
    pick_out = (own_grid[:, None] == jnp.arange(grid_slot.shape[0], dtype=jnp.int32)[None, :]).astype(bf16)

    def to_images(rows):
        every = lax.all_gather(rows, "narrow", axis=0, tiled=True)
        return jnp.dot(pick_in, every, preferred_element_type=f32)

    def to_rows(rows):
        every = lax.all_gather(rows, "narrow", axis=0, tiled=True)
        return jnp.dot(pick_out, every, preferred_element_type=f32).astype(bf16)

    steps_all = lax.all_gather(time_index, "wide", axis=0, tiled=True)
    step_hot = (steps_all[:, None] == jnp.arange(time_table.shape[0], dtype=jnp.int32)[None, :]).astype(bf16)
    time_rows = jnp.dot(step_hot, time_table, preferred_element_type=f32).astype(bf16)
    time_slice = lax.dynamic_slice_in_dim(time_rows, wide_at * in_rows, in_rows, axis=1)
    time_weight = attn_weight[:, 3:6]
    time_share = jnp.einsum("id,ljdc->ljic", time_slice, time_weight, preferred_element_type=f32)
    time_share = lax.psum_scatter(time_share, "wide", scatter_dimension=2, tiled=True)
    time_share = lax.all_gather(time_share, "narrow", axis=3, tiled=True)
    time_part = lax.dynamic_index_in_dim(time_share, narrow_at, axis=2, keepdims=False)

    tables = lax.all_gather(rel_table, "narrow", axis=1, tiled=True)
    qkv_bias_all = lax.all_gather(qkv_bias, "narrow", axis=2, tiled=True)
    up_bias_all = lax.all_gather(up_bias, "narrow", axis=1, tiled=True)

    def layer_params(at):
        return (norm_gain[at], norm_shift[at], qkv_bias_all[at], out_bias[at])

    weights = []
    for at in range(layer_count):
        packed = jnp.concatenate([attn_weight[at, 0], attn_weight[at, 1], attn_weight[at, 2], out_weight[at]], axis=1)
        weights.append((gather_unit(packed), gather_unit(mlp_weight[at, 0]), gather_unit(mlp_weight[at, 1])))

    residual = to_images(tokens)
    kept = []
    for at in range(layer_count):
        pairs = pair_bias(tables[at])
        middle, attn_saved = attention_forward(residual, weights[at][0], time_part[at], layer_params(at), pairs)
        residual, mlp_saved = mlp_forward(middle, weights[at][1], weights[at][2], layer_params(at), up_bias_all[at])
        kept.append((attn_saved, mlp_saved))
    block_output = to_rows(residual.astype(bf16))
    gradient = to_images(cotangent)
    attn_grads, out_grads, mlp_grads = [], [], []
    time_sums, small = [], []
    for at in reversed(range(layer_count)):
        attn_saved, mlp_saved = kept[at]
        grad_mid, up_grad, down_grad, mlp_small = mlp_backward(
            gradient, weights[at][1], weights[at][2], layer_params(at), mlp_saved
        )
        mlp_grads.insert(0, jnp.stack([scatter_unit(up_grad), scatter_unit(down_grad)]))
        gradient, proj_grad, sums, table_grad, attn_small = attention_backward(
            grad_mid, weights[at][0], layer_params(at), attn_saved
        )
        packed = scatter_unit(proj_grad)
        attn_grads.insert(0, jnp.stack([packed[:, j * cols : (j + 1) * cols] for j in range(3)]))
        out_grads.insert(0, packed[:, 3 * cols :])
        time_sums.insert(0, sums)
        small.insert(
            0,
            (
                jnp.stack([attn_small[0], mlp_small[0]]),
                jnp.stack([attn_small[1], mlp_small[1]]),
                jnp.stack([attn_small[2], mlp_small[2]]),
                jnp.stack([sums[0], sums[2]]),
                mlp_small[3],
                table_grad,
            ),
        )
    input_grad = to_rows(gradient.astype(bf16))

    def stacked(index_at):
        return jnp.stack([entry[index_at] for entry in small])

    totals = lax.psum(tuple(stacked(index_at) for index_at in range(6)), ("wide", "narrow"))

    def own_part(array, axis):
        size = array.shape[axis] // lax.axis_size("narrow")
        return lax.dynamic_slice_in_dim(array, narrow_at * size, size, axis=axis)

    time_low = jnp.stack(time_sums).astype(bf16)
    time_all = lax.all_gather(time_low, ("wide", "narrow"), axis=0, tiled=False)
    time_own = own_part(time_all, 3)
    time_weight_grad = jnp.einsum("id,iljc->ljdc", time_slice, time_own, preferred_element_type=f32)
    trow_share = jnp.einsum("iljc,ljdc->id", time_own, time_weight, preferred_element_type=f32)
    trow_share = lax.psum(trow_share, "narrow")
    trow = lax.all_gather(trow_share, "wide", axis=1, tiled=True)
    time_grad = jnp.einsum("is,id->sd", step_hot.astype(f32), trow, precision=highest)
    attn_grad = jnp.concatenate([jnp.stack(attn_grads).astype(f32), time_weight_grad], axis=1)
    return (
        block_output,
        input_grad,
        time_grad,
        totals[0],
        totals[1],
        attn_grad,
        jnp.stack(out_grads).astype(f32),
        own_part(totals[3], 2),
        totals[2],
        jnp.stack(mlp_grads).astype(f32),
        own_part(totals[4], 1),
        own_part(totals[5], 1),
    )


def bias_windows(tables):
    layers, heads = tables.shape[:2]
    near = jnp.arange(GRID, dtype=jnp.int32)
    span = jnp.arange(SPAN, dtype=jnp.int32)
    steps = (span[None, :, None] == near[:, None, None] - near[None, None, :] + (GRID - 1)).astype(f32)
    grid = tables.reshape(layers, heads, SPAN, SPAN)[:, :, ::-1]
    windows = jnp.einsum("lhab,xby->lhxay", grid, steps, precision=highest)
    windows = windows.reshape(layers, heads * GRID, SPAN * GRID)
    return jnp.pad(windows, ((0, 0), (0, 0), (0, 512 - SPAN * GRID)))


def fold_windows(windows):
    layers, heads = windows.shape[0], windows.shape[1] // GRID
    near = jnp.arange(GRID, dtype=jnp.int32)
    span = jnp.arange(SPAN, dtype=jnp.int32)
    steps = (span[None, :, None] == near[:, None, None] - near[None, None, :] + (GRID - 1)).astype(f32)
    grid = windows[:, :, : SPAN * GRID].reshape(layers, heads, GRID, SPAN, GRID)
    tables = jnp.einsum("lhxay,xby->lhab", grid, steps, precision=highest)
    return tables[:, :, ::-1].reshape(layers, heads, SPAN * SPAN)


def shards(
    tokens,
    cotangent,
    segment_ids,
    patch_pos,
    time_index,
    time_table,
    norm_gain,
    norm_shift,
    attn_weight,
    out_weight,
    qkv_bias,
    out_bias,
    mlp_weight,
    up_bias,
    rel_table,
):
    image_count = time_index.shape[0]
    layer_count = attn_weight.shape[0]
    in_rows, cols = attn_weight.shape[2:]
    by_links = lax.axis_size("wide") == 8 and lax.axis_size("narrow") == 4 and in_rows % 16 == 0
    if not by_links:
        return shards_plain(
            tokens, cotangent, segment_ids, patch_pos, time_index, time_table, norm_gain, norm_shift,
            attn_weight, out_weight, qkv_bias, out_bias, mlp_weight, up_bias, rel_table,
        )
    narrow_at = lax.axis_index("narrow")
    wide_at = lax.axis_index("wide")
    own_rows, d_model = tokens.shape
    image_local = segment_ids % image_count
    grid_slot = image_local * PATCHES + patch_pos
    own_slots = narrow_at * own_rows + jnp.arange(own_rows, dtype=jnp.int32)
    pick_in = (own_slots[:, None] == grid_slot[None, :]).astype(bf16)
    own_grid = lax.dynamic_slice_in_dim(grid_slot, narrow_at * own_rows, own_rows)
    pick_out = (own_grid[:, None] == jnp.arange(grid_slot.shape[0], dtype=jnp.int32)[None, :]).astype(bf16)

    step_own = (time_index[:, None] == jnp.arange(time_table.shape[0], dtype=jnp.int32)[None, :]).astype(bf16)
    time_own = jnp.dot(step_own, time_table, preferred_element_type=f32).astype(bf16)
    digits = jnp.stack([time_index // 32, time_index % 32]).astype(bf16)
    digits = jnp.pad(digits, ((0, 16 - image_count - 2), (0, d_model - image_count)))
    time_own = jnp.concatenate([time_own, digits], axis=0)
    time_weight = attn_weight[:, 3:6]
    time_packed = jnp.concatenate(
        [time_weight[:, 0], time_weight[:, 1], time_weight[:, 2], jnp.zeros_like(time_weight[:, 0])], axis=2
    )
    qkv_packed = jnp.concatenate(
        [qkv_bias[:, 0], jnp.zeros_like(qkv_bias[:, 0]), qkv_bias[:, 1], jnp.zeros_like(qkv_bias[:, 0])], axis=1
    )
    small_own = jnp.pad(jnp.concatenate([up_bias, qkv_packed], axis=0), ((0, 8 - 2 * layer_count), (0, 0)))
    pieces = []
    for at in range(layer_count):
        packed = jnp.concatenate([attn_weight[at, 0], attn_weight[at, 1], attn_weight[at, 2], out_weight[at]], axis=1)
        pieces += [packed, mlp_weight[at, 0], mlp_weight[at, 1]]
    wholes, saved, (block_low, gradient, time_all, time_sel) = forward_all(
        tokens,
        cotangent,
        pick_in,
        time_own,
        time_packed,
        bias_windows(rel_table),
        small_own,
        norm_gain.reshape(-1, d_model),
        norm_shift.reshape(-1, d_model),
        out_bias.reshape(-1, d_model),
        pieces,
    )
    time_all = time_all.reshape(8, 16, d_model)
    steps_all = time_all[:, image_count : image_count + 2, :image_count].astype(f32)
    steps_all = (steps_all[:, 0] * 32 + steps_all[:, 1]).astype(jnp.int32).reshape(-1)
    step_hot = (steps_all[:, None] == jnp.arange(time_table.shape[0], dtype=jnp.int32)[None, :]).astype(f32)
    time_slice = time_sel.reshape(8, 16, in_rows)[:, :image_count].reshape(-1, in_rows)

    def layer_back(at, grad, rows_in):
        return backward_layer(
            at == layer_count - 1, grad, saved[at], norm_gain[at], norm_shift[at], pick_out, rows_in,
            wholes[3 * at : 3 * at + 3],
        )

    attn_grads, out_grads, mlp_grads = [], [], []
    time_sums, small = [], []
    block_output = None
    for at in reversed(range(layer_count)):
        packed, up_part, down_part, gradient, moved, sums, windows, _ = layer_back(at, gradient, block_low)
        if at == layer_count - 1:
            block_output = moved
        mlp_grads.insert(0, jnp.stack([up_part, down_part]))
        attn_grads.insert(0, jnp.stack([packed[:, j * cols : (j + 1) * cols] for j in range(3)]))
        out_grads.insert(0, packed[:, 3 * cols :])
        qkv_sums = jnp.stack([sums[10:14, j * cols : (j + 1) * cols].reshape(-1) for j in range(3)])
        time_sums.insert(0, qkv_sums)
        small.insert(
            0,
            (
                sums[0:2],
                sums[2:4],
                sums[4:6],
                jnp.stack([qkv_sums[0], qkv_sums[2]]),
                sums[6:10].reshape(-1),
                windows.reshape(-1, 512),
            ),
        )
    input_grad = moved

    def stacked(index_at):
        return jnp.stack([entry[index_at] for entry in small])

    tables = fold_windows(stacked(5))
    totals = lax.psum(tuple(stacked(index_at) for index_at in range(5)) + (tables,), ("wide", "narrow"))

    def own_part(array, axis):
        size = array.shape[axis] // lax.axis_size("narrow")
        return lax.dynamic_slice_in_dim(array, narrow_at * size, size, axis=axis)

    time_low = jnp.stack(time_sums).astype(bf16)
    time_every = lax.all_gather(time_low, ("wide", "narrow"), axis=0, tiled=False)
    time_part = own_part(time_every, 3)
    time_weight_grad = jnp.einsum("id,iljc->ljdc", time_slice, time_part, preferred_element_type=f32)
    trow_share = jnp.einsum("iljc,ljdc->id", time_part, time_weight, preferred_element_type=f32)
    trow_share = lax.psum(trow_share, "narrow")
    trow = lax.all_gather(trow_share, "wide", axis=1, tiled=True)
    time_grad = jnp.einsum("is,id->sd", step_hot, trow, precision=highest)
    attn_grad = jnp.concatenate([jnp.stack(attn_grads), time_weight_grad], axis=1)
    return (
        block_output,
        input_grad,
        time_grad,
        totals[0],
        totals[1],
        attn_grad,
        jnp.stack(out_grads),
        own_part(totals[3], 2),
        totals[2],
        jnp.stack(mlp_grads),
        own_part(totals[4], 1),
        own_part(totals[5], 1),
    )


def solution(mesh):
    return jax.shard_map(
        shards,
        mesh=mesh,
        in_specs=(
            P(("wide", "narrow"), None),
            P(("wide", "narrow"), None),
            P("wide"),
            P("wide"),
            P("wide"),
            P(),
            P(),
            P(),
            P(None, None, "wide", "narrow"),
            P(None, "wide", "narrow"),
            P(None, None, "narrow"),
            P(),
            P(None, None, "wide", "narrow"),
            P(None, "narrow"),
            P(None, "narrow", None),
        ),
        out_specs=(
            P(("wide", "narrow"), None),
            P(("wide", "narrow"), None),
            P(),
            P(),
            P(),
            P(None, None, "wide", "narrow"),
            P(None, "wide", "narrow"),
            P(None, None, "narrow"),
            P(),
            P(None, None, "wide", "narrow"),
            P(None, "narrow"),
            P(None, "narrow", None),
        ),
        check_vma=False,
    )
```

time: 1390 us -> 1030 us (0.74)
  matrix products: 273 us -> 12.9 us
  local copies, waits for them, and re-layouts: 213 us -> 43.7 us
  blocking collectives: 260 us -> 92.7 us
  Pallas kernels: 573 us -> 724 us
  waiting for transfers between devices: 1.21 us -> 120 us
  other arithmetic: 47.2 us -> 15.5 us
    dot_general x53 -> x6, matrix products: 273 us -> 12.9 us  [the longest x1 6.68 us: fold_windows(): tables = jnp.einsum('lhxay,xby->lhab', grid, steps, precision=highest)]
    all_gather x5 -> x1, blocking collectives: 225 us -> 68.6 us  [shards(): lax.all_gather(time_low, ('wide', 'narrow'), axis=0, tiled=False)]
    pallas_call x3, Pallas kernels: 573 us -> 724 us  [the longest x2 371 us: backward_layer(): pl.pallas_call(functools.partial(backward_kernel, last_layer), out_shape=...]
    psum x2, waiting for transfers between devices: 0.01 us -> 120 us  [shards(): lax.psum(tuple((stacked(index_at) for index_at in range(5))) + (tables,),...]
    reshape x16 -> x8, local copies, waits for them, and re-layouts: 97.6 us -> 9.35 us  [the longest x1 4.86 us: fold_windows(): grid = windows[:, :, :SPAN * GRID].reshape(layers, heads, GRID, SPAN, GRID)]
    slice x17 -> x7, local copies, waits for them, and re-layouts: 41.2 us -> 4.57 us  [the longest x4 3 us: shards(): sums[10:14, j * cols:(j + 1) * cols].reshape(-1)]
    transpose x6 -> x1, local copies, waits for them, and re-layouts: 31.4 us -> 0.9 us  [bias_windows(): windows = jnp.einsum('lhab,xby->lhxay', grid, steps, precision=highest)]
    concatenate x4 -> x3, other arithmetic: 22.2 us -> 2.99 us  [the longest x1 1.73 us: shards(): jnp.concatenate([jnp.stack(attn_grads), time_weight_grad], axis=1)]
  transfers between devices with their start and end apart: 7 -> 2, of which waited for: 0 -> 1; matrix products, arithmetic and copies ran while one was open for 25% -> 4% of each run, Pallas kernels for 41% -> 0%
where the time goes in v2:
time: 1030 us; the launch traced here: 1020 us
  Pallas kernels  724 us (70%)
  waiting for transfers between devices  120 us (12%)
  blocking collectives  92.7 us (9%)
  local copies, waits for them, and re-layouts  43.7 us (4%)
  other arithmetic  15.5 us (2%)
  between operations  15 us (1%)
  matrix products  12.9 us (1%)
    pallas_call x2, Pallas kernels, backward_layer(): pl.pallas_call(functools.partial(backward_kernel, last_layer), out_shape=...  371 us
    pallas_call x1, Pallas kernels, forward_all(): pl.pallas_call(functools.partial(forward_kernel, layers), out_shape=out_s...  353 us
    psum x2, waiting for transfers between devices, shards(): lax.psum(tuple((stacked(index_at) for index_at in range(5))) + (tables,),...  120 us
    all_gather x1, blocking collectives, shards(): lax.all_gather(time_low, ('wide', 'narrow'), axis=0, tiled=False)  68.6 us
  transfers between devices with their start and end apart: 2, of which 1 were waited for; matrix products, arithmetic and copies ran while one was open for 4% of the time, Pallas kernels for 0%

profile of v2, /device:TPU:0, one launch (start us, length us, event | category | flops | bytes accessed | tf_op | source)
XLA Modules:
  0.0 1024.3 jit_solution(15771824075197357688)
XLA Ops:
  7.3 2.1 slice_bitcast_fusion.16
  9.4 2.1 slice_bitcast_fusion.12
  14.1 2.4 slice_bitcast_fusion
  18.5 0.9 copy.71
  19.4 1.5 reshape.126
  21.5 0.9 compare_convert_fusion.refs_2_
  22.6 0.9 fusion.refs_5_
  26.3 1.9 concatenate.33.refs_10_
  28.2 1.0 concatenate.34.refs_13_
  29.3 1.5 concatenate.30.refs_4_
  30.8 353.0 %forward_all.1 = (bf16[4,1152,1152]{2,1,0:T(8,128)(2,1)}, bf16[4,1152,1152]{2,1,0:T(8,128)(2,1)}, bf16[4,1152,1152]{2,1,0:T(8,128)(2,1)}, bf16[4,1152,1152]{2,1,...) custom-call(bf16[256,1152]{1,0:T(8,128)(2,1)} %refs_0_.1, ...), custom_call_target="tpu_custom_call" | custom-call | tf_op jit(solution)/shard_map/forward_all/pallas_call | solution.py:715
  383.8 168.6 %backward_last.1 = (f32[144,1152]{1,0:T(8,128)}, f32[144,1152]{1,0:T(8,128)}, f32[144,1152]{1,0:T(8,128)}, f32[256,1152]{1,0:T(8,128)}, bf16[256,1152]{1,0:T(8,1...) custom-call(f32[256,1152]{1,0:T(8,128)} %get-tuple-element.47.refs_0_, ...), custom_call_target="tpu_custom_call" | custom-call | tf_op jit(solution)/shard_map/backward_last/pallas_call | solution.py:1172
  552.4 202.8 %backward_first.1 = (f32[144,1152]{1,0:T(8,128)}, f32[144,1152]{1,0:T(8,128)}, f32[144,1152]{1,0:T(8,128)}, f32[256,1152]{1,0:T(8,128)}, bf16[256,1152]{1,0:T(8,...) custom-call(f32[256,1152]{1,0:T(8,128)} %get-tuple-element.59.refs_0_, ...), custom_call_target="tpu_custom_call" | custom-call | tf_op jit(solution)/shard_map/backward_first/pallas_call | solution.py:1172
  756.0 0.9 slice_bitcast_fusion.24
  757.0 0.9 slice_bitcast_fusion.26
  761.5 1.2 copy.80
  763.1 4.9 reshape.133
  768.0 6.7 convolution_bitcast_fusion.2
  774.9 0.9 reshape.134
  775.9 1.5 slice.251
  779.4 0.9 slice_bitcast_fusion.4
  782.6 68.6 %all_gather.7 = bf16[32,2,3,1152]{3,1,2,0:T(2,128)(2,1)S(1)} all-gather(bf16[1,2,3,1152]{3,1,2,0:T(2,128)(2,1)S(1)} %copy.75), channel_id=1, replica_groups=mesh['wide'=8,'narrow'=4] {'wide','narrow'}, dimensions={0}, use_global_device_ids=true | all-gather | bytes 456192 | tf_op jit(solution)/shard_map/all_gather | solution.py:1452
  853.0 16.2 %psum.49 = f32[32,144]{1,0:T(8,128)S(1)} all-reduce(f32[32,144]{1,0:T(8,128)S(1)} %convolution_bitcast_fusion.3), channel_id=1, replica_groups=mesh['wide'=8,'narrow'=4] {'narrow'}, use_global_device_ids=true, to_apply=%region_0.1 | all-reduce | flops 4608 | bytes 36864 | tf_op jit(solution)/shard_map/psum | solution.py:1456
  869.2 7.9 all-gather
  878.9 1.4 maximum_bitcast_fusion
  880.6 1.7 pad_maximum_fusion.1
  883.1 4.4 fusion.6
  887.6 1.7 pad_maximum_fusion
  889.4 1.3 constant_dynamic-slice_fusion.1
  890.7 1.4 constant_dynamic-slice_fusion.2
  892.1 120.0 %all-reduce.7.cloned.1.call-done = f32[2,16,961]{2,1,0:T(8,128)} async-done(((f32[2,16,961]{2,1,0:T(8,128)}), f32[2,16,961]{2,1,0:T(8,128)}) %all-reduce.7.cloned.1.call-update) | async-done | bytes 123024 | tf_op jit(solution)/shard_map/psum | solution.py:1445
  1012.1 1.5 constant_dynamic-slice_fusion
  (144 shorter events, 25.6 us)
Async XLA Ops:
  7.2 4.3 copy-start.18
  7.2 5.0 copy-start.19
  7.2 6.2 copy-start.17
  7.2 6.9 copy-start.27
  7.2 882.1 %all-reduce.9.cloned.1.call-start = ((), (), s32[]{:S(2)}) async-start(), calls=%async_computation.1 | async-start | bytes 221184 | tf_op jit(solution)/shard_map/psum | solution.py:1445
  9.4 7.1 copy-start.30
  9.4 7.6 copy-start
  14.1 3.5 copy-start.21
  18.4 2.5 copy-start.22
  18.4 3.1 copy-start.28
  18.4 3.1 copy-start.29
  19.4 5.0 copy-start.26
  19.4 6.9 copy-start.13
  19.4 8.9 copy-start.14
  19.4 8.9 copy-start.15
  20.9 7.4 copy-start.16
  20.9 8.4 copy-start.4
  20.9 8.4 copy-start.5
  552.4 204.5 %copy-start.20 = (f32[16,1152]{1,0:T(8,128)S(1)}, f32[16,1152]{1,0:T(8,128)}, u32[]{:S(2)}) copy-start(f32[16,1152]{1,0:T(8,128)} %get-tuple-element.72) | copy-start | bytes 221188
  552.4 210.4 %copy-start.12 = (f32[4,64,512]{2,1,0:T(8,128)S(1)}, f32[4,64,512]{2,1,0:T(8,128)}, u32[]{:S(2)}) copy-start(f32[4,64,512]{2,1,0:T(8,128)} %get-tuple-element.81) | copy-start | bytes 1572868
  761.5 250.6 %all-reduce.7.cloned.1.call-start = ((), (), s32[]{:S(2)}) async-start(), calls=%async_computation | async-start | bytes 262144 | tf_op jit(solution)/shard_map/psum | solution.py:1445
  774.6 4.5 copy-start.3
  774.6 4.8 copy-start.2
  775.8 76.4 %copy-start.1 = (bf16[2,6,144,288]{3,2,1,0:T(8,128)(2,1)S(1)}, bf16[2,6,144,288]{3,2,1,0:T(8,128)(2,1)}, u32[]{:S(2)}) copy-start(bf16[2,6,144,288]{3,2,1,0:T(8,128)(2,1)} %param.23) | copy-start | bytes 2985988
  878.1 2.3 copy-start.7
  880.6 2.5 copy-start.9
  883.1 4.5 copy-start.6
  887.6 125.9 %copy-start.10 = (bf16[256,1152]{1,0:T(8,128)(2,1)S(1)}, bf16[256,1152]{1,0:T(8,128)(2,1)}, u32[]{:S(2)}) copy-start(bf16[256,1152]{1,0:T(8,128)(2,1)} %get-tuple-element.144) | copy-start | bytes 1769476
  887.6 126.7 %copy-start.11 = (bf16[256,1152]{1,0:T(8,128)(2,1)S(1)}, bf16[256,1152]{1,0:T(8,128)(2,1)}, u32[]{:S(2)}) copy-start(bf16[256,1152]{1,0:T(8,128)(2,1)} %get-tuple-element.145) | copy-start | bytes 1769476
  889.4 125.8 %copy-start.25 = (f32[2,2,1152]{2,1,0:T(2,128)S(1)}, f32[2,2,1152]{2,1,0:T(2,128)}, u32[]{:S(2)}) copy-start(f32[2,2,1152]{2,1,0:T(2,128)} %get-tuple-element.147) | copy-start | bytes 55300
  889.4 126.4 %copy-start.24 = (f32[2,2,1152]{2,1,0:T(2,128)S(1)}, f32[2,2,1152]{2,1,0:T(2,128)}, u32[]{:S(2)}) copy-start(f32[2,2,1152]{2,1,0:T(2,128)} %get-tuple-element.148) | copy-start | bytes 55300
  889.4 127.0 %copy-start.23 = (f32[2,2,1152]{2,1,0:T(2,128)S(1)}, f32[2,2,1152]{2,1,0:T(2,128)}, u32[]{:S(2)}) copy-start(f32[2,2,1152]{2,1,0:T(2,128)} %get-tuple-element.152) | copy-start | bytes 55300
  (1 other events, 1.5 us)
Sparse Core Ops, SparseCore 0:
  761.6 121.4 all-reduce.8
  888.7 123.3 all-reduce.6

commit v3 on v2

--- a/solution.py
+++ b/solution.py
@@ -251,6 +251,8 @@
 
 
 LINE_SEMS = 5
+Z_AHEAD = 43.0
+UNIT_TIME = 43.0
 GATHER_SEMS = 58
 Y_FIRST, X_LAST, X_NEAR, X_FAR, Y_NEAR, Y_FAR = 5, 9, 13, 17, 21, 25
 C_OWN, C_Y, C_X, C_X_NEAR, C_Y_NEAR, C_X_FAR, C_Y_FAR = 29, 33, 37, 41, 45, 49, 53
@@ -291,50 +293,56 @@
         self.line.begin(self.piece)
         self.put(Y_FIRST, "y", z, 0, 0, self.first, self.piece.at[self.first])
         self.put(X_LAST, "x", z, 0, 0, self.last, self.piece.at[self.last])
+        self.put(X_NEAR, "x", z, 0, 0, self.first, self.piece.at[self.first])
+        self.put(Y_NEAR, "y", z, 0, 0, self.last, self.piece.at[self.last])
         self.put(C_OWN, "c", z, 0, 0, self.every, self.piece)
         self.local = pltpu.make_async_copy(self.piece, self.block(z, 0, 0, self.every), self.send.at[GATHER_SEMS - 1])
         self.local.start()
 
-    def second(self):
+    def along_z(self, far):
         def then(origin):
             self.put(Y_FIRST, "y", origin, 0, 0, self.first)
             self.put(X_LAST, "x", origin, 0, 0, self.last)
-            self.put(C_OWN, "c", origin, 0, 0, self.every)
-
-        for far in (1, 2, 3):
-            self.line.arrive(far, then)
-            yield
-
-    def third(self):
-        self.local.wait()
-        for origin in self.order:
             self.put(X_NEAR, "x", origin, 0, 0, self.first)
             self.put(Y_NEAR, "y", origin, 0, 0, self.last)
-        for at, origin in enumerate(self.order):
-            self.wait(Y_FIRST, "y", origin, 1, 0, self.first)
-            self.put(X_FAR, "x", origin, 1, 0, self.first)
-            self.put(C_Y, "c", origin, 1, 0, self.first)
-            self.wait(X_LAST, "x", origin, 0, 1, self.last)
-            self.put(Y_FAR, "y", origin, 0, 1, self.last)
-            self.put(C_X, "c", origin, 0, 1, self.last)
-            if at % 2:
-                yield
-
-    def fourth(self):
-        for at, origin in enumerate(self.order):
-            self.wait(X_NEAR, "x", origin, 0, 1, self.first)
-            self.put(C_X_NEAR, "c", origin, 0, 1, self.first)
-            self.wait(Y_NEAR, "y", origin, 1, 0, self.last)
-            self.put(C_Y_NEAR, "c", origin, 1, 0, self.last)
-            if at % 2:
-                yield
-        for at, origin in enumerate(self.order):
-            self.wait(X_FAR, "x", origin, 1, 1, self.first)
-            self.put(C_X_FAR, "c", origin, 1, 1, self.first)
-            self.wait(Y_FAR, "y", origin, 1, 1, self.last)
-            self.put(C_Y_FAR, "c", origin, 1, 1, self.last)
-            if at % 2:
-                yield
+            self.put(C_OWN, "c", origin, 0, 0, self.every)
+
+        self.line.arrive(far, then)
+
+    def across(self, at):
+        origin = self.order[at]
+        self.wait(Y_FIRST, "y", origin, 1, 0, self.first)
+        self.put(X_FAR, "x", origin, 1, 0, self.first)
+        self.put(C_Y, "c", origin, 1, 0, self.first)
+        self.wait(X_LAST, "x", origin, 0, 1, self.last)
+        self.put(Y_FAR, "y", origin, 0, 1, self.last)
+        self.put(C_X, "c", origin, 0, 1, self.last)
+
+    def near_to_core(self, at):
+        origin = self.order[at]
+        self.wait(X_NEAR, "x", origin, 0, 1, self.first)
+        self.put(C_X_NEAR, "c", origin, 0, 1, self.first)
+        self.wait(Y_NEAR, "y", origin, 1, 0, self.last)
+        self.put(C_Y_NEAR, "c", origin, 1, 0, self.last)
+
+    def far_to_core(self, at):
+        origin = self.order[at]
+        self.wait(X_FAR, "x", origin, 1, 1, self.first)
+        self.put(C_X_FAR, "c", origin, 1, 1, self.first)
+        self.wait(Y_FAR, "y", origin, 1, 1, self.last)
+        self.put(C_Y_FAR, "c", origin, 1, 1, self.last)
+
+    def steps(self, base):
+        start = max(0.0, base - Z_AHEAD)
+        out = [(start, self.begin)]
+        out += [(start + 1.0 + 7.5 * far, functools.partial(self.along_z, far)) for far in (1, 2, 3)]
+        for at in range(4):
+            known = start + 24.0 if at else 0.0
+            out.append((max(known, base + 9.0 + 9.0 * at), functools.partial(self.across, at)))
+            out.append((max(known + 1.0, base + 15.0 + 9.0 * at), functools.partial(self.near_to_core, at)))
+            out.append((max(known + 2.0, base + 25.0 + 9.0 * at), functools.partial(self.far_to_core, at)))
+        out.append((base + 56.0, self.finish))
+        return out
 
     def finish(self):
         firsts = (Y_FIRST, X_NEAR, X_FAR, C_Y, C_X_NEAR, C_X_FAR)
@@ -352,6 +360,7 @@
                 self.copy(base, "c", origin, 0, 0, self.last).wait_send()
             self.copy(C_OWN, "c", origin, 0, 0, self.every).wait_send()
         self.line.finish()
+        self.local.wait()
 
 
 def column_ids(width):
@@ -405,6 +414,10 @@
 
 FORWARD_IN = 17
 LAYER_SAVED = 6
+
+
+def edges(head_cols):
+    return 3 * head_cols // 128 * 128, -(-3 * head_cols // 128) * 128
 
 
 def gelu(values):
@@ -436,7 +449,7 @@
     (
         send, recv, z_send, z_recv, t_send, t_recv, save_sem, w_sem,
         w_slots, tok_all, cot_all, windows_all, small_all, time_all, share, share_y, share_x, share_c, share_z,
-        x_buf, mid_buf, low_buf, acc_buf, s_buf, att_buf, act_buf, hid_buf, bias_buf,
+        x_buf, mid_buf, low_buf, acc_buf, s_buf, att_buf, act_buf, hid_buf, bias_buf, mixed_buf,
     ) = refs
     place = Place()
     place.greet()
@@ -444,42 +457,43 @@
         GatherUnit(place, pieces[u], wholes[u], send.at[u], recv.at[u], unit_cut(u, pieces[u].shape[0]))
         for u in range(units)
     ]
-    state = {"done": 0}
+    state = set()
     tokens_n, d_model = tokens.shape
     head_cols = d_model // 4
     yp, xp, cp = ((place.wide(1, 0, 0), place.z), (place.wide(0, 1, 0), place.z), (place.wide(0, 0, 1), place.z))
     py, px, pc = place.y, place.x, place.c
 
-    def comm_steps():
-        gather[0].begin()
+    tok, win, small, cots, rz = (
+        z_line(place, every, z_send.at[at], z_recv.at[at])
+        for at, every in enumerate((tok_all, windows_all, small_all, cot_all, share_z))
+    )
+    kept = [
+        pltpu.make_async_copy(src, every.at[place.z], save_sem.at[at])
+        for at, (src, every) in enumerate(
+            ((tokens, tok_all), (windows_own, windows_all), (small_own, small_all), (cot, cot_all))
+        )
+    ]
+    given = {}
+
+    def give(slot, src, dst, peer):
+        given[slot] = remote(src, dst, t_send.at[slot], t_recv.at[slot], peer)
+
+    def time_core():
+        for copy in kept:
+            copy.start()
         time_all[py, px, pc] = time_own[...]
-        first = remote(time_all.at[py, px, pc], time_all.at[py, px, pc], t_send.at[0], t_recv.at[0], cp)
-        tok, win, small, cots, rz = (
-            z_line(place, every, z_send.at[at], z_recv.at[at])
-            for at, every in enumerate((tok_all, windows_all, small_all, cot_all, share_z))
-        )
-        small.begin(small_own)
-        tok.begin(tokens)
-        win.begin(windows_own)
-        own = [
-            pltpu.make_async_copy(tokens, tok_all.at[place.z], save_sem.at[0]),
-            pltpu.make_async_copy(windows_own, windows_all.at[place.z], save_sem.at[1]),
-            pltpu.make_async_copy(small_own, small_all.at[place.z], save_sem.at[2]),
-            pltpu.make_async_copy(cot, cot_all.at[place.z], save_sem.at[3]),
-        ]
-        for copy in own:
-            copy.start()
-        gather[1].begin()
-        first.wait_recv()
-        second = remote(time_all.at[py, px], time_all.at[py, px], t_send.at[1], t_recv.at[1], xp)
-        yield from gather[0].second()
-        small.arrive(1)
-        tok.arrive(1)
-        win.arrive(1)
-        second.wait_recv()
-        third = remote(time_all.at[py], time_all.at[py], t_send.at[2], t_recv.at[2], yp)
-        yield from gather[0].third()
-        third.wait_recv()
+        give(0, time_all.at[py, px, pc], time_all.at[py, px, pc], cp)
+
+    def time_x():
+        given[0].wait_recv()
+        give(1, time_all.at[py, px], time_all.at[py, px], xp)
+
+    def time_y():
+        given[1].wait_recv()
+        give(2, time_all.at[py], time_all.at[py], yp)
+
+    def time_share():
+        given[2].wait_recv()
         rows = time_all[...].reshape(128, d_model)
         cut = time_weight.shape[1]
         at_row = lax.broadcasted_iota(jnp.int32, (d_model, cut), 0)
@@ -491,54 +505,55 @@
         for layer in range(layers):
             part = dot_plain(picked, time_weight[layer]).reshape(2, 2, 2, 16, d_model)
             share[:, :, :, layer] = part[:, :, :, :8]
-        ry = remote(share.at[1 - py], share_y, t_send.at[3], t_recv.at[3], yp)
-        gather[2].begin()
-        small.arrive(2)
-        tok.arrive(2)
-        win.arrive(2)
-        ry.wait_recv()
+        give(3, share.at[1 - py], share_y, yp)
+
+    def share_step_x():
+        given[3].wait_recv()
         share[py] = share[py] + share_y[...]
-        rx = remote(share.at[py, 1 - px], share_x, t_send.at[4], t_recv.at[4], xp)
-        yield from gather[1].second()
-        rx.wait_recv()
+        give(4, share.at[py, 1 - px], share_x, xp)
+
+    def share_step_c():
+        given[4].wait_recv()
         share[py, px] = share[py, px] + share_x[...]
-        rc = remote(share.at[py, px, 1 - pc], share_c, t_send.at[5], t_recv.at[5], cp)
-        rc.wait_recv()
+        give(5, share.at[py, px, 1 - pc], share_c, cp)
+
+    def share_step_z():
+        given[5].wait_recv()
         share[py, px, pc] = share[py, px, pc] + share_c[...]
         share_z[place.z] = share[py, px, pc]
         rz.begin(share_z.at[place.z])
-        yield from gather[0].fourth()
-        rz.arrive(1)
-        yield from gather[1].third()
-        rz.arrive(2)
-        gather[0].finish()
-        for line in (small, tok, win, rz):
-            line.arrive(3)
-            line.finish()
-        for copy in own:
-            copy.wait()
-        state["done"] = 1
-        for copy in (first, second, third, ry, rx, rc):
-            copy.wait_send()
-        yield
-        for unit in range(3, units + 3):
-            if unit < units:
-                gather[unit].begin()
-                yield
-            if unit - 1 < units:
-                yield from gather[unit - 1].second()
-                yield from gather[unit - 1].third()
-            if unit - 2 < units:
-                yield from gather[unit - 2].fourth()
-                gather[unit - 2].finish()
-                state["done"] = unit - 1
-                yield
-            if unit == 3:
-                cots.begin(cot)
-            elif unit <= 6:
-                cots.arrive(unit - 3)
-            if unit == 6:
-                cots.finish()
+        for slot in range(6):
+            given[slot].wait_send()
+
+    def line_steps(line, own, start, pace):
+        steps = [(start, functools.partial(line.begin, own))]
+        steps += [(start + pace * far, functools.partial(line.arrive, far)) for far in (1, 2, 3)]
+        return steps + [(start + 3 * pace + 4.0, line.finish)]
+
+    def mark(key):
+        if key == "rows":
+            for copy in kept:
+                copy.wait()
+        state.add(key)
+
+    events = [
+        (0.1, time_core),
+        (3.0, time_x),
+        (7.0, time_y),
+        (11.0, time_share),
+        (18.0, share_step_x),
+        (24.0, share_step_c),
+        (28.0, share_step_z),
+    ]
+    events += line_steps(small, small_own, 0.2, 5.0)
+    events += [(28.0 + 8.0 * far, functools.partial(rz.arrive, far)) for far in (1, 2, 3)] + [(56.0, rz.finish)]
+    events += line_steps(win, windows_own, 34.0, 10.0)
+    events += line_steps(tok, tokens, 36.0, 14.0)
+    events += [(84.0, functools.partial(mark, "rows"))]
+    events += line_steps(cots, cot, 130.0, 16.0)
+    for at, unit in enumerate(gather):
+        events += unit.steps(UNIT_TIME * at)
+        events.append((UNIT_TIME * at + 56.5, functools.partial(mark, at)))
 
     stream = Stream(w_slots, w_sem, [wholes[u].at[z] for u in range(units) for z in range(4)])
     pending = {}
@@ -555,16 +570,17 @@
     def weights(unit, z):
         at = unit * 4 + z
         stream.ensure(at)
-        ready = state["done"] * 4
-        stream.ensure(min(at + 1, ready - 1))
+        if (at + 1) // 4 in state:
+            stream.ensure(at + 1)
         return stream.take(at)
 
     def compute_steps():
         columns = column_ids(d_model)
+        out_start, qkv_end = edges(head_cols)
         for layer in range(layers):
             x_save, mid_save, s_save, att_save, hid_save, act_save = saved[layer]
             row = 2 * layer
-            yield 3 * layer + 1
+            yield (3 * layer if layer else "rows"), 2.0
             if layer == 0:
                 total = dot_plain(pick[:, 0:tokens_n], tok_all[0])
                 for z in range(1, 4):
@@ -577,13 +593,15 @@
             low_buf[...] = (unit * gains[row : row + 1, :] + shifts[row : row + 1, :]).astype(bf16)
             settle(6)
             for z in range(4):
-                yield 3 * layer + 1
+                yield 3 * layer, 2.0
                 w = weights(3 * layer, z)
                 share_rows = share_z[z, layer]
                 at_image = lax.broadcasted_iota(jnp.int32, share_rows.shape, 0) == place.z
                 offset = jnp.sum(jnp.where(at_image, share_rows, 0.0), axis=0, keepdims=True)
                 offset = offset + small_all[z, 2 + layer : 3 + layer, :]
-                s_buf[z] = (dot_plain(low_buf[...], w[...]) + offset).astype(bf16)
+                spatial = dot_plain(low_buf[...], w[:, :qkv_end]) + offset[:, :qkv_end]
+                s_buf[z, :, :qkv_end] = spatial.astype(bf16)
+                yield 3 * layer, 2.0
                 q = s_buf[z, :, 0:head_cols]
                 k = s_buf[z, :, head_cols : 2 * head_cols]
                 v = s_buf[z, :, 2 * head_cols : 3 * head_cols]
@@ -591,7 +609,7 @@
                 slot = z % 2
                 settle(8 + slot)
 
-                def one_head(head, mixed):
+                def one_head(head, carry):
                     here = head_of == head
 
                     def put(grid_row, block):
@@ -605,12 +623,17 @@
                     exponent = jnp.exp(scores - top)
                     attention = exponent / jnp.sum(exponent, axis=-1, keepdims=True)
                     att_buf[slot, head] = attention
-                    return mixed + dot_plain(attention.astype(bf16), jnp.where(here, v, 0))
-
-                mixed = lax.fori_loop(0, 4, one_head, jnp.zeros((tokens_n, head_cols), f32))
+                    mixed_buf[...] += dot_plain(attention.astype(bf16), jnp.where(here, v, 0))
+                    return carry
+
+                mixed_buf[...] = jnp.zeros_like(mixed_buf)
+                for pair in range(2):
+                    lax.fori_loop(2 * pair, 2 * pair + 2, one_head, 0)
+                    yield 3 * layer, 2.0
                 save(8 + slot, att_buf.at[slot], att_save.at[z])
-                s_buf[z, :, 3 * head_cols :] = mixed.astype(bf16)
-                branch = dot_turned(jnp.where(columns >= 3 * head_cols, s_buf[z], 0), w[...])
+                s_buf[z, :, 3 * head_cols :] = mixed_buf[...].astype(bf16)
+                heads = jnp.where(columns[:, out_start:] >= 3 * head_cols, s_buf[z, :, out_start:], 0)
+                branch = dot_turned(heads, w[:, out_start:])
                 acc_buf[...] = branch if z == 0 else acc_buf[...] + branch
             save(6, s_buf, s_save)
             settle(4)
@@ -620,7 +643,7 @@
             low_buf[...] = (unit * gains[row + 1 : row + 2, :] + shifts[row + 1 : row + 2, :]).astype(bf16)
             settle(7)
             for z in range(4):
-                yield 3 * layer + 2
+                yield 3 * layer + 1, 2.5
                 w = weights(3 * layer + 1, z)
                 slot = z % 2
                 settle(10 + slot)
@@ -629,7 +652,7 @@
                 act_buf[z] = gelu(hid_buf[slot]).astype(bf16)
             save(7, act_buf, act_save)
             for z in range(4):
-                yield 3 * layer + 3
+                yield 3 * layer + 2, 1.8
                 w = weights(3 * layer + 2, z)
                 branch = dot_turned(act_buf[z], w[...])
                 acc_buf[...] = branch if z == 0 else acc_buf[...] + branch
@@ -642,18 +665,21 @@
         for slot in list(pending):
             settle(slot)
 
-    interleave(comm_steps(), compute_steps(), state)
-
-
-def interleave(comm, compute, state, pace=1):
-    need = next(compute)
-    count = 0
-    for _ in comm:
-        count += 1
-        if count % pace == 0 and need is not None and state["done"] >= need:
-            need = next(compute, None)
-    while need is not None:
-        need = next(compute, None)
+    interleave(events, compute_steps(), state)
+
+
+def interleave(events, compute, state):
+    events = sorted(events, key=lambda item: item[0])
+    clock = 0.0
+    wanted = next(compute)
+    while wanted is not None or events:
+        if events and (events[0][0] <= clock or wanted is None or wanted[0] not in state):
+            at, step = events.pop(0)
+            clock = max(clock, at)
+            step()
+            continue
+        clock += wanted[1]
+        wanted = next(compute, None)
 
 
 def forward_all(tokens, cot, pick, time_own, time_weight, windows_own, small_own, gains, shifts, out_bias, pieces):
@@ -711,6 +737,7 @@
         pltpu.VMEM((4, rows, d_model), bf16),
         pltpu.VMEM((2, rows, d_model), f32),
         pltpu.VMEM((rows, rows), f32),
+        pltpu.VMEM((rows, d_model // 4), f32),
     ]
     out = pl.pallas_call(
         functools.partial(forward_kernel, layers),
@@ -764,16 +791,8 @@
 SCATTER_SEMS = 23
 
 
-def add_rows(total, part, rows):
-    step = 16
-
-    def one(at, carry):
-        here = pl.ds(pl.multiple_of(at * step, step), step)
-        both = total[here, :].astype(f32) + part[here, :].astype(f32)
-        total[here, :] = both.astype(total.dtype)
-        return carry
-
-    lax.fori_loop(0, rows // step, one, 0)
+def add_into(total, part):
+    total[...] = total[...] + part[...]
 
 
 class ScatterUnit:
@@ -803,18 +822,18 @@
         p = self.place
         self.copies[4 + k].wait_recv()
         for block in range(2):
-            add_rows(self.total.at[k, block, p.x, self.first], self.far.at[k, block, self.first], self.cut)
+            add_into(self.total.at[k, block, p.x, self.first], self.far.at[k, block, self.first])
         self.put(12 + k, (p.wide(1, 0), p.z), self.total.at[k, 1 - p.y, p.x, self.first], self.near.at[k, self.first])
         self.copies[8 + k].wait_recv()
         for block in range(2):
-            add_rows(self.total.at[k, p.y, block, self.last], self.far.at[k, block, self.last], self.rows - self.cut)
+            add_into(self.total.at[k, p.y, block, self.last], self.far.at[k, block, self.last])
         self.put(16 + k, (p.wide(0, 1), p.z), self.total.at[k, p.y, 1 - p.x, self.last], self.near.at[k, self.last])
 
     def third_stage(self, k):
         p = self.place
         self.copies[12 + k].wait_recv()
         self.copies[16 + k].wait_recv()
-        add_rows(self.total.at[k, p.y, p.x], self.near.at[k], self.rows)
+        add_into(self.total.at[k, p.y, p.x], self.near.at[k])
         if k:
             self.put(19 + k, (p.wide(), p.along_z(k)), self.total.at[k, p.y, p.x], self.from_z.at[k - 1])
             self.closed.add(k)
@@ -823,18 +842,10 @@
         p = self.place
         for k in (1, 2, 3):
             self.copies[19 + k].wait_recv()
-        own = self.total.at[0, p.y, p.x]
-        step = 16
-
-        def one(at, carry):
-            here = pl.ds(pl.multiple_of(at * step, step), step)
-            both = own[here, :].astype(f32)
-            for k in range(3):
-                both = both + self.from_z[k, here, :].astype(f32)
-            self.out[here, :] = both
-            return carry
-
-        lax.fori_loop(0, self.rows // step, one, 0)
+        both = self.total[0, p.y, p.x].astype(f32)
+        for k in range(3):
+            both = both + self.from_z[k].astype(f32)
+        self.out[...] = both
         self.settle(list(self.copies))
         self.closed.add(0)
 
@@ -862,12 +873,14 @@
         return out
 
     (
-        grad, x_in, mid_in, gains, shifts, pick, rows_in, s_all, att_all, hid_all, act_all, proj, up, down,
-    ) = take(14)
-    proj_out, up_out, down_out, grad_out, rows_out, small_out, table_out, rows_all = take(8)
+        grad, mid_in, gains, shifts, trow_in, x_in, pick_in, time_weight, rows_in, s_all, att_all, hid_all, act_all,
+        proj, up, down,
+    ) = take(16)
+    proj_out, up_out, down_out, grad_out, rows_out, row_sums, table_sums, time_sums, trow_out, rows_all = take(10)
     (
         total_a, total_b, far, near, from_z, right_a, right_b, left, turned,
-        w_slots, s_slots, att_slots, hid_slots, acc_buf, mid_grad, low_buf, head_grads,
+        w_slots, s_slots, att_slots, hid_slots, acc_buf, low_buf, head_grads,
+        row_parts, rows_z, rows_w, table_parts, table_z, table_w, trow_z, small_send, small_recv,
         send, recv, left_send, left_recv, line_send, line_recv, w_sem, s_sem, att_sem, hid_sem, load_sem, credit,
     ) = refs
     place = Place()
@@ -878,6 +891,7 @@
     core = (place.wide(0, 0, 1), place.z)
     zs = {k: place.along_z(k) for k in range(4)}
     columns = column_ids(d_model)
+    out_start, qkv_end = edges(head_cols)
     units = {
         name: ScatterUnit(
             place, out, total, far.at[at], near.at[at], from_z.at[at], send.at[at], recv.at[at], unit_cut(at, cut)
@@ -902,7 +916,7 @@
             for copy in left_copies[at - 2]:
                 copy.wait_send()
         flipped = turned.at[at % 2]
-        flipped[...] = values.astype(f32).T.astype(bf16)
+        flipped[...] = values.T
         copies = []
         for block in range(4):
             mine = pl.multiple_of((2 * block + place.c) * cut, 16)
@@ -944,32 +958,124 @@
 
     def weight_grad(name, k, buffer, *lefts):
         unit = units[name]
-        part = dot_plain(left[lefts[0]], buffer[zs[k]])
-        if len(lefts) > 1:
-            part = jnp.where(columns < 3 * head_cols, part, dot_plain(left[lefts[1]], buffer[zs[k]]))
-        low = part.astype(bf16)
-        for block in range(4):
-            unit.total[k, block // 2, block % 2] = low[block * cut : (block + 1) * cut]
+        if len(lefts) == 1:
+            ranges = [(0, d_model, dot_plain(left[lefts[0]], buffer[zs[k]]))]
+        else:
+            first = dot_plain(left[lefts[0]], buffer[zs[k], :, 0:qkv_end])
+            last = dot_plain(left[lefts[1]], buffer[zs[k], :, out_start:])
+            edge = jnp.where(
+                columns[:, out_start:qkv_end] < 3 * head_cols, first[:, out_start:], last[:, : qkv_end - out_start]
+            )
+            ranges = [
+                (0, out_start, first[:, :out_start]), (out_start, qkv_end, edge),
+                (qkv_end, d_model, last[:, qkv_end - out_start :]),
+            ]
+        for start, stop, part in ranges:
+            low = part.astype(bf16)
+            for block in range(4):
+                unit.total[k, block // 2, block % 2, :, start:stop] = low[block * cut : (block + 1) * cut]
+
+    late = {}
+
+    def late_load(src, dst, slot):
+        late[slot] = pltpu.make_async_copy(src, dst, load_sem.at[slot])
+        late[slot].start()
+
+    def late_wait(slot):
+        late[slot].wait()
+
+    def put_row(row, values):
+        for z in range(4):
+            row_parts[z, row : row + 1, :] = values
+
+    small = {}
+    axes = ((core, 6), ((place.wide(0, 1, 0), place.z), 9), ((place.wide(1, 0, 0), place.z), 12))
+    own_time = (
+        time_sums.at[place.y, place.x, place.c], time_sums.at[place.y, place.x], time_sums.at[place.y]
+    )
+    own_trow = (trow_out.at[place.y, place.x, place.c], trow_out.at[place.y, place.x], trow_out.at[place.y])
+
+    def give(slot, src, dst, peer):
+        small[slot] = remote(src, dst, small_send.at[slot], small_recv.at[slot], peer)
+
+    def small_begin():
+        for k in (1, 2, 3):
+            peer = (place.wide(), zs[k])
+            give(k - 1, row_parts.at[zs[k]], rows_z.at[k - 1], peer)
+            give(k + 2, table_parts.at[zs[k]], table_z.at[k - 1], peer)
+        return ((9.0, small_along_z),)
+
+    def small_along_z():
+        for slot in range(6):
+            small[slot].wait_recv()
+        totals = row_parts[place.z]
+        at_row = lax.broadcasted_iota(jnp.int32, (16, d_model), 0)
+        times = jnp.where(at_row == place.z, totals[7:8, :], 0.0)
+        tables = table_parts[place.z]
+        for k in (1, 2, 3):
+            part = rows_z[k - 1]
+            times = jnp.where(at_row == place.along_z(4 - k), part[7:8, :], times)
+            totals = totals + part
+            tables = tables + table_z[k - 1]
+        row_sums[...] = totals
+        table_sums[...] = tables
+        time_sums[place.y, place.x, place.c] = times.astype(bf16)
+        small_across(0)
+        return ((4.0, functools.partial(small_step, 0)),)
+
+    def small_across(axis):
+        peer, slot = axes[axis]
+        give(slot, row_sums, rows_w.at[axis], peer)
+        give(slot + 1, table_sums, table_w.at[axis], peer)
+        give(slot + 2, own_time[axis], own_time[axis], peer)
+
+    def small_step(axis):
+        slot = axes[axis][1]
+        for at in range(slot, slot + 3):
+            small[at].wait_recv()
+            small[at].wait_send()
+        row_sums[...] = row_sums[...] + rows_w[axis]
+        table_sums[...] = table_sums[...] + table_w[axis]
+        if axis < 2:
+            small_across(axis + 1)
+            return ((5.0, functools.partial(small_step, axis + 1)),)
+        late_wait(6)
+        times = jnp.where(columns < 3 * head_cols, time_sums[...].reshape(128, d_model), 0)
+        part = dot_turned(times, s_slots[0, 0:cut]).reshape(8, 16, cut)[:, :8]
+        part = part + trow_in[...]
+        trow_out[place.y, place.x, place.c] = part
+        if last_layer:
+            return None
+        for k in (1, 2, 3):
+            give(14 + k, own_trow[0], trow_z.at[k - 1], (place.wide(), zs[k]))
+        return ((6.0, trow_along_z),)
+
+    def trow_along_z():
+        for slot in (15, 16, 17):
+            small[slot].wait_recv()
+            small[slot].wait_send()
+        here = trow_out[place.y, place.x, place.c] + trow_z[0] + trow_z[1] + trow_z[2]
+        trow_out[place.y, place.x, place.c] = here
+        give(18, own_trow[0], own_trow[0], axes[0][0])
+        return ((4.0, functools.partial(trow_step, 0)),)
+
+    def trow_step(axis):
+        small[18 + axis].wait_recv()
+        small[18 + axis].wait_send()
+        if axis < 2:
+            give(19 + axis, own_trow[axis + 1], own_trow[axis + 1], axes[axis + 1][0])
+            return ((5.0, functools.partial(trow_step, axis + 1)),)
 
     def compute():
         low_buf[0] = grad[...].astype(bf16)
-        small_out[...] = jnp.zeros_like(small_out)
-        small_out[5:6, :] = column_sums(low_buf[0].astype(f32))
+        put_row(5, column_sums(low_buf[0].astype(f32)))
         make_left(0, low_buf[0])
         left_ready(0)
-        for k, load in loads:
-            load.wait()
+        for at, k in enumerate(FAR_FIRST):
+            loads[at][1].wait()
             right_copies["down", k].wait_recv()
             weight_grad("down", k, right_a, 0)
-            yield 2.0, [(units["down"], k)]
-        for k, load in loads:
-            right_copies["down", k].wait_send()
-        pl.semaphore_signal(credit, inc=1, device_id=core, device_id_type=MESH)
-        unit, scale = unit_rows(mid_in[...])
-        make_left(1, (unit * gains[1:2, :] + shifts[1:2, :]).astype(bf16))
-        left_ready(1)
-        yield 3.0, []
-        for at, k in enumerate(FAR_FIRST):
+            yield 1.8, [(units["down"], k)]
             w = weights.take(2 * at)
             hid = hidden.take(at)
             act_grad = dot_plain(low_buf[0], w[...])
@@ -978,26 +1084,33 @@
             weights.ensure(2 * at + 2)
             hidden.ensure(at + 2)
             give_right("up", 1, k, right_b.at[zs[k], pl.ds(0, rows)], right_b)
-            small_out[pl.ds(6 + zs[k], 1), :] = column_sums(hid_grad.astype(f32))
+            row_parts[zs[k], 6:7, :] = column_sums(hid_grad.astype(f32))
             yield 2.5, []
             w = weights.take(2 * at + 1)
             part = dot_turned(right_b[zs[k], 0:rows], w[...])
             acc_buf[...] = part if at == 0 else acc_buf[...] + part
             weights.ensure(2 * at + 3)
             yield 1.5, []
-            right_copies["up", k].wait_recv()
-            weight_grad("up", k, right_b, 1)
-            yield 1.5, [(units["up"], k)]
+        for k in FAR_FIRST:
+            right_copies["down", k].wait_send()
+        pl.semaphore_signal(credit, inc=1, device_id=core, device_id_type=MESH)
         unit, scale = unit_rows(mid_in[...])
+        make_left(1, (unit * gains[1:2, :] + shifts[1:2, :]).astype(bf16))
         from_norm = norm_back(acc_buf[...], unit, scale, gains[1:2, :])
-        small_out[1:2, :] = column_sums(acc_buf[...] * unit)
-        small_out[3:4, :] = column_sums(acc_buf[...])
-        mid_grad[...] = grad[...] + from_norm
-        low_buf[0] = mid_grad[...].astype(bf16)
-        small_out[4:5, :] = column_sums(low_buf[0].astype(f32))
-        yield 3.0, []
+        put_row(1, column_sums(acc_buf[...] * unit))
+        put_row(3, column_sums(acc_buf[...]))
+        grad_out[...] = grad[...] + from_norm
+        low_buf[0] = grad_out[...].astype(bf16)
+        put_row(4, column_sums(low_buf[0].astype(f32)))
+        late_load(x_in, hid_slots.at[0], 5)
+        yield 4.0, []
+        left_ready(1)
+        right_copies["up", FAR_FIRST[0]].wait_recv()
+        weight_grad("up", FAR_FIRST[0], right_b, 1)
+        yield 1.5, [(units["up"], FAR_FIRST[0])]
         make_left(2, low_buf[0])
-        unit, scale = unit_rows(x_in[...])
+        late_wait(5)
+        unit, scale = unit_rows(hid_slots[0])
         make_left(3, (unit * gains[0:1, :] + shifts[0:1, :]).astype(bf16))
         left_ready(2)
         left_ready(3)
@@ -1006,10 +1119,14 @@
         head_of = column_ids(head_cols) // HEAD_DIM
         score_scale = HEAD_DIM ** (-0.5)
         for at, k in enumerate(FAR_FIRST):
+            if at:
+                right_copies["up", k].wait_recv()
+                weight_grad("up", k, right_b, 1)
+                yield 1.5, [(units["up"], k)]
             w = weights.take(8 + at)
             s = saved.take(at)
             attention_slot = attentions.take(at)
-            low_buf[1] = dot_plain(low_buf[0], w[...]).astype(bf16)
+            low_buf[1, :, out_start:] = dot_plain(low_buf[0], w[:, out_start:]).astype(bf16)
             mixed_grad = low_buf[1, :, 3 * head_cols :]
             q = s[:, 0:head_cols]
             key = s[:, head_cols : 2 * head_cols]
@@ -1024,13 +1141,15 @@
                 both = attention * dot_back
                 score_low = (both - attention * jnp.sum(both, axis=-1, keepdims=True)).astype(bf16)
                 first_row = pl.multiple_of(head * GRID, GRID)
-                table_out[zs[k], pl.ds(first_row, GRID), :] = fold_window(score_low.astype(f32))
+                table_parts[zs[k], pl.ds(first_row, GRID), :] = fold_window(score_low.astype(f32))
                 head_grads[0] += dot_plain(score_low, jnp.where(here, key, 0))
                 head_grads[1] += dot_rows(score_low, jnp.where(here, q, 0))
                 head_grads[2] += dot_rows(attention.astype(bf16), own_grad)
                 return carry
 
-            lax.fori_loop(0, 4, one_head, 0)
+            lax.fori_loop(0, 2, one_head, 0)
+            yield 2.5, []
+            lax.fori_loop(2, 4, one_head, 0)
             here = right_a.at[zs[k]]
             here[0:rows, 0:head_cols] = (head_grads[0] * score_scale).astype(bf16)
             here[0:rows, head_cols : 2 * head_cols] = (head_grads[1] * score_scale).astype(bf16)
@@ -1039,52 +1158,57 @@
             give_right("proj", 2, k, right_a.at[zs[k], pl.ds(0, rows)], right_a)
             saved.ensure(at + 2)
             attentions.ensure(at + 2)
-            yield 6.0, []
+            yield 2.5, []
             own = right_a[zs[k], 0:rows]
-            small_out[pl.ds(10 + zs[k], 1), :] = column_sums(own.astype(f32))
-            part = dot_turned(jnp.where(columns < 3 * head_cols, own, 0), w[...])
+            row_parts[zs[k], 7:8, :] = column_sums(own.astype(f32))
+            own = jnp.where(columns < 3 * head_cols, own, 0)
+            part = dot_turned(own[:, :qkv_end], w[:, :qkv_end])
             acc_buf[...] = part if at == 0 else acc_buf[...] + part
             weights.ensure(8 + at + 2)
+            yield 1.5, []
+        for k in FAR_FIRST:
             right_copies["proj", k].wait_recv()
-            yield 2.0, [], (units["down"], k)
+            yield 0.2, [], (units["down"], k)
             units["down"].settle((4 + k, 8 + k, 12 + k, 16 + k, 19 + k))
             weight_grad("proj", k, right_a, 3, 2)
             yield 2.0, [(units["proj"], k)]
-        unit, scale = unit_rows(x_in[...])
+        unit, scale = unit_rows(hid_slots[0])
         from_norm = norm_back(acc_buf[...], unit, scale, gains[0:1, :])
-        small_out[0:1, :] = column_sums(acc_buf[...] * unit)
-        small_out[2:3, :] = column_sums(acc_buf[...])
-        grad_out[...] = mid_grad[...] + from_norm
+        put_row(0, column_sums(acc_buf[...] * unit))
+        put_row(2, column_sums(acc_buf[...]))
+        grad_out[...] = grad_out[...] + from_norm
+        late_load(time_weight, s_slots.at[0, pl.ds(0, cut)], 6)
+        late_load(pick_in, s_slots.at[1, :, pl.ds(0, 4 * rows)], 7)
+        following = [(0.0, small_begin)]
         if not last_layer:
             low_buf[0] = grad_out[...].astype(bf16)
             line.begin(low_buf.at[0])
             keep.append(pltpu.make_async_copy(low_buf.at[0], rows_all.at[place.z], load_sem.at[4]))
             keep[0].start()
-        yield 2.0, []
-
-    def more_events():
-        if last_layer:
-            return [(20.0 * far_off, functools.partial(line.arrive, far_off)) for far_off in (1, 2, 3)]
-        return []
-
-    merge_steps(compute(), more_events(), 10.7, 9.0)
+            following += [(14.0 * far_off, functools.partial(line.arrive, far_off)) for far_off in (1, 2, 3)]
+        yield 2.0, [], None, following
+
+    first_events = []
+    if last_layer:
+        first_events = [(20.0 * far_off, functools.partial(line.arrive, far_off)) for far_off in (1, 2, 3)]
+    merge_steps(compute(), first_events, 10.7, 12.0)
+    for slot in range(6):
+        small[slot].wait_send()
     for (name, k), copy in right_copies.items():
         if name != "down":
             copy.wait_send()
     for at in (2, 3):
         for copy in left_copies[at]:
             copy.wait_send()
-    if not last_layer:
-        for far_off in (1, 2, 3):
-            line.arrive(far_off)
     line.finish()
     keep[0].wait()
     gathered = pltpu.make_async_copy(rows_all, right_b.at[:, pl.ds(0, rows)], load_sem.at[4])
     gathered.start()
     gathered.wait()
-    total = dot_plain(pick[:, 0:rows], right_b[0, 0:rows])
+    late_wait(7)
+    total = dot_plain(s_slots[1, :, 0:rows], right_b[0, 0:rows])
     for z in range(1, 4):
-        total = total + dot_plain(pick[:, z * rows : (z + 1) * rows], right_b[z, 0:rows])
+        total = total + dot_plain(s_slots[1, :, z * rows : (z + 1) * rows], right_b[z, 0:rows])
     rows_out[...] = total.astype(bf16)
 
 
@@ -1111,15 +1235,17 @@
             start = max(clock, link_free)
             link_free = start + links
             events.append((start + late, functools.partial(scatter_step, unit, k, late)))
-        if len(made) > 2:
+        if len(made) > 2 and made[2]:
             unit, k = made[2]
             while k not in unit.closed:
                 clock = run_first()
+        if len(made) > 3:
+            events += [(clock + delay, step) for delay, step in made[3]]
     while events:
         clock = run_first()
 
 
-def backward_layer(last_layer, grad, saved, gains, shifts, pick, rows_in, weights):
+def backward_layer(last_layer, grad, saved, gains, shifts, trow, pick, time_weight, rows_in, weights):
     x_in, mid_in, s_all, att_all, hid_all, act_all = saved
     proj, up, down = weights
     rows, d_model = grad.shape
@@ -1133,8 +1259,10 @@
         block,
         jax.ShapeDtypeStruct((rows, d_model), f32),
         jax.ShapeDtypeStruct((rows, d_model), bf16),
-        jax.ShapeDtypeStruct((16, d_model), f32),
-        jax.ShapeDtypeStruct((4, 4 * GRID, 512), f32),
+        jax.ShapeDtypeStruct((8, d_model), f32),
+        jax.ShapeDtypeStruct((4 * GRID, 512), f32),
+        jax.ShapeDtypeStruct((2, 2, 2, 16, d_model), bf16),
+        jax.ShapeDtypeStruct((2, 2, 2, 8, 8, cut), f32),
         jax.ShapeDtypeStruct((4, rows, d_model), bf16),
     ]
     dma = pltpu.SemaphoreType.DMA
@@ -1153,9 +1281,17 @@
         pltpu.VMEM((2, 4, rows, rows), f32),
         pltpu.VMEM((2, rows, d_model), f32),
         pltpu.VMEM((rows, d_model), f32),
-        pltpu.VMEM((rows, d_model), f32),
         pltpu.VMEM((2, rows, d_model), bf16),
         pltpu.VMEM((3, rows, d_model // 4), f32),
+        pltpu.VMEM((4, 8, d_model), f32),
+        pltpu.VMEM((3, 8, d_model), f32),
+        pltpu.VMEM((3, 8, d_model), f32),
+        pltpu.VMEM((4, 4 * GRID, 512), f32),
+        pltpu.VMEM((3, 4 * GRID, 512), f32),
+        pltpu.VMEM((3, 4 * GRID, 512), f32),
+        pltpu.VMEM((3, 8, 8, cut), f32),
+        dma((21,)),
+        dma((21,)),
         dma((3, SCATTER_SEMS)),
         dma((3, SCATTER_SEMS)),
         dma((4, 4)),
@@ -1166,20 +1302,23 @@
         dma((2,)),
         dma((2,)),
         dma((2,)),
-        dma((5,)),
+        dma((8,)),
         pltpu.SemaphoreType.REGULAR,
     ]
     return pl.pallas_call(
         functools.partial(backward_kernel, last_layer),
         out_shape=out_shape,
-        in_specs=[vmem] * 6 + [any_space] * 8,
-        out_specs=[vmem] * 7 + [any_space],
+        in_specs=[vmem] * 5 + [any_space] * 11,
+        out_specs=[vmem] * 9 + [any_space],
         scratch_shapes=scratch,
         compiler_params=pltpu.CompilerParams(
             collective_id=1 if last_layer else 2, has_side_effects=True, vmem_limit_bytes=63 * 2**20
         ),
         name="backward_last" if last_layer else "backward_first",
-    )(grad, x_in, mid_in, gains, shifts, pick, rows_in, s_all, att_all, hid_all, act_all, proj, up, down)
+    )(
+        grad, mid_in, gains, shifts, trow, x_in, pick, time_weight, rows_in, s_all, att_all, hid_all, act_all,
+        proj, up, down,
+    )
 
 
 def shards_plain(
@@ -1407,69 +1546,47 @@
     step_hot = (steps_all[:, None] == jnp.arange(time_table.shape[0], dtype=jnp.int32)[None, :]).astype(f32)
     time_slice = time_sel.reshape(8, 16, in_rows)[:, :image_count].reshape(-1, in_rows)
 
-    def layer_back(at, grad, rows_in):
-        return backward_layer(
-            at == layer_count - 1, grad, saved[at], norm_gain[at], norm_shift[at], pick_out, rows_in,
+    attn_grads, out_grads, mlp_grads = [], [], []
+    row_sums, table_sums, time_sums = [], [], []
+    block_output = None
+    trow = jnp.zeros((8, 8, in_rows), f32)
+    for at in reversed(range(layer_count)):
+        last_layer = at == layer_count - 1
+        packed, up_part, down_part, gradient, moved, rows_part, tables_part, times_part, trow, _ = backward_layer(
+            last_layer, gradient, saved[at], norm_gain[at], norm_shift[at], trow, pick_out, time_packed[at], block_low,
             wholes[3 * at : 3 * at + 3],
         )
-
-    attn_grads, out_grads, mlp_grads = [], [], []
-    time_sums, small = [], []
-    block_output = None
-    for at in reversed(range(layer_count)):
-        packed, up_part, down_part, gradient, moved, sums, windows, _ = layer_back(at, gradient, block_low)
-        if at == layer_count - 1:
+        if last_layer:
             block_output = moved
+            trow = lax.dynamic_index_in_dim(trow.reshape(8, 8, 8, in_rows), wide_at, axis=0, keepdims=False)
         mlp_grads.insert(0, jnp.stack([up_part, down_part]))
         attn_grads.insert(0, jnp.stack([packed[:, j * cols : (j + 1) * cols] for j in range(3)]))
         out_grads.insert(0, packed[:, 3 * cols :])
-        qkv_sums = jnp.stack([sums[10:14, j * cols : (j + 1) * cols].reshape(-1) for j in range(3)])
-        time_sums.insert(0, qkv_sums)
-        small.insert(
-            0,
-            (
-                sums[0:2],
-                sums[2:4],
-                sums[4:6],
-                jnp.stack([qkv_sums[0], qkv_sums[2]]),
-                sums[6:10].reshape(-1),
-                windows.reshape(-1, 512),
-            ),
-        )
+        row_sums.insert(0, rows_part)
+        table_sums.insert(0, tables_part)
+        time_sums.insert(0, times_part.reshape(8, 16, d_model)[:, :image_count].reshape(-1, d_model))
     input_grad = moved
-
-    def stacked(index_at):
-        return jnp.stack([entry[index_at] for entry in small])
-
-    tables = fold_windows(stacked(5))
-    totals = lax.psum(tuple(stacked(index_at) for index_at in range(5)) + (tables,), ("wide", "narrow"))
-
-    def own_part(array, axis):
-        size = array.shape[axis] // lax.axis_size("narrow")
-        return lax.dynamic_slice_in_dim(array, narrow_at * size, size, axis=axis)
-
-    time_low = jnp.stack(time_sums).astype(bf16)
-    time_every = lax.all_gather(time_low, ("wide", "narrow"), axis=0, tiled=False)
-    time_part = own_part(time_every, 3)
-    time_weight_grad = jnp.einsum("id,iljc->ljdc", time_slice, time_part, preferred_element_type=f32)
-    trow_share = jnp.einsum("iljc,ljdc->id", time_part, time_weight, preferred_element_type=f32)
-    trow_share = lax.psum(trow_share, "narrow")
-    trow = lax.all_gather(trow_share, "wide", axis=1, tiled=True)
+    row_sums = jnp.stack(row_sums)
+    table_grad = fold_windows(jnp.stack(table_sums))
+    time_weight_grad = jnp.einsum("id,lic->ldc", time_slice, jnp.stack(time_sums), preferred_element_type=f32)
+    time_weight_grad = jnp.stack([time_weight_grad[:, :, j * cols : (j + 1) * cols] for j in range(3)], axis=1)
+    trow = trow.reshape(8, 8, 8, in_rows)[:, :, :image_count].transpose(1, 2, 0, 3).reshape(-1, d_model)
     time_grad = jnp.einsum("is,id->sd", step_hot, trow, precision=highest)
     attn_grad = jnp.concatenate([jnp.stack(attn_grads), time_weight_grad], axis=1)
+    qkv_bias_grad = jnp.stack([row_sums[:, 7, :cols], row_sums[:, 7, 2 * cols : 3 * cols]], axis=1)
     return (
         block_output,
         input_grad,
         time_grad,
-        totals[0],
-        totals[1],
+        row_sums[:, 0:2],
+        row_sums[:, 2:4],
         attn_grad,
         jnp.stack(out_grads),
-        own_part(totals[3], 2),
-        totals[2],
+        qkv_bias_grad,
+        row_sums[:, 4:6],
         jnp.stack(mlp_grads),
-        own_part(totals[4], 1),
-        own_part(totals[5], 1),
+        row_sums[:, 6],
+        table_grad,
     )
 
 

time: 1030 us -> 783 us (0.76)
  waiting for transfers between devices: 120 us -> 0 us
  blocking collectives: 92.7 us -> 0 us
  local copies, waits for them, and re-layouts: 43.7 us -> 26.9 us
  between operations: 15 us -> 1.2 us
    psum x2 -> x0, waiting for transfers between devices: 120 us -> none  [shards(): lax.psum(tuple((stacked(index_at) for index_at in range(5))) + (tables,),...]
    all_gather x2 -> x0, blocking collectives: 76.4 us -> none  [the longest x1 68.6 us: shards(): lax.all_gather(time_low, ('wide', 'narrow'), axis=0, tiled=False)]
    psum x1 -> x0, blocking collectives: 16.2 us -> none  [shards(): trow_share = lax.psum(trow_share, 'narrow')]
  transfers between devices with their start and end apart: 2 -> 0, of which waited for: 1 -> 0; matrix products, arithmetic and copies ran while one was open for 4% -> 0% of each run, Pallas kernels for 0% -> 0%
where the time goes in v3:
time: 783 us; the launch traced here: 773 us
  Pallas kernels  722 us (92%)
  local copies, waits for them, and re-layouts  26.9 us (3%)
  other arithmetic  12.9 us (2%)
  matrix products  9.64 us (1%)
    pallas_call x2, Pallas kernels, backward_layer(): pl.pallas_call(functools.partial(backward_kernel, last_layer), out_shape=...  379 us
    pallas_call x1, Pallas kernels, forward_all(): pl.pallas_call(functools.partial(forward_kernel, layers), out_shape=out_s...  343 us

profile of v3, /device:TPU:0, one launch (start us, length us, event | category | flops | bytes accessed | tf_op | source)
XLA Modules:
  0.0 772.6 jit_solution(17780513810260566157)
XLA Ops:
  2.2 0.8 fusion.32
  3.1 2.2 convolution_convert_fusion
  9.4 0.9 compare_convert_fusion.refs_2_
  10.4 0.9 fusion.refs_6_
  11.4 1.0 concatenate.26.refs_13_
  12.3 0.9 concatenate.25.refs_10_
  14.0 1.0 slice_bitcast_fusion.3
  15.0 1.6 convolution_bitcast_fusion.1
  16.6 2.1 copy.40
  18.7 1.5 reshape.108
  20.9 2.4 slice_bitcast_fusion.5
  23.3 343.0 %forward_all.1 = (bf16[4,1152,1152]{2,1,0:T(8,128)(2,1)}, bf16[4,1152,1152]{2,1,0:T(8,128)(2,1)}, bf16[4,1152,1152]{2,1,0:T(8,128)(2,1)}, bf16[4,1152,1152]{2,1,...) custom-call(bf16[256,1152]{1,0:T(8,128)(2,1)} %refs_0_.1, ...), custom_call_target="tpu_custom_call" | custom-call | tf_op jit(solution)/shard_map/forward_all/pallas_call | solution.py:742
  366.9 174.2 %backward_last.1 = (f32[144,1152]{1,0:T(8,128)}, f32[144,1152]{1,0:T(8,128)}, f32[144,1152]{1,0:T(8,128)}, f32[256,1152]{1,0:T(8,128)}, bf16[256,1152]{1,0:T(8,1...) custom-call(f32[256,1152]{1,0:T(8,128)} %get-tuple-element.51.refs_0, ...), custom_call_target="tpu_custom_call" | custom-call | tf_op jit(solution)/shard_map/backward_last/pallas_call | solution.py:1308
  541.9 0.8 slice.208
  542.7 1.5 dynamic-slice_bitcast_fusion.refs_4_
  544.2 204.8 %backward_first.1 = (f32[144,1152]{1,0:T(8,128)}, f32[144,1152]{1,0:T(8,128)}, f32[144,1152]{1,0:T(8,128)}, f32[256,1152]{1,0:T(8,128)}, bf16[256,1152]{1,0:T(8,...) custom-call(f32[256,1152]{1,0:T(8,128)} %get-tuple-element.63.refs_0, ...), custom_call_target="tpu_custom_call" | custom-call | tf_op jit(solution)/shard_map/backward_first/pallas_call | solution.py:1308
  749.1 1.2 slice.201
  750.5 0.9 fusion.27
  752.0 0.8 pad_maximum_fusion.5
  752.8 1.5 fusion.19
  754.9 0.9 slice.206
  755.9 0.9 slice.207
  757.4 0.8 pad_maximum_fusion.2
  759.0 1.7 pad_maximum_fusion
  760.8 1.0 copy-done.4
  762.1 1.7 pad_maximum_fusion.1
  763.8 0.8 reshape.120
  764.5 1.0 convolution_bitcast_fusion.2
  765.6 0.7 reshape.121
  766.4 4.4 fusion.9
  770.8 0.8 copy.69
  771.6 0.8 copy.70
  (82 shorter events, 11.9 us)
Async XLA Ops:
  0.6 6.0 copy-start.15
  0.7 5.4 copy-start.14
  0.7 8.5 %copy-start.16 = (f32[2,4,961]{2,1,0:T(4,128)S(1)}, f32[2,4,961]{2,1,0:T(4,128)}, u32[]{:S(2)}) copy-start(f32[2,4,961]{2,1,0:T(4,128)} %param.29) | copy-start | bytes 92260
  0.7 6.6 copy-start.18
  0.7 4.7 copy-start.17
  0.7 8.7 %copy-start.11 = (bf16[2,144,288]{2,1,0:T(8,128)(2,1)S(1)}, bf16[2,144,288]{2,1,0:T(8,128)(2,1)}, u32[]{:S(2)}) copy-start(bf16[2,144,288]{2,1,0:T(8,128)(2,1)} %param.24) | copy-start | bytes 497668
  3.1 8.2 %copy-start.1 = (bf16[2,6,144,288]{3,2,1,0:T(8,128)(2,1)S(1)}, bf16[2,6,144,288]{3,2,1,0:T(8,128)(2,1)}, u32[]{:S(2)}) copy-start(bf16[2,6,144,288]{3,2,1,0:T(8,128)(2,1)} %param.23) | copy-start | bytes 2985988
  14.0 4.7 copy-start
  544.2 206.4 %copy-start.10 = (f32[8,1152]{1,0:T(8,128)S(1)}, f32[8,1152]{1,0:T(8,128)}, u32[]{:S(2)}) copy-start(f32[8,1152]{1,0:T(8,128)} %get-tuple-element.78) | copy-start | bytes 110596
  749.0 7.8 %copy-start.12 = (f32[64,512]{1,0:T(8,128)S(1)}, f32[64,512]{1,0:T(8,128)}, u32[]{:S(2)}) copy-start(f32[64,512]{1,0:T(8,128)} %get-tuple-element.89) | copy-start | bytes 393220
  749.0 7.8 %copy-start.13 = (f32[64,512]{1,0:T(8,128)S(1)}, f32[64,512]{1,0:T(8,128)}, u32[]{:S(2)}) copy-start(f32[64,512]{1,0:T(8,128)} %get-tuple-element.88) | copy-start | bytes 393220
  749.0 7.9 %copy-start.3 = (f32[144,1152]{1,0:T(8,128)S(1)}, f32[144,1152]{1,0:T(8,128)}, u32[]{:S(2)}) copy-start(f32[144,1152]{1,0:T(8,128)} %get-tuple-element.79) | copy-start | bytes 1990660
  750.5 6.7 copy-start.2
  759.0 1.8 copy-start.6
  759.0 1.7 copy-start.7
  760.7 1.1 copy-start.4
  760.7 1.3 copy-start.5
  766.4 4.4 copy-start.8
  766.4 5.2 copy-start.9

commit v4 on v3

--- a/solution.py
+++ b/solution.py
@@ -252,7 +252,7 @@
 
 LINE_SEMS = 5
 Z_AHEAD = 43.0
-UNIT_TIME = 43.0
+UNIT_TIME = 46.0
 GATHER_SEMS = 58
 Y_FIRST, X_LAST, X_NEAR, X_FAR, Y_NEAR, Y_FAR = 5, 9, 13, 17, 21, 25
 C_OWN, C_Y, C_X, C_X_NEAR, C_Y_NEAR, C_X_FAR, C_Y_FAR = 29, 33, 37, 41, 45, 49, 53
@@ -442,7 +442,11 @@
         return out
 
     (tokens, cot, pick, time_own, time_weight, windows_own, small_own, gains, shifts, out_bias) = take(10)
-    pieces = take(units)
+    packed = take(layers)
+    (mlp_weight,) = take(1)
+    pieces = []
+    for layer in range(layers):
+        pieces += [packed[layer], mlp_weight.at[layer, 0], mlp_weight.at[layer, 1]]
     wholes = take(units)
     saved = [take(LAYER_SAVED) for _ in range(layers)]
     block_out, grad_out, time_out, time_sel_out = take(4)
@@ -682,11 +686,13 @@
         wanted = next(compute, None)
 
 
-def forward_all(tokens, cot, pick, time_own, time_weight, windows_own, small_own, gains, shifts, out_bias, pieces):
-    layers = len(pieces) // 3
-    units = len(pieces)
+def forward_all(
+    tokens, cot, pick, time_own, time_weight, windows_own, small_own, gains, shifts, out_bias, packed, mlp_weight
+):
+    layers = len(packed)
+    units = 3 * layers
     rows, d_model = tokens.shape
-    piece_rows = pieces[0].shape[0]
+    piece_rows = packed[0].shape[0]
     any_space = pl.BlockSpec(memory_space=pl.ANY)
     vmem = pl.BlockSpec(memory_space=pltpu.VMEM)
     layer_shapes = [
@@ -742,14 +748,14 @@
     out = pl.pallas_call(
         functools.partial(forward_kernel, layers),
         out_shape=out_shape,
-        in_specs=[any_space] * 2 + [vmem] * 8 + [any_space] * units,
+        in_specs=[any_space] * 2 + [vmem] * 8 + [any_space] * (layers + 1),
         out_specs=[any_space] * (units + LAYER_SAVED * layers) + [vmem] * 4,
         scratch_shapes=scratch,
         compiler_params=pltpu.CompilerParams(
             collective_id=0, has_side_effects=True, vmem_limit_bytes=60 * 2**20
         ),
         name="forward_all",
-    )(tokens, cot, pick, time_own, time_weight, windows_own, small_own, gains, shifts, out_bias, *pieces)
+    )(tokens, cot, pick, time_own, time_weight, windows_own, small_own, gains, shifts, out_bias, *packed, mlp_weight)
     wholes = out[:units]
     saved = [out[units + LAYER_SAVED * at : units + LAYER_SAVED * (at + 1)] for at in range(layers)]
     return wholes, saved, out[units + LAYER_SAVED * layers :]
@@ -880,7 +886,7 @@
     (
         total_a, total_b, far, near, from_z, right_a, right_b, left, turned,
         w_slots, s_slots, att_slots, hid_slots, acc_buf, low_buf, head_grads,
-        row_parts, rows_z, rows_w, table_parts, table_z, table_w, trow_z, small_send, small_recv,
+        row_parts, rows_z, rows_w, table_parts, table_low, table_z, table_w, trow_z, trow_kept, small_send, small_recv,
         send, recv, left_send, left_recv, line_send, line_recv, w_sem, s_sem, att_sem, hid_sem, load_sem, credit,
     ) = refs
     place = Place()
@@ -999,10 +1005,11 @@
         small[slot] = remote(src, dst, small_send.at[slot], small_recv.at[slot], peer)
 
     def small_begin():
+        table_low[...] = table_parts[...].astype(bf16)
         for k in (1, 2, 3):
             peer = (place.wide(), zs[k])
             give(k - 1, row_parts.at[zs[k]], rows_z.at[k - 1], peer)
-            give(k + 2, table_parts.at[zs[k]], table_z.at[k - 1], peer)
+            give(k + 2, table_low.at[zs[k]], table_z.at[k - 1], peer)
         return ((9.0, small_along_z),)
 
     def small_along_z():
@@ -1016,7 +1023,7 @@
             part = rows_z[k - 1]
             times = jnp.where(at_row == place.along_z(4 - k), part[7:8, :], times)
             totals = totals + part
-            tables = tables + table_z[k - 1]
+            tables = tables + table_z[k - 1].astype(f32)
         row_sums[...] = totals
         table_sums[...] = tables
         time_sums[place.y, place.x, place.c] = times.astype(bf16)
@@ -1026,7 +1033,8 @@
     def small_across(axis):
         peer, slot = axes[axis]
         give(slot, row_sums, rows_w.at[axis], peer)
-        give(slot + 1, table_sums, table_w.at[axis], peer)
+        table_low[place.z] = table_sums[...].astype(bf16)
+        give(slot + 1, table_low.at[place.z], table_w.at[axis], peer)
         give(slot + 2, own_time[axis], own_time[axis], peer)
 
     def small_step(axis):
@@ -1035,14 +1043,15 @@
             small[at].wait_recv()
             small[at].wait_send()
         row_sums[...] = row_sums[...] + rows_w[axis]
-        table_sums[...] = table_sums[...] + table_w[axis]
+        table_sums[...] = table_low[place.z].astype(f32) + table_w[axis].astype(f32)
         if axis < 2:
             small_across(axis + 1)
             return ((5.0, functools.partial(small_step, axis + 1)),)
         late_wait(6)
         times = jnp.where(columns < 3 * head_cols, time_sums[...].reshape(128, d_model), 0)
         part = dot_turned(times, s_slots[0, 0:cut]).reshape(8, 16, cut)[:, :8]
-        part = part + trow_in[...]
+        late_wait(8)
+        part = part + trow_kept[...]
         trow_out[place.y, place.x, place.c] = part
         if last_layer:
             return None
@@ -1065,6 +1074,24 @@
         if axis < 2:
             give(19 + axis, own_trow[axis + 1], own_trow[axis + 1], axes[axis + 1][0])
             return ((5.0, functools.partial(trow_step, axis + 1)),)
+
+    def close_rows():
+        unit, scale = unit_rows(hid_slots[0])
+        from_norm = norm_back(acc_buf[...], unit, scale, gains[0:1, :])
+        put_row(0, column_sums(acc_buf[...] * unit))
+        put_row(2, column_sums(acc_buf[...]))
+        grad_out[...] = grad_out[...] + from_norm
+        late_load(time_weight, s_slots.at[0, pl.ds(0, cut)], 6)
+        late_load(trow_in.at[place.y, place.x, place.c], trow_kept, 8)
+        late_load(pick_in, s_slots.at[1, :, pl.ds(0, 4 * rows)], 7)
+        following = [(0.0, small_begin)]
+        if not last_layer:
+            low_buf[0] = grad_out[...].astype(bf16)
+            line.begin(low_buf.at[0])
+            keep.append(pltpu.make_async_copy(low_buf.at[0], rows_all.at[place.z], load_sem.at[4]))
+            keep[0].start()
+            following += [(14.0 * far_off, functools.partial(line.arrive, far_off)) for far_off in (1, 2, 3)]
+        return following
 
     def compute():
         low_buf[0] = grad[...].astype(bf16)
@@ -1166,32 +1193,18 @@
             acc_buf[...] = part if at == 0 else acc_buf[...] + part
             weights.ensure(8 + at + 2)
             yield 1.5, []
+        yield 2.0, [], None, close_rows()
         for k in FAR_FIRST:
             right_copies["proj", k].wait_recv()
             yield 0.2, [], (units["down"], k)
             units["down"].settle((4 + k, 8 + k, 12 + k, 16 + k, 19 + k))
             weight_grad("proj", k, right_a, 3, 2)
             yield 2.0, [(units["proj"], k)]
-        unit, scale = unit_rows(hid_slots[0])
-        from_norm = norm_back(acc_buf[...], unit, scale, gains[0:1, :])
-        put_row(0, column_sums(acc_buf[...] * unit))
-        put_row(2, column_sums(acc_buf[...]))
-        grad_out[...] = grad_out[...] + from_norm
-        late_load(time_weight, s_slots.at[0, pl.ds(0, cut)], 6)
-        late_load(pick_in, s_slots.at[1, :, pl.ds(0, 4 * rows)], 7)
-        following = [(0.0, small_begin)]
-        if not last_layer:
-            low_buf[0] = grad_out[...].astype(bf16)
-            line.begin(low_buf.at[0])
-            keep.append(pltpu.make_async_copy(low_buf.at[0], rows_all.at[place.z], load_sem.at[4]))
-            keep[0].start()
-            following += [(14.0 * far_off, functools.partial(line.arrive, far_off)) for far_off in (1, 2, 3)]
-        yield 2.0, [], None, following
 
     first_events = []
     if last_layer:
         first_events = [(20.0 * far_off, functools.partial(line.arrive, far_off)) for far_off in (1, 2, 3)]
-    merge_steps(compute(), first_events, 10.7, 12.0)
+    merge_steps(compute(), first_events, 10.7, 12.0 if last_layer else 12.0, 12.0)
     for slot in range(6):
         small[slot].wait_send()
     for (name, k), copy in right_copies.items():
@@ -1212,7 +1225,7 @@
     rows_out[...] = total.astype(bf16)
 
 
-def merge_steps(compute, events, links, late):
+def merge_steps(compute, events, links, late, follow):
     clock, link_free = 0.0, 0.0
     events = list(events)
 
@@ -1234,7 +1247,7 @@
             unit.first_stage(k)
             start = max(clock, link_free)
             link_free = start + links
-            events.append((start + late, functools.partial(scatter_step, unit, k, late)))
+            events.append((start + late, functools.partial(scatter_step, unit, k, follow)))
         if len(made) > 2 and made[2]:
             unit, k = made[2]
             while k not in unit.closed:
@@ -1287,9 +1300,11 @@
         pltpu.VMEM((3, 8, d_model), f32),
         pltpu.VMEM((3, 8, d_model), f32),
         pltpu.VMEM((4, 4 * GRID, 512), f32),
-        pltpu.VMEM((3, 4 * GRID, 512), f32),
-        pltpu.VMEM((3, 4 * GRID, 512), f32),
+        pltpu.VMEM((4, 4 * GRID, 512), bf16),
+        pltpu.VMEM((3, 4 * GRID, 512), bf16),
+        pltpu.VMEM((3, 4 * GRID, 512), bf16),
         pltpu.VMEM((3, 8, 8, cut), f32),
+        pltpu.VMEM((8, 8, cut), f32),
         dma((21,)),
         dma((21,)),
         dma((3, SCATTER_SEMS)),
@@ -1302,13 +1317,13 @@
         dma((2,)),
         dma((2,)),
         dma((2,)),
-        dma((8,)),
+        dma((9,)),
         pltpu.SemaphoreType.REGULAR,
     ]
     return pl.pallas_call(
         functools.partial(backward_kernel, last_layer),
         out_shape=out_shape,
-        in_specs=[vmem] * 5 + [any_space] * 11,
+        in_specs=[vmem] * 4 + [any_space] * 12,
         out_specs=[vmem] * 9 + [any_space],
         scratch_shapes=scratch,
         compiler_params=pltpu.CompilerParams(
@@ -1523,10 +1538,10 @@
         [qkv_bias[:, 0], jnp.zeros_like(qkv_bias[:, 0]), qkv_bias[:, 1], jnp.zeros_like(qkv_bias[:, 0])], axis=1
     )
     small_own = jnp.pad(jnp.concatenate([up_bias, qkv_packed], axis=0), ((0, 8 - 2 * layer_count), (0, 0)))
-    pieces = []
-    for at in range(layer_count):
-        packed = jnp.concatenate([attn_weight[at, 0], attn_weight[at, 1], attn_weight[at, 2], out_weight[at]], axis=1)
-        pieces += [packed, mlp_weight[at, 0], mlp_weight[at, 1]]
+    packed_own = [
+        jnp.concatenate([attn_weight[at, 0], attn_weight[at, 1], attn_weight[at, 2], out_weight[at]], axis=1)
+        for at in range(layer_count)
+    ]
     wholes, saved, (block_low, gradient, time_all, time_sel) = forward_all(
         tokens,
         cotangent,
@@ -1538,7 +1553,8 @@
         norm_gain.reshape(-1, d_model),
         norm_shift.reshape(-1, d_model),
         out_bias.reshape(-1, d_model),
-        pieces,
+        packed_own,
+        mlp_weight,
     )
     time_all = time_all.reshape(8, 16, d_model)
     steps_all = time_all[:, image_count : image_count + 2, :image_count].astype(f32)
@@ -1549,7 +1565,7 @@
     attn_grads, out_grads, mlp_grads = [], [], []
     row_sums, table_sums, time_sums = [], [], []
     block_output = None
-    trow = jnp.zeros((8, 8, in_rows), f32)
+    trow = jnp.zeros((2, 2, 2, 8, 8, in_rows), f32)
     for at in reversed(range(layer_count)):
         last_layer = at == layer_count - 1
         packed, up_part, down_part, gradient, moved, rows_part, tables_part, times_part, trow, _ = backward_layer(
@@ -1558,7 +1574,6 @@
         )
         if last_layer:
             block_output = moved
-            trow = lax.dynamic_index_in_dim(trow.reshape(8, 8, 8, in_rows), wide_at, axis=0, keepdims=False)
         mlp_grads.insert(0, jnp.stack([up_part, down_part]))
         attn_grads.insert(0, jnp.stack([packed[:, j * cols : (j + 1) * cols] for j in range(3)]))
         out_grads.insert(0, packed[:, 3 * cols :])

time: 783 us -> 764 us (0.976)
  Pallas kernels: 722 us -> 707 us
    pallas_call x2, Pallas kernels: 379 us -> 359 us  [backward_layer(): pl.pallas_call(functools.partial(backward_kernel, last_layer), out_shape=...]
where the time goes in v4:
time: 764 us; the launch traced here: 754 us
  Pallas kernels  707 us (93%)
  local copies, waits for them, and re-layouts  23.3 us (3%)
  other arithmetic  12.9 us (2%)
  matrix products  9.64 us (1%)
    pallas_call x2, Pallas kernels, backward_layer(): pl.pallas_call(functools.partial(backward_kernel, last_layer), out_shape=...  359 us
    pallas_call x1, Pallas kernels, forward_all(): pl.pallas_call(functools.partial(forward_kernel, layers), out_shape=out_s...  348 us

profile of v4, /device:TPU:0, one launch (start us, length us, event | category | flops | bytes accessed | tf_op | source)
XLA Modules:
  0.0 753.6 jit_solution(12103255317012672835)
XLA Ops:
  0.7 0.7 convert_bitcast_fusion
  2.2 0.8 fusion.32
  3.2 2.2 convolution_convert_fusion
  9.4 0.9 compare_convert_fusion.refs_2_
  10.4 0.9 fusion.refs_6_
  11.4 1.0 concatenate.26.refs_11_
  12.4 0.9 concatenate.25.refs_10_
  14.0 1.0 slice_bitcast_fusion.3
  15.0 1.6 convolution_bitcast_fusion.1
  16.6 2.1 copy.40
  18.7 1.5 reshape.105
  21.0 347.7 %forward_all.1 = (bf16[4,1152,1152]{2,1,0:T(8,128)(2,1)}, bf16[4,1152,1152]{2,1,0:T(8,128)(2,1)}, bf16[4,1152,1152]{2,1,0:T(8,128)(2,1)}, bf16[4,1152,1152]{2,1,...) custom-call(bf16[256,1152]{1,0:T(8,128)(2,1)} %refs_0_.1, ...), custom_call_target="tpu_custom_call" | custom-call | tf_op jit(solution)/shard_map/forward_all/pallas_call | solution.py:748
  368.7 0.8 broadcast_in_dim.5.refs_4_
  369.5 166.3 %backward_last.1 = (f32[144,1152]{1,0:T(8,128)}, f32[144,1152]{1,0:T(8,128)}, f32[144,1152]{1,0:T(8,128)}, f32[256,1152]{1,0:T(8,128)}, bf16[256,1152]{1,0:T(8,1...) custom-call(f32[256,1152]{1,0:T(8,128)} %get-tuple-element.51.refs_0, ...), custom_call_target="tpu_custom_call" | custom-call | tf_op jit(solution)/shard_map/backward_last/pallas_call | solution.py:1323
  535.9 192.5 %backward_first.1 = (f32[144,1152]{1,0:T(8,128)}, f32[144,1152]{1,0:T(8,128)}, f32[144,1152]{1,0:T(8,128)}, f32[256,1152]{1,0:T(8,128)}, bf16[256,1152]{1,0:T(8,...) custom-call(f32[256,1152]{1,0:T(8,128)} %get-tuple-element.63.refs_0, ...), custom_call_target="tpu_custom_call" | custom-call | tf_op jit(solution)/shard_map/backward_first/pallas_call | solution.py:1323
  728.4 1.2 slice.185
  730.7 0.9 fusion.27
  732.2 0.8 pad_maximum_fusion.5
  733.0 1.5 fusion.19
  735.1 0.8 slice.192
  735.9 0.9 slice.190
  736.9 0.9 slice.191
  738.4 0.8 pad_maximum_fusion.2
  740.0 1.7 pad_maximum_fusion
  741.8 1.0 copy-done.4
  743.1 1.7 pad_maximum_fusion.1
  744.8 0.8 reshape.116
  745.5 1.0 convolution_bitcast_fusion.2
  746.6 0.7 reshape.117
  747.4 4.4 fusion.9
  751.8 0.8 copy.69
  752.6 0.8 copy.70
  (80 shorter events, 10.5 us)
Async XLA Ops:
  0.6 6.0 copy-start.15
  0.7 5.4 copy-start.14
  0.7 8.5 %copy-start.16 = (f32[2,4,961]{2,1,0:T(4,128)S(1)}, f32[2,4,961]{2,1,0:T(4,128)}, u32[]{:S(2)}) copy-start(f32[2,4,961]{2,1,0:T(4,128)} %param.29) | copy-start | bytes 92260
  0.7 6.6 copy-start.18
  0.7 4.7 copy-start.17
  0.7 8.7 %copy-start.11 = (bf16[2,144,288]{2,1,0:T(8,128)(2,1)S(1)}, bf16[2,144,288]{2,1,0:T(8,128)(2,1)}, u32[]{:S(2)}) copy-start(bf16[2,144,288]{2,1,0:T(8,128)(2,1)} %param.24) | copy-start | bytes 497668
  3.2 8.2 %copy-start.1 = (bf16[2,6,144,288]{3,2,1,0:T(8,128)(2,1)S(1)}, bf16[2,6,144,288]{3,2,1,0:T(8,128)(2,1)}, u32[]{:S(2)}) copy-start(bf16[2,6,144,288]{3,2,1,0:T(8,128)(2,1)} %param.23) | copy-start | bytes 2985988
  14.0 4.7 copy-start
  535.9 194.9 %copy-start.10 = (f32[8,1152]{1,0:T(8,128)S(1)}, f32[8,1152]{1,0:T(8,128)}, u32[]{:S(2)}) copy-start(f32[8,1152]{1,0:T(8,128)} %get-tuple-element.78) | copy-start | bytes 110596
  728.4 9.4 %copy-start.12 = (f32[64,512]{1,0:T(8,128)S(1)}, f32[64,512]{1,0:T(8,128)}, u32[]{:S(2)}) copy-start(f32[64,512]{1,0:T(8,128)} %get-tuple-element.89) | copy-start | bytes 393220
  728.4 9.4 %copy-start.13 = (f32[64,512]{1,0:T(8,128)S(1)}, f32[64,512]{1,0:T(8,128)}, u32[]{:S(2)}) copy-start(f32[64,512]{1,0:T(8,128)} %get-tuple-element.88) | copy-start | bytes 393220
  728.4 9.5 %copy-start.3 = (f32[144,1152]{1,0:T(8,128)S(1)}, f32[144,1152]{1,0:T(8,128)}, u32[]{:S(2)}) copy-start(f32[144,1152]{1,0:T(8,128)} %get-tuple-element.79) | copy-start | bytes 1990660
  730.7 7.5 copy-start.2
  740.0 1.8 copy-start.6
  740.0 1.7 copy-start.7
  741.7 1.1 copy-start.4
  741.7 1.3 copy-start.5
  747.4 4.4 copy-start.8
  747.4 5.2 copy-start.9

commit v5 on v4

--- a/solution.py
+++ b/solution.py
@@ -655,6 +655,12 @@
                 save(10 + slot, hid_buf.at[slot], hid_save.at[z])
                 act_buf[z] = gelu(hid_buf[slot]).astype(bf16)
             save(7, act_buf, act_save)
+            if layer == layers - 1:
+                yield 3 * layer + 1, 1.5
+                total = dot_plain(pick[:, 0:tokens_n], cot_all[0])
+                for z in range(1, 4):
+                    total = total + dot_plain(pick[:, z * tokens_n : (z + 1) * tokens_n], cot_all[z])
+                grad_out[...] = total
             for z in range(4):
                 yield 3 * layer + 2, 1.8
                 w = weights(3 * layer + 2, z)
@@ -662,10 +668,6 @@
                 acc_buf[...] = branch if z == 0 else acc_buf[...] + branch
             x_buf[...] = mid_buf[...] + (acc_buf[...] + out_bias[row + 1 : row + 2, :])
         block_out[...] = x_buf[...].astype(bf16)
-        total = dot_plain(pick[:, 0:tokens_n], cot_all[0])
-        for z in range(1, 4):
-            total = total + dot_plain(pick[:, z * tokens_n : (z + 1) * tokens_n], cot_all[z])
-        grad_out[...] = total
         for slot in list(pending):
             settle(slot)
 

time: 764 us -> 763 us (level)
  no operation moved by 1% of the time
where the time goes in v5:
time: 763 us; the launch traced here: 753 us
  Pallas kernels  706 us (93%)
  local copies, waits for them, and re-layouts  23.3 us (3%)
  other arithmetic  12.9 us (2%)
  matrix products  9.64 us (1%)
    pallas_call x2, Pallas kernels, backward_layer(): pl.pallas_call(functools.partial(backward_kernel, last_layer), out_shape=...  359 us
    pallas_call x1, Pallas kernels, forward_all(): pl.pallas_call(functools.partial(forward_kernel, layers), out_shape=out_s...  347 us

profile of v5, /device:TPU:0, one launch (start us, length us, event | category | flops | bytes accessed | tf_op | source)
XLA Modules:
  0.0 753.1 jit_solution(4546323728148591450)
XLA Ops:
  0.7 0.7 convert_bitcast_fusion
  2.2 0.8 fusion.32
  3.2 2.2 convolution_convert_fusion
  9.4 0.9 compare_convert_fusion.refs_2_
  10.4 0.9 fusion.refs_6_
  11.4 1.0 concatenate.26.refs_11_
  12.4 0.9 concatenate.25.refs_10_
  14.0 1.0 slice_bitcast_fusion.3
  15.0 1.6 convolution_bitcast_fusion.1
  16.6 2.1 copy.40
  18.7 1.5 reshape.105
  21.0 347.1 %forward_all.1 = (bf16[4,1152,1152]{2,1,0:T(8,128)(2,1)}, bf16[4,1152,1152]{2,1,0:T(8,128)(2,1)}, bf16[4,1152,1152]{2,1,0:T(8,128)(2,1)}, bf16[4,1152,1152]{2,1,...) custom-call(bf16[256,1152]{1,0:T(8,128)(2,1)} %refs_0_.1, ...), custom_call_target="tpu_custom_call" | custom-call | tf_op jit(solution)/shard_map/forward_all/pallas_call | solution.py:750
  368.1 0.8 broadcast_in_dim.5.refs_4_
  368.9 166.3 %backward_last.1 = (f32[144,1152]{1,0:T(8,128)}, f32[144,1152]{1,0:T(8,128)}, f32[144,1152]{1,0:T(8,128)}, f32[256,1152]{1,0:T(8,128)}, bf16[256,1152]{1,0:T(8,1...) custom-call(f32[256,1152]{1,0:T(8,128)} %get-tuple-element.51.refs_0, ...), custom_call_target="tpu_custom_call" | custom-call | tf_op jit(solution)/shard_map/backward_last/pallas_call | solution.py:1325
  535.2 192.7 %backward_first.1 = (f32[144,1152]{1,0:T(8,128)}, f32[144,1152]{1,0:T(8,128)}, f32[144,1152]{1,0:T(8,128)}, f32[256,1152]{1,0:T(8,128)}, bf16[256,1152]{1,0:T(8,...) custom-call(f32[256,1152]{1,0:T(8,128)} %get-tuple-element.63.refs_0, ...), custom_call_target="tpu_custom_call" | custom-call | tf_op jit(solution)/shard_map/backward_first/pallas_call | solution.py:1325
  728.0 1.2 slice.185
  730.3 0.9 fusion.27
  731.7 0.8 pad_maximum_fusion.5
  732.5 1.5 fusion.19
  734.6 0.8 slice.192
  735.4 0.9 slice.190
  736.4 0.9 slice.191
  738.0 0.8 pad_maximum_fusion.2
  739.5 1.7 pad_maximum_fusion
  741.3 1.0 copy-done.4
  742.6 1.7 pad_maximum_fusion.1
  744.3 0.8 reshape.116
  745.0 1.0 convolution_bitcast_fusion.2
  746.1 0.7 reshape.117
  746.9 4.4 fusion.9
  751.3 0.8 copy.69
  752.1 0.8 copy.70
  (80 shorter events, 10.5 us)
Async XLA Ops:
  0.6 6.0 copy-start.15
  0.7 5.4 copy-start.14
  0.7 8.5 %copy-start.16 = (f32[2,4,961]{2,1,0:T(4,128)S(1)}, f32[2,4,961]{2,1,0:T(4,128)}, u32[]{:S(2)}) copy-start(f32[2,4,961]{2,1,0:T(4,128)} %param.29) | copy-start | bytes 92260
  0.7 6.6 copy-start.18
  0.7 4.7 copy-start.17
  0.7 8.7 %copy-start.11 = (bf16[2,144,288]{2,1,0:T(8,128)(2,1)S(1)}, bf16[2,144,288]{2,1,0:T(8,128)(2,1)}, u32[]{:S(2)}) copy-start(bf16[2,144,288]{2,1,0:T(8,128)(2,1)} %param.24) | copy-start | bytes 497668
  3.2 8.2 %copy-start.1 = (bf16[2,6,144,288]{3,2,1,0:T(8,128)(2,1)S(1)}, bf16[2,6,144,288]{3,2,1,0:T(8,128)(2,1)}, u32[]{:S(2)}) copy-start(bf16[2,6,144,288]{3,2,1,0:T(8,128)(2,1)} %param.23) | copy-start | bytes 2985988
  14.0 4.7 copy-start
  535.2 195.0 %copy-start.10 = (f32[8,1152]{1,0:T(8,128)S(1)}, f32[8,1152]{1,0:T(8,128)}, u32[]{:S(2)}) copy-start(f32[8,1152]{1,0:T(8,128)} %get-tuple-element.78) | copy-start | bytes 110596
  727.9 9.4 %copy-start.12 = (f32[64,512]{1,0:T(8,128)S(1)}, f32[64,512]{1,0:T(8,128)}, u32[]{:S(2)}) copy-start(f32[64,512]{1,0:T(8,128)} %get-tuple-element.89) | copy-start | bytes 393220
  727.9 9.4 %copy-start.13 = (f32[64,512]{1,0:T(8,128)S(1)}, f32[64,512]{1,0:T(8,128)}, u32[]{:S(2)}) copy-start(f32[64,512]{1,0:T(8,128)} %get-tuple-element.88) | copy-start | bytes 393220
  728.0 9.5 %copy-start.3 = (f32[144,1152]{1,0:T(8,128)S(1)}, f32[144,1152]{1,0:T(8,128)}, u32[]{:S(2)}) copy-start(f32[144,1152]{1,0:T(8,128)} %get-tuple-element.79) | copy-start | bytes 1990660
  730.3 7.5 copy-start.2
  739.5 1.8 copy-start.6
  739.5 1.7 copy-start.7
  741.2 1.1 copy-start.4
  741.2 1.3 copy-start.5
  746.9 4.4 copy-start.8
  746.9 5.2 copy-start.9
